TPU v7x, 32 devices: a whole 2x2x4 slice. The times are simulated.
32 devices in a mesh: elem: 32 (over z, y, x, core).
Axes of the slice: x: 2, y: 2, z: 4, core: 2. Of those that a mesh axis runs over, the one named last changes fastest.
Arguments:
- a_blocks: float32 [1024, 7, 4096], P('elem'), may hold values from -0.25 to 0.25
- p_blocks: float32 [1024, 2, 4096], P('elem'), may hold values from -1.2 to 1.2
- a_slot: int32 [1024, 7], P('elem'), may hold values from 0 to 93
- serve_rows: int32 [32, 31, 2], P('elem'), may hold values from 0 to 31
- row_count: int32 [32], P('elem'), may hold values from 8 to 32, as said below
- contrib_slot: int32 [1024, 28], P('elem'), may hold values from 0 to 127
- recv_tile: int32 [32, 32, 4], P('elem'), may hold values from 0 to 7
Outputs:
- coarse: float32 [256, 4096], P('elem')
Inputs may be any that keep to these rules, and one draw needn't show every extreme that they name: `row_count`: rows of a device at or beyond its count are padding and contribute nothing; some device has exactly 32.
All inputs are finite; a program needn't handle non-finite values.
Results may differ from a plain program's by a relative error of at most 0.0003.
Values sent between devices are 32-bit elements; how exact they have to be, the bound alone decides.
No kernel may reach another device: no remote copies, remote signals or barrier semaphores. Data moves between devices by JAX's collectives and lax.ppermute only.
A program may use at most 192 MiB of HBM per device.

v0:
```python
import functools

import jax
import jax.numpy as jnp
from jax import lax
from jax.experimental import pallas as pl
from jax.experimental.pallas import tpu as pltpu
from jax.sharding import PartitionSpec as P

B = 64
HALF = B // 2
LANES = 2 * B
TO = 8
PLACES = 4
GROUP = 2 * PLACES
CHUNKS = 4
FIRST = 24
REST = HALF - FIRST
DEPTH = 3
UNROLL = 16
META = 8
MIB = 1 << 20


def low_lanes(rows):
    return lax.broadcasted_iota(jnp.int32, (rows, LANES), 1) < B


def split_rows(value):
    high = value.astype(jnp.bfloat16)
    low = (value - high.astype(jnp.float32)).astype(jnp.bfloat16)
    return jnp.concatenate([high, high, low, low], axis=0)


def params(mib, **more):
    return pltpu.CompilerParams(vmem_limit_bytes=mib * MIB, **more)


def prep_kernel(n, me_ref, serve_hbm, p_hbm, own, send_hbm, p_ref, send, serve_ref, p_sems, serve_sem, send_sems):
    rows = p_ref.shape[0]
    serve_count = serve_ref.shape[0]
    mask = low_lanes(HALF)
    chunk = rows // CHUNKS

    def chunk_copy(i):
        part = pl.ds(i * chunk, chunk)
        return pltpu.make_async_copy(p_hbm.at[part], p_ref.at[part], p_sems.at[i])

    serve_copy = pltpu.make_async_copy(serve_hbm, serve_ref, serve_sem)
    for i in range(CHUNKS):
        chunk_copy(i).start()
    serve_copy.start()

    def relayout(i, carry):
        first = p_ref[i, pl.ds(0, HALF, stride=2), :]
        second = p_ref[i, pl.ds(1, HALF, stride=2), :]
        turned = pltpu.roll(jnp.where(mask, second, first), B, 1)
        own[i, pl.ds(0, HALF, stride=2), :] = jnp.where(mask, first, turned)
        own[i, pl.ds(1, HALF, stride=2), :] = jnp.where(mask, turned, second)
        return carry

    for i in range(CHUNKS):
        chunk_copy(i).wait()
        lax.fori_loop(i * chunk, (i + 1) * chunk, relayout, 0, unroll=4)
    serve_copy.wait()
    me = me_ref[0]

    targets = n // CHUNKS

    def serve(target, carry):
        offset = target - me - 1
        offset = jnp.where(offset < 0, offset + n, offset)
        offset = jnp.minimum(offset, n - 2)
        for c in range(serve_count):
            send[target, c] = own[serve_ref[c, offset]]
        return carry

    def send_copy(i):
        part = pl.ds(i * targets, targets)
        return pltpu.make_async_copy(send.at[part], send_hbm.at[part], send_sems.at[i])

    for i in range(CHUNKS):
        lax.fori_loop(i * targets, (i + 1) * targets, serve, 0, unroll=4)
        send_copy(i).start()
    for i in range(CHUNKS):
        send_copy(i).wait()


def add_products(acc, out, dest):
    mask = low_lanes(B)
    for p in range(2):
        rows = out[p * B : (p + 1) * B]
        left = jnp.where(mask, rows, 0.0)
        acc[dest[2 * p]] += left
        acc[dest[2 * p + 1]] += rows - left


def add_entry(acc, meta, e, lp, right_ref):
    weights = split_rows(right_ref[meta[e * META]])
    out = jnp.dot(jnp.concatenate([lp, lp], axis=1), weights, preferred_element_type=jnp.float32)
    add_products(acc, out, [meta[e * META + 1 + j] for j in range(4)])


def fold(acc, slot):
    mask = low_lanes(HALF)
    even, odd = acc[slot, :HALF], acc[slot, HALF:]
    return jnp.where(mask, even, odd) + pltpu.roll(jnp.where(mask, odd, even), B, 1)


def near_kernel(
    n, count_row, a_slot, contrib, me_ref, own_ref, a_ref, left_hbm, slots_hbm, meta_ref, acc, left_ref, slots_ref, turned_rows, near_meta, place_of, sems
):
    step = pl.program_id(0)
    rows = own_ref.shape[0]
    blocks = a_ref.shape[1]
    slot_count = slots_ref.shape[0]
    per_row = contrib.shape[1] // 2
    entries = rows * blocks
    last = near_meta.shape[0] - 1

    @pl.when(step == 0)
    def start():
        me = me_ref[0]

        def put(ref, at, row, i, k):
            ref[at * META] = row
            for p in range(2):
                for q in range(2):
                    ref[at * META + 1 + 2 * p + q] = contrib[i, p * per_row + 2 * k + q]

        def put_pad(ref, at):
            ref[at * META] = 0
            for j in range(4):
                ref[at * META + 1 + j] = slot_count

        def scan_row(i, carry):
            near_count, far_count = carry
            for k in range(blocks):
                slot = a_slot[k, i]
                is_near = slot < rows
                index = slot - rows
                source = me - 1 - index // 2
                source = jnp.where(source < 0, source + n, source)
                put(near_meta, near_count, jnp.where(is_near, slot, 0), i, k)
                put(meta_ref, far_count, jnp.where(is_near, 0, source * 2 + index % 2), i, k)
                place_of[i * blocks + k] = jnp.where(is_near, entries - 1 - near_count, far_count)
                near_count = near_count + jnp.where(is_near, 1, 0)
                far_count = far_count + jnp.where(is_near, 0, 1)
            return near_count, far_count

        def skip_row(i, carry):
            for k in range(blocks):
                place_of[i * blocks + k] = entries
            return carry

        live = jnp.minimum(count_row[0], rows)
        near_count, far_count = lax.fori_loop(0, live, scan_row, (0, 0))
        lax.fori_loop(live, rows, skip_row, 0)
        for j in range(UNROLL):
            put_pad(near_meta, near_count + j)
            put_pad(meta_ref, far_count + j)
        near_meta[last] = near_count
        meta_ref[last] = far_count
        acc[...] = jnp.zeros_like(acc)

    mask = low_lanes(HALF)
    y_even = own_ref[step, pl.ds(0, HALF, stride=2), :]
    y_odd = own_ref[step, pl.ds(1, HALF, stride=2), :]
    p_rows = jnp.concatenate([y_even, y_odd], axis=0)
    high = p_rows.astype(jnp.bfloat16).astype(jnp.float32)
    turned_rows[...] = jnp.concatenate([high, p_rows - high], axis=0).T
    pair = [turned_rows[pl.ds(p * B + parity, HALF, stride=2), :] for p in range(2) for parity in range(2)]
    pair = jnp.concatenate(pair, axis=0).astype(jnp.bfloat16)
    lhs = jnp.concatenate([pair, pair], axis=1)
    for k in range(blocks):
        tile = a_ref[0, k]
        turned = pltpu.roll(tile, B, 1)
        both = jnp.concatenate([jnp.where(mask, tile, turned), jnp.where(mask, turned, tile)], axis=0)
        left = jnp.dot(lhs, split_rows(both), preferred_element_type=jnp.float32)
        left_high = left.astype(jnp.bfloat16).astype(jnp.float32)
        packed = jnp.where(low_lanes(2 * B), left_high, left - left_high)
        left_ref[place_of[step * blocks + k]] = packed.astype(jnp.bfloat16)

    @pl.when(step == pl.num_programs(0) - 1)
    def own_products():
        left_copy = pltpu.make_async_copy(left_ref, left_hbm, sems.at[0])
        left_copy.start()

        def products(g, carry):
            for u in range(UNROLL):
                e = g * UNROLL + u
                add_entry(acc, near_meta, e, left_ref[jnp.maximum(entries - 1 - e, 0)], own_ref)
            return carry

        lax.fori_loop(0, (near_meta[last] + UNROLL - 1) // UNROLL, products, 0)

        def pack(slot, carry):
            slots_ref[slot] = fold(acc, slot)
            return carry

        lax.fori_loop(0, slot_count, pack, 0, unroll=8)
        slots_copy = pltpu.make_async_copy(slots_ref, slots_hbm, sems.at[1])
        slots_copy.start()
        left_copy.wait()
        slots_copy.wait()


def far_kernel(n, cap, me_ref, meta, left_hbm, recv, near_hbm, *refs):
    groups = n // GROUP
    far_slots, rest_slots = refs[:PLACES], refs[PLACES : PLACES + groups - 1]
    own_mine, own_other, acc, near, ring, ring_sems, near_sem = refs[PLACES + groups - 1 :]
    me = me_ref[0]
    count = meta[meta.shape[0] - 1]
    turns = (count + UNROLL - 1) // UNROLL

    def left_copy(g):
        buffer = lax.rem(g, DEPTH)
        return pltpu.make_async_copy(left_hbm.at[pl.ds(g * UNROLL, UNROLL)], ring.at[buffer], ring_sems.at[buffer])

    def fetch(g):
        @pl.when(g < turns)
        def go():
            left_copy(g).start()

    for g in range(DEPTH - 1):
        fetch(g)
    near_copy = pltpu.make_async_copy(near_hbm, near, near_sem)
    near_copy.start()
    acc[...] = jnp.zeros_like(acc)

    def products(g, carry):
        fetch(g + DEPTH - 1)
        left_copy(g).wait()
        for u in range(UNROLL):
            add_entry(acc, meta, g * UNROLL + u, ring[lax.rem(g, DEPTH), u], recv)
        return carry

    lax.fori_loop(0, turns, products, 0)
    near_copy.wait()
    place = lax.rem(me // 2, PLACES)
    group = me // GROUP

    core = lax.rem(me, 2)

    def packed(j, step, side):
        at = group + step
        at = jnp.where(at >= groups, at - groups, at)
        m = at * GROUP + (place ^ j) * 2 + side - me
        m = jnp.where(m < 0, m + n, m)
        return [fold(acc, m * cap + c) + near[m * cap + c] for c in range(cap)]

    for j in range(PLACES):
        for other in range(2):
            side = 1 - core if other else core
            for step in range(1, groups):
                for c, slot in enumerate(packed(j, step, side)):
                    far_slots[j][step - 1, side, c] = slot[:FIRST]
                    rest_slots[step - 1][other, j, c] = slot[FIRST:]
            for c, slot in enumerate(packed(j, 0, side)):
                (own_other if other else own_mine)[j, c] = slot


def add_slots(target, table, entry, m, slots, first=0):
    for c in range(slots.shape[0]):
        target[table[entry * slots.shape[0] + c, m], pl.ds(first, slots.shape[1]), :] += slots[c]


def combine_far_kernel(n, me_ref, table, *refs):
    slots, (mine, other) = refs[:PLACES], refs[PLACES:]
    groups = n // GROUP
    me = me_ref[0]
    core = lax.rem(me, 2)
    place = lax.rem(me // 2, PLACES)
    group = me // GROUP

    def gather(step, carry):
        at = group + step
        at = jnp.where(at >= groups, at - groups, at)
        for target, side in ((mine, core), (other, 1 - core)):
            tiles = target.at[step - 1]
            tiles[...] = jnp.zeros_like(tiles)
            for j in range(PLACES):
                m = (at - group) * GROUP + (place - (place ^ j)) * 2 + side - core
                m = jnp.where(m < 0, m + n, m)
                add_slots(tiles, table, (at ^ group) * 2 + (side ^ core), m, slots[j].at[step - 1, side])
        return carry

    lax.fori_loop(1, groups, gather, 0)


def combine_own_kernel(n, me_ref, table, mine, got, rest_got, *refs):
    rest_mine, tiles = refs[:-PLACES], refs[-PLACES:]
    me = me_ref[0]
    core = lax.rem(me, 2)
    place = lax.rem(me // 2, PLACES)
    for j in range(PLACES):
        tiles[j][...] = jnp.zeros_like(tiles[j])
        for other in range(2):
            m = ((place ^ j) - place) * 2 + other * (2 * core - 1)
            m = jnp.where(m < 0, m + n, m)
            add_slots(tiles[j], table, j, m, (got if other else mine).at[j])
            for step, rest in enumerate(rest_mine, 1):
                at = m + step * GROUP
                at = jnp.where(at >= n, at - n, at)
                add_slots(tiles[j], table, j, at, rest_got.at[step - 1, j] if other else rest.at[0, j], FIRST)


def final_kernel(*refs):
    own, far, out_ref, total = refs[:PLACES], refs[PLACES:-2], refs[-2], refs[-1]
    for t in range(TO):
        total[t * HALF : (t + 1) * HALF] = own[0][t] + own[1][t] + own[2][t] + own[3][t]
        value = far[0][t]
        for part in far[1:]:
            value = value + part[t]
        total[t * HALF : t * HALF + FIRST] += value
    for r in range(HALF):
        out_ref[:, r * LANES : (r + 1) * LANES] = total[pl.ds(r, TO, stride=HALF), :]


def spec(space):
    return pl.BlockSpec(memory_space=space)


def body(a_blocks, p_blocks, a_slot, serve_rows, row_count, contrib_slot, recv_tile):
    n = lax.axis_size("elem")
    rows, blocks, _ = a_blocks.shape
    cap = recv_tile.shape[2]
    serve_count = serve_rows.shape[2]
    f32, i32, bf16 = jnp.float32, jnp.int32, jnp.bfloat16
    smem, vmem, hbm = spec(pltpu.SMEM), spec(pltpu.VMEM), spec(pl.ANY)
    pinned = n <= 32
    me = lax.axis_index("elem").astype(i32).reshape(1)

    def shape(dims, dtype):
        return pltpu.VMEM(dims, dtype) if pinned else jax.ShapeDtypeStruct(dims, dtype)

    def pin(value):
        return pltpu.with_memory_space_constraint(value, pltpu.VMEM) if pinned else value

    def pin_hbm(value):
        return pltpu.with_memory_space_constraint(value, pltpu.HBM)

    def across(value, partner):
        return lax.ppermute(value, "elem", [(i, partner(i)) for i in range(n)])

    p_view = p_blocks.reshape(rows, 2, HALF, LANES).transpose(0, 2, 1, 3).reshape(rows, B, LANES)
    own, send = pl.pallas_call(
        functools.partial(prep_kernel, n),
        out_shape=(shape((rows, B, LANES), f32), pltpu.HBM((n, serve_count, B, LANES), f32)),
        in_specs=[smem, hbm, hbm],
        out_specs=(vmem, hbm),
        scratch_shapes=[
            pltpu.VMEM((rows, B, LANES), f32),
            pltpu.VMEM((n, serve_count, B, LANES), f32),
            pltpu.SMEM((serve_count, n - 1), i32),
            pltpu.SemaphoreType.DMA((CHUNKS,)),
            pltpu.SemaphoreType.DMA,
            pltpu.SemaphoreType.DMA((CHUNKS,)),
        ],
        compiler_params=params(8 + n // 8),
        name="prep",
    )(me, pin_hbm(serve_rows[0].T), pin_hbm(p_view))

    recv = lax.all_to_all(
        send.reshape(n, serve_count * B, LANES), "elem", split_axis=0, concat_axis=0, tiled=True
    ).reshape(n * serve_count, B, LANES)

    groups = n // GROUP
    table = recv_tile.transpose(0, 2, 1)
    own_table = jnp.concatenate([table] + [across(table, lambda i, j=j: i ^ (2 * j)) for j in range(1, PLACES)], axis=0)
    pair = jnp.concatenate([table, across(table, lambda i: i ^ 1)], axis=0)
    a_blocks, pair = lax.optimization_barrier((a_blocks, pair))
    far_table = jnp.concatenate(
        [pair] + [across(pair, lambda i, step=step: i ^ (step * GROUP)) for step in range(1, groups)], axis=0
    )
    recv, own_table, far_table = lax.optimization_barrier((recv, own_table, far_table))
    own_table, far_table = own_table.reshape(-1, n), far_table.reshape(-1, n)

    entries = rows * blocks
    slot_count = n * cap
    meta_size = (entries + 2 * UNROLL) * META
    a_tiles = a_blocks.reshape(rows, blocks, HALF, LANES)
    left, near_slots, meta = pl.pallas_call(
        functools.partial(near_kernel, n),
        grid=(rows,),
        out_shape=(
            pltpu.HBM((entries + UNROLL, 2 * B, LANES), bf16),
            pltpu.HBM((slot_count, HALF, LANES), f32),
            jax.ShapeDtypeStruct((meta_size,), i32),
        ),
        in_specs=[smem, smem, smem, smem, vmem, pl.BlockSpec((1, blocks, HALF, LANES), lambda i: (i, 0, 0, 0))],
        out_specs=(hbm, hbm, smem),
        scratch_shapes=[
            pltpu.VMEM((slot_count + 1, B, LANES), f32),
            pltpu.VMEM((entries + UNROLL, 2 * B, LANES), bf16),
            pltpu.VMEM((slot_count, HALF, LANES), f32),
            pltpu.VMEM((2 * B, LANES), f32),
            pltpu.SMEM((meta_size,), i32),
            pltpu.SMEM((entries,), i32),
            pltpu.SemaphoreType.DMA((2,)),
        ],
        compiler_params=params(20 + n // 4, dimension_semantics=("arbitrary",)),
        cost_estimate=pl.CostEstimate(flops=8 * entries * 2 * B * LANES * LANES, bytes_accessed=16 << 20, transcendentals=0),
        name="near",
    )(row_count, a_slot.T, contrib_slot, me, pin(own), a_tiles)

    slot_shapes = [shape((groups - 1, 2, cap, FIRST, LANES), f32)] * PLACES
    slot_shapes += [shape((2, PLACES, cap, REST, LANES), f32)] * (groups - 1)
    slot_shapes += [shape((PLACES, cap, HALF, LANES), f32)] * 2
    slots = pl.pallas_call(
        functools.partial(far_kernel, n, cap),
        out_shape=slot_shapes,
        in_specs=[smem, smem, hbm, vmem, hbm],
        out_specs=[vmem] * len(slot_shapes),
        scratch_shapes=[
            pltpu.VMEM((slot_count + 1, B, LANES), f32),
            pltpu.VMEM((slot_count, HALF, LANES), f32),
            pltpu.VMEM((DEPTH, UNROLL, 2 * B, LANES), bf16),
            pltpu.SemaphoreType.DMA((DEPTH,)),
            pltpu.SemaphoreType.DMA,
        ],
        compiler_params=params(16 + n // 4),
        cost_estimate=pl.CostEstimate(flops=4 * entries * 2 * B * LANES * LANES, bytes_accessed=16 << 20, transcendentals=0),
        name="far",
    )(me, meta, pin_hbm(left), pin(recv), pin_hbm(near_slots))

    def combine(kernel, out_shape, table, parts):
        return pl.pallas_call(
            functools.partial(kernel, n),
            out_shape=out_shape,
            in_specs=[smem, smem] + [vmem] * len(parts),
            out_specs=[vmem] * len(out_shape),
            compiler_params=params(8 + n // 4),
            name=kernel.__name__,
        )(me, table, *[pin(part) for part in parts])

    def in_group(values):
        return [values[0]] + [across(values[j], lambda i, j=j: i ^ (2 * j)) for j in range(1, PLACES)]

    def over_groups(values):
        return [across(value, lambda i, step=step: (i + step * GROUP) % n) for step, value in enumerate(values, 1)]

    def other_core(value):
        return across(value, lambda i: i ^ 1)

    own_mine, own_other = slots[-2:]
    rest = over_groups(slots[PLACES:-2])
    far_slots = in_group(slots[:PLACES])
    rest_got = other_core(jnp.stack([part[1] for part in rest]))
    own_shape = [shape((TO, HALF, LANES), f32)] * PLACES
    own_tiles = combine(combine_own_kernel, own_shape, own_table, [own_mine, other_core(own_other), rest_got] + rest)
    far_shape = [shape((groups - 1, TO, FIRST, LANES), f32)] * 2
    mine, other = combine(combine_far_kernel, far_shape, far_table, far_slots)
    got = other_core(other)
    summed = [mine[step] + got[step] for step in range(groups - 1)]
    summed, own_tiles = lax.optimization_barrier((summed, own_tiles))
    far_parts = over_groups(summed)
    parts = in_group(own_tiles) + far_parts

    return pl.pallas_call(
        final_kernel,
        out_shape=jax.ShapeDtypeStruct((TO, B * B), f32),
        in_specs=[vmem] * len(parts),
        out_specs=vmem,
        scratch_shapes=[pltpu.VMEM((TO * HALF, LANES), f32)],
        compiler_params=params(8),
        name="final",
    )(*[pin(part) for part in parts])


def solution(mesh):
    in_specs = (
        P("elem", None, None),
        P("elem", None, None),
        P("elem", None),
        P("elem", None, None),
        P("elem"),
        P("elem", None),
        P("elem", None, None),
    )
    out_specs = P("elem", None)
    return jax.shard_map(body, mesh=mesh, in_specs=in_specs, out_specs=out_specs, check_vma=False)
```

profile of v0, /device:TPU:0, one launch (start us, length us, event | category | flops | bytes accessed | tf_op | source)
XLA Modules:
  0.0 100.3 jit_solution(11209728044649791322)
XLA Ops:
  0.0 3.2 %prep.1 = (f32[32,64,128]{2,1,0:T(8,128)S(1)}, f32[32,2,64,128]{3,2,1,0:T(8,128)}) custom-call(s32[1]{0:T(128)} %bitcast.me_ref, s32[2,31]{1,0:T(2,128)} %bitcast.41, f32[32,64,128]{2,1,0:T(8,128)} %bitcast.34), custom_call_target="tpu_custom_call" | custom-call | tf_op jit(solution)/shard_map/prep/pallas_call | solution.py:347
  3.2 7.3 %all-to-all-start = ((f32[32,128,128]{2,1,0:T(8,128)}), f32[32,128,128]{2,1,0:T(8,128)S(1)}, u32[]{:S(2)}, u32[]{:S(2)}) async-start(f32[32,128,128]{2,1,0:T(8,128)} %bitcast.33), calls=%async_computation | async-start | bytes 4194304 | tf_op jit(solution)/shard_map/all_to_all | solution.py:364
  10.8 2.6 %collective-permute-start.2 = (s32[1,4,32]{2,1,0:T(4,128)S(1)}, s32[1,4,32]{2,1,0:T(4,128)S(1)}, u32[]{:S(2)}, u32[]{:S(2)}) collective-permute-start(s32[1,4,32]{2,1,0:T(4,128)S(1)} %bitcast.36), channel_id=1, source_target_pairs={{0,6},{1,7},{2,4},{3,5},{4,2},{5,3},{6,0},{7,1},{8,14},{9,15},{10,... | collective-permute-start | bytes 1544 | tf_op jit(solution)/shard_map/ppermute | solution.py:344
  15.0 3.6 %collective-permute-start.6 = (s32[2,4,32]{2,1,0:T(4,128)S(1)}, s32[2,4,32]{2,1,0:T(4,128)S(1)}, u32[]{:S(2)}, u32[]{:S(2)}) collective-permute-start(s32[2,4,32]{2,1,0:T(4,128)S(1)} %pad_add_fusion.2), channel_id=1, source_target_pairs={{0,24},{1,25},{2,26},{3,27},{4,28},{5,29},{6,30},{7,31},{8,16},{9,... | collective-permute-start | bytes 3080 | tf_op jit(solution)/shard_map/ppermute | solution.py:344
  18.6 2.7 %copy.12 = f32[28,8,32,128]{3,2,1,0:T(8,128)S(1)} copy(f32[28,8,32,128]{3,1,2,0:T(8,128)} %bitcast.32) | data formatting | bytes 7340032
  22.0 22.7 %near.1 = (bf16[240,128,128]{2,1,0:T(8,128)(2,1)}, f32[128,32,128]{2,1,0:T(8,128)}, s32[2048]{0:T(1024)S(1)}) custom-call(s32[1]{0:T(128)S(6)} %copy.13.count_row, s32[7,32]{1,0:T(8,128)S(1)} %bitcast.30, s32[32,28]{1,0:T(8,128)S(1)} %copy-done, s32[1]{0:T(128)} %bitcast.me_ref, f32[32,64,128]{2,1,0:T(8,128)S(1)} %get-tuple-element.40.own_ref, ...), custom_call_target="tpu_custom_call" | custom-call | flops 3758096384 | bytes 16777216 | tf_op jit(solution)/shard_map/near/pallas_call | solution.py:383
  44.9 4.5 %collective-permute-done.6 = s32[2,4,32]{2,1,0:T(4,128)S(1)} collective-permute-done((s32[2,4,32]{2,1,0:T(4,128)S(1)}, s32[2,4,32]{2,1,0:T(4,128)S(1)}, u32[]{:S(2)}, u32[]{:S(2)}) %collective-permute-start.6) | collective-permute-done | bytes 1056 | tf_op jit(solution)/shard_map/ppermute | solution.py:344
  49.3 10.4 %collective-permute-done.5 = s32[2,4,32]{2,1,0:T(4,128)S(1)} collective-permute-done((s32[2,4,32]{2,1,0:T(4,128)S(1)}, s32[2,4,32]{2,1,0:T(4,128)S(1)}, u32[]{:S(2)}, u32[]{:S(2)}) %collective-permute-start.5) | collective-permute-done | bytes 1056 | tf_op jit(solution)/shard_map/ppermute | solution.py:344
  59.8 4.8 %far.1 = (f32[3,2,4,24,128]{4,3,2,1,0:T(8,128)S(1)}, f32[3,2,4,24,128]{4,3,2,1,0:T(8,128)S(1)}, f32[3,2,4,24,128]{4,3,2,1,0:T(8,128)S(1)}, f32[3,2,4,24,128]{4,3...) custom-call(s32[1]{0:T(128)} %bitcast.me_ref, ...), custom_call_target="tpu_custom_call" | custom-call | flops 1879048192 | bytes 16777216 | tf_op jit(solution)/shard_map/far/pallas_call | solution.py:410
  64.6 2.0 %collective-permute-start.7 = (f32[3,2,4,24,128]{4,3,2,1,0:T(8,128)S(1)}, f32[3,2,4,24,128]{4,3,2,1,0:T(8,128)S(1)}, u32[]{:S(2)}, u32[]{:S(2)}) collective-permute-start(f32[3,2,4,24,128]{4,3,2,1,0:T(8,128)S(1)} %get-tuple-element.47), channel_id=1, source_target_pairs={{0,2},{1,3},{2,0},{3,1},{4,6},{5,7},{6,4},{7,5},{8,10},{9,11},{10,... | collective-permute-start | bytes 884744 | tf_op jit(solution)/shard_map/ppermute | solution.py:344
  66.6 2.6 %collective-permute-start.8 = (f32[3,2,4,24,128]{4,3,2,1,0:T(8,128)S(1)}, f32[3,2,4,24,128]{4,3,2,1,0:T(8,128)S(1)}, u32[]{:S(2)}, u32[]{:S(2)}) collective-permute-start(f32[3,2,4,24,128]{4,3,2,1,0:T(8,128)S(1)} %get-tuple-element.48), channel_id=1, source_target_pairs={{0,4},{1,5},{2,6},{3,7},{4,0},{5,1},{6,2},{7,3},{8,12},{9,13},{10,... | collective-permute-start | bytes 884744 | tf_op jit(solution)/shard_map/ppermute | solution.py:344
  69.2 1.1 %collective-permute-start.9 = (f32[3,2,4,24,128]{4,3,2,1,0:T(8,128)S(1)}, f32[3,2,4,24,128]{4,3,2,1,0:T(8,128)S(1)}, u32[]{:S(2)}, u32[]{:S(2)}) collective-permute-start(f32[3,2,4,24,128]{4,3,2,1,0:T(8,128)S(1)} %get-tuple-element.49), channel_id=1, source_target_pairs={{0,6},{1,7},{2,4},{3,5},{4,2},{5,3},{6,0},{7,1},{8,14},{9,15},{10,... | collective-permute-start | bytes 884744 | tf_op jit(solution)/shard_map/ppermute | solution.py:344
  70.3 2.0 %collective-permute-start.13 = (f32[2,4,4,8,128]{4,3,2,1,0:T(8,128)S(1)}, f32[2,4,4,8,128]{4,3,2,1,0:T(8,128)S(1)}, u32[]{:S(2)}, u32[]{:S(2)}) collective-permute-start(f32[2,4,4,8,128]{4,3,2,1,0:T(8,128)S(1)} %get-tuple-element.56), channel_id=1, source_target_pairs={{0,16},{1,17},{2,18},{3,19},{4,20},{5,21},{6,22},{7,23},{8,24},{9,... | collective-permute-start | bytes 393224 | tf_op jit(solution)/shard_map/ppermute | solution.py:344
  72.3 5.0 %collective-permute-done.12.refs_0_ = f32[2,4,4,8,128]{4,3,2,1,0:T(8,128)S(1)} collective-permute-done((f32[2,4,4,8,128]{4,3,2,1,0:T(8,128)S(1)}, f32[2,4,4,8,128]{4,3,2,1,0:T(8,128)S(1)}, u32[]{:S(2)}, u32[]{:S(2)}) %collective-permute-start.12) | collective-permute-done | bytes 131104 | tf_op jit(solution)/shard_map/ppermute | solution.py:344
  77.3 3.2 %collective-permute-done.13.refs_1_ = f32[2,4,4,8,128]{4,3,2,1,0:T(8,128)S(1)} collective-permute-done((f32[2,4,4,8,128]{4,3,2,1,0:T(8,128)S(1)}, f32[2,4,4,8,128]{4,3,2,1,0:T(8,128)S(1)}, u32[]{:S(2)}, u32[]{:S(2)}) %collective-permute-start.13) | collective-permute-done | bytes 131104 | tf_op jit(solution)/shard_map/ppermute | solution.py:344
  80.5 1.7 %collective-permute-done.14.refs_2_ = f32[2,4,4,8,128]{4,3,2,1,0:T(8,128)S(1)} collective-permute-done((f32[2,4,4,8,128]{4,3,2,1,0:T(8,128)S(1)}, f32[2,4,4,8,128]{4,3,2,1,0:T(8,128)S(1)}, u32[]{:S(2)}, u32[]{:S(2)}) %collective-permute-start.14) | collective-permute-done | bytes 131104 | tf_op jit(solution)/shard_map/ppermute | solution.py:344
  82.3 1.2 %combine_far_kernel.1 = (f32[3,8,24,128]{3,2,1,0:T(8,128)S(1)}, f32[3,8,24,128]{3,2,1,0:T(8,128)S(1)}) custom-call(s32[1]{0:T(128)} %bitcast.me_ref, s32[32,32]{1,0:T(8,128)S(1)} %bitcast.28, f32[3,2,4,24,128]{4,3,2,1,0:T(8,128)S(1)} %get-tuple-element.46.refs_0_, f32[3,2,4,24,128]{4,3,2,1,0:T(8,128)S(1)} %collective-permute-done.7.refs_1_, ...), custom_call_target="tpu_custom_call" | custom-call | tf_op jit(solution)/shard_map/combine_far_kernel/pallas_call | solution.py:428
  84.1 1.3 %collective-permute-done.15.rest_got = f32[3,4,4,8,128]{4,3,2,1,0:T(8,128)S(1)} collective-permute-done((f32[3,4,4,8,128]{4,3,2,1,0:T(8,128)S(1)}, f32[3,4,4,8,128]{4,3,2,1,0:T(8,128)S(1)}, u32[]{:S(2)}, u32[]{:S(2)}) %collective-permute-start.15) | collective-permute-done | bytes 196640 | tf_op jit(solution)/shard_map/ppermute | solution.py:344
  86.5 1.4 %collective-permute-start.19 = (f32[8,24,128]{2,1,0:T(8,128)S(1)}, f32[8,24,128]{2,1,0:T(8,128)S(1)}, u32[]{:S(2)}, u32[]{:S(2)}) collective-permute-start(f32[8,24,128]{2,1,0:T(8,128)S(1)} %get-tuple-element.66), channel_id=1, source_target_pairs={{0,8},{1,9},{2,10},{3,11},{4,12},{5,13},{6,14},{7,15},{8,16},{9,17... | collective-permute-start | bytes 294920 | tf_op jit(solution)/shard_map/ppermute | solution.py:344
  87.8 1.6 %collective-permute-start.16 = (f32[8,32,128]{2,1,0:T(8,128)S(1)}, f32[8,32,128]{2,1,0:T(8,128)S(1)}, u32[]{:S(2)}, u32[]{:S(2)}) collective-permute-start(f32[8,32,128]{2,1,0:T(8,128)S(1)} %get-tuple-element.63), channel_id=1, source_target_pairs={{0,2},{1,3},{2,0},{3,1},{4,6},{5,7},{6,4},{7,5},{8,10},{9,11},{10,... | collective-permute-start | bytes 393224 | tf_op jit(solution)/shard_map/ppermute | solution.py:344
  89.4 1.2 %collective-permute-start.17 = (f32[8,32,128]{2,1,0:T(8,128)S(1)}, f32[8,32,128]{2,1,0:T(8,128)S(1)}, u32[]{:S(2)}, u32[]{:S(2)}) collective-permute-start(f32[8,32,128]{2,1,0:T(8,128)S(1)} %get-tuple-element.64), channel_id=1, source_target_pairs={{0,4},{1,5},{2,6},{3,7},{4,0},{5,1},{6,2},{7,3},{8,12},{9,13},{10,... | collective-permute-start | bytes 393224 | tf_op jit(solution)/shard_map/ppermute | solution.py:344
  91.3 2.0 %collective-permute-start.20 = (f32[8,24,128]{2,1,0:T(8,128)S(1)}, f32[8,24,128]{2,1,0:T(8,128)S(1)}, u32[]{:S(2)}, u32[]{:S(2)}) collective-permute-start(f32[8,24,128]{2,1,0:T(8,128)S(1)} %get-tuple-element.67), channel_id=1, source_target_pairs={{0,16},{1,17},{2,18},{3,19},{4,20},{5,21},{6,22},{7,23},{8,24},{9,... | collective-permute-start | bytes 294920 | tf_op jit(solution)/shard_map/ppermute | solution.py:344
  93.3 2.4 %collective-permute-start.21 = (f32[8,24,128]{2,1,0:T(8,128)S(1)}, f32[8,24,128]{2,1,0:T(8,128)S(1)}, u32[]{:S(2)}, u32[]{:S(2)}) collective-permute-start(f32[8,24,128]{2,1,0:T(8,128)S(1)} %get-tuple-element.68), channel_id=1, source_target_pairs={{0,24},{1,25},{2,26},{3,27},{4,28},{5,29},{6,30},{7,31},{8,0},{9,1... | collective-permute-start | bytes 294920 | tf_op jit(solution)/shard_map/ppermute | solution.py:344
  95.7 3.8 %collective-permute-done.20.refs_5_ = f32[8,24,128]{2,1,0:T(8,128)S(1)} collective-permute-done((f32[8,24,128]{2,1,0:T(8,128)S(1)}, f32[8,24,128]{2,1,0:T(8,128)S(1)}, u32[]{:S(2)}, u32[]{:S(2)}) %collective-permute-start.20) | collective-permute-done | bytes 98336 | tf_op jit(solution)/shard_map/ppermute | solution.py:344
  (44 shorter events, 5.3 us)
Async XLA Ops:
  0.0 10.5 %copy-start.2 = (s32[1,32,4]{1,2,0:T(4,128)S(1)}, s32[1,32,4]{1,2,0:T(4,128)}, u32[]{:S(2)}) copy-start(s32[1,32,4]{1,2,0:T(4,128)} %param.13) | copy-start | bytes 1540
  3.2 56.6 %all-to-all-start = ((f32[32,128,128]{2,1,0:T(8,128)}), f32[32,128,128]{2,1,0:T(8,128)S(1)}, u32[]{:S(2)}, u32[]{:S(2)}) async-start(f32[32,128,128]{2,1,0:T(8,128)} %bitcast.33), calls=%async_computation | async-start | bytes 4194304 | tf_op jit(solution)/shard_map/all_to_all | solution.py:364
  10.5 4.5 %collective-permute-start.3 = (s32[1,4,32]{2,1,0:T(4,128)S(1)}, s32[1,4,32]{2,1,0:T(4,128)S(1)}, u32[]{:S(2)}, u32[]{:S(2)}) collective-permute-start(s32[1,4,32]{2,1,0:T(4,128)S(1)} %bitcast.35), channel_id=1, source_target_pairs={{0,1},{1,0},{2,3},{3,2},{4,5},{5,4},{6,7},{7,6},{8,9},{9,8},{10,11... | collective-permute-start | bytes 1544 | tf_op jit(solution)/shard_map/ppermute | solution.py:344
  10.8 33.9 %collective-permute-start.2 = (s32[1,4,32]{2,1,0:T(4,128)S(1)}, s32[1,4,32]{2,1,0:T(4,128)S(1)}, u32[]{:S(2)}, u32[]{:S(2)}) collective-permute-start(s32[1,4,32]{2,1,0:T(4,128)S(1)} %bitcast.36), channel_id=1, source_target_pairs={{0,6},{1,7},{2,4},{3,5},{4,2},{5,3},{6,0},{7,1},{8,14},{9,15},{10,... | collective-permute-start | bytes 1544 | tf_op jit(solution)/shard_map/ppermute | solution.py:344
  13.4 31.4 %collective-permute-start.1 = (s32[1,4,32]{2,1,0:T(4,128)S(1)}, s32[1,4,32]{2,1,0:T(4,128)S(1)}, u32[]{:S(2)}, u32[]{:S(2)}) collective-permute-start(s32[1,4,32]{2,1,0:T(4,128)S(1)} %bitcast.37), channel_id=1, source_target_pairs={{0,4},{1,5},{2,6},{3,7},{4,0},{5,1},{6,2},{7,3},{8,12},{9,13},{10,... | collective-permute-start | bytes 1544 | tf_op jit(solution)/shard_map/ppermute | solution.py:344
  14.0 30.9 %collective-permute-start = (s32[1,4,32]{2,1,0:T(4,128)S(1)}, s32[1,4,32]{2,1,0:T(4,128)S(1)}, u32[]{:S(2)}, u32[]{:S(2)}) collective-permute-start(s32[1,4,32]{2,1,0:T(4,128)S(1)} %bitcast.38), channel_id=1, source_target_pairs={{0,2},{1,3},{2,0},{3,1},{4,6},{5,7},{6,4},{7,5},{8,10},{9,11},{10,... | collective-permute-start | bytes 1544 | tf_op jit(solution)/shard_map/ppermute | solution.py:344
  15.0 34.3 %collective-permute-start.6 = (s32[2,4,32]{2,1,0:T(4,128)S(1)}, s32[2,4,32]{2,1,0:T(4,128)S(1)}, u32[]{:S(2)}, u32[]{:S(2)}) collective-permute-start(s32[2,4,32]{2,1,0:T(4,128)S(1)} %pad_add_fusion.2), channel_id=1, source_target_pairs={{0,24},{1,25},{2,26},{3,27},{4,28},{5,29},{6,30},{7,31},{8,16},{9,... | collective-permute-start | bytes 3080 | tf_op jit(solution)/shard_map/ppermute | solution.py:344
  18.6 41.2 %collective-permute-start.5 = (s32[2,4,32]{2,1,0:T(4,128)S(1)}, s32[2,4,32]{2,1,0:T(4,128)S(1)}, u32[]{:S(2)}, u32[]{:S(2)}) collective-permute-start(s32[2,4,32]{2,1,0:T(4,128)S(1)} %pad_add_fusion.2), channel_id=1, source_target_pairs={{0,16},{1,17},{2,18},{3,19},{4,20},{5,21},{6,22},{7,23},{8,24},{9,... | collective-permute-start | bytes 3080 | tf_op jit(solution)/shard_map/ppermute | solution.py:344
  44.8 15.0 %collective-permute-start.4 = (s32[2,4,32]{2,1,0:T(4,128)S(1)}, s32[2,4,32]{2,1,0:T(4,128)S(1)}, u32[]{:S(2)}, u32[]{:S(2)}) collective-permute-start(s32[2,4,32]{2,1,0:T(4,128)S(1)} %pad_add_fusion.2), channel_id=1, source_target_pairs={{0,8},{1,9},{2,10},{3,11},{4,12},{5,13},{6,14},{7,15},{8,0},{9,1},... | collective-permute-start | bytes 3080 | tf_op jit(solution)/shard_map/ppermute | solution.py:344
  64.6 17.7 %collective-permute-start.7 = (f32[3,2,4,24,128]{4,3,2,1,0:T(8,128)S(1)}, f32[3,2,4,24,128]{4,3,2,1,0:T(8,128)S(1)}, u32[]{:S(2)}, u32[]{:S(2)}) collective-permute-start(f32[3,2,4,24,128]{4,3,2,1,0:T(8,128)S(1)} %get-tuple-element.47), channel_id=1, source_target_pairs={{0,2},{1,3},{2,0},{3,1},{4,6},{5,7},{6,4},{7,5},{8,10},{9,11},{10,... | collective-permute-start | bytes 884744 | tf_op jit(solution)/shard_map/ppermute | solution.py:344
  66.6 15.6 %collective-permute-start.8 = (f32[3,2,4,24,128]{4,3,2,1,0:T(8,128)S(1)}, f32[3,2,4,24,128]{4,3,2,1,0:T(8,128)S(1)}, u32[]{:S(2)}, u32[]{:S(2)}) collective-permute-start(f32[3,2,4,24,128]{4,3,2,1,0:T(8,128)S(1)} %get-tuple-element.48), channel_id=1, source_target_pairs={{0,4},{1,5},{2,6},{3,7},{4,0},{5,1},{6,2},{7,3},{8,12},{9,13},{10,... | collective-permute-start | bytes 884744 | tf_op jit(solution)/shard_map/ppermute | solution.py:344
  69.2 13.1 %collective-permute-start.9 = (f32[3,2,4,24,128]{4,3,2,1,0:T(8,128)S(1)}, f32[3,2,4,24,128]{4,3,2,1,0:T(8,128)S(1)}, u32[]{:S(2)}, u32[]{:S(2)}) collective-permute-start(f32[3,2,4,24,128]{4,3,2,1,0:T(8,128)S(1)} %get-tuple-element.49), channel_id=1, source_target_pairs={{0,6},{1,7},{2,4},{3,5},{4,2},{5,3},{6,0},{7,1},{8,14},{9,15},{10,... | collective-permute-start | bytes 884744 | tf_op jit(solution)/shard_map/ppermute | solution.py:344
  70.3 7.0 %collective-permute-start.12 = (f32[2,4,4,8,128]{4,3,2,1,0:T(8,128)S(1)}, f32[2,4,4,8,128]{4,3,2,1,0:T(8,128)S(1)}, u32[]{:S(2)}, u32[]{:S(2)}) collective-permute-start(f32[2,4,4,8,128]{4,3,2,1,0:T(8,128)S(1)} %get-tuple-element.55), channel_id=1, source_target_pairs={{0,8},{1,9},{2,10},{3,11},{4,12},{5,13},{6,14},{7,15},{8,16},{9,17... | collective-permute-start | bytes 393224 | tf_op jit(solution)/shard_map/ppermute | solution.py:344
  70.3 10.2 %collective-permute-start.13 = (f32[2,4,4,8,128]{4,3,2,1,0:T(8,128)S(1)}, f32[2,4,4,8,128]{4,3,2,1,0:T(8,128)S(1)}, u32[]{:S(2)}, u32[]{:S(2)}) collective-permute-start(f32[2,4,4,8,128]{4,3,2,1,0:T(8,128)S(1)} %get-tuple-element.56), channel_id=1, source_target_pairs={{0,16},{1,17},{2,18},{3,19},{4,20},{5,21},{6,22},{7,23},{8,24},{9,... | collective-permute-start | bytes 393224 | tf_op jit(solution)/shard_map/ppermute | solution.py:344
  77.3 5.0 %collective-permute-start.14 = (f32[2,4,4,8,128]{4,3,2,1,0:T(8,128)S(1)}, f32[2,4,4,8,128]{4,3,2,1,0:T(8,128)S(1)}, u32[]{:S(2)}, u32[]{:S(2)}) collective-permute-start(f32[2,4,4,8,128]{4,3,2,1,0:T(8,128)S(1)} %get-tuple-element.57), channel_id=1, source_target_pairs={{0,24},{1,25},{2,26},{3,27},{4,28},{5,29},{6,30},{7,31},{8,0},{9,1... | collective-permute-start | bytes 393224 | tf_op jit(solution)/shard_map/ppermute | solution.py:344
  80.5 3.6 %collective-permute-start.11 = (f32[4,4,32,128]{3,2,1,0:T(8,128)S(1)}, f32[4,4,32,128]{3,2,1,0:T(8,128)S(1)}, u32[]{:S(2)}, u32[]{:S(2)}) collective-permute-start(f32[4,4,32,128]{3,2,1,0:T(8,128)S(1)} %get-tuple-element.54), channel_id=1, source_target_pairs={{0,1},{1,0},{2,3},{3,2},{4,5},{5,4},{6,7},{7,6},{8,9},{9,8},{10,11... | collective-permute-start | bytes 786440 | tf_op jit(solution)/shard_map/ppermute | solution.py:344
  83.5 2.9 %collective-permute-start.10 = (f32[3,8,24,128]{3,2,1,0:T(8,128)S(1)}, f32[3,8,24,128]{3,2,1,0:T(8,128)S(1)}, u32[]{:S(2)}, u32[]{:S(2)}) collective-permute-start(f32[3,8,24,128]{3,2,1,0:T(8,128)S(1)} %get-tuple-element.51), channel_id=1, source_target_pairs={{0,1},{1,0},{2,3},{3,2},{4,5},{5,4},{6,7},{7,6},{8,9},{9,8},{10,11... | collective-permute-start | bytes 884744 | tf_op jit(solution)/shard_map/ppermute | solution.py:344
  83.6 1.8 %collective-permute-start.15 = (f32[3,4,4,8,128]{4,3,2,1,0:T(8,128)S(1)}, f32[3,4,4,8,128]{4,3,2,1,0:T(8,128)S(1)}, u32[]{:S(2)}, u32[]{:S(2)}) collective-permute-start(f32[3,4,4,8,128]{4,3,2,1,0:T(8,128)S(1)} %pad_maximum_fusion), channel_id=1, source_target_pairs={{0,1},{1,0},{2,3},{3,2},{4,5},{5,4},{6,7},{7,6},{8,9},{9,8},{10,11... | collective-permute-start | bytes 589832 | tf_op jit(solution)/shard_map/ppermute | solution.py:344
  86.5 6.8 %collective-permute-start.19 = (f32[8,24,128]{2,1,0:T(8,128)S(1)}, f32[8,24,128]{2,1,0:T(8,128)S(1)}, u32[]{:S(2)}, u32[]{:S(2)}) collective-permute-start(f32[8,24,128]{2,1,0:T(8,128)S(1)} %get-tuple-element.66), channel_id=1, source_target_pairs={{0,8},{1,9},{2,10},{3,11},{4,12},{5,13},{6,14},{7,15},{8,16},{9,17... | collective-permute-start | bytes 294920 | tf_op jit(solution)/shard_map/ppermute | solution.py:344
  87.8 11.7 %collective-permute-start.16 = (f32[8,32,128]{2,1,0:T(8,128)S(1)}, f32[8,32,128]{2,1,0:T(8,128)S(1)}, u32[]{:S(2)}, u32[]{:S(2)}) collective-permute-start(f32[8,32,128]{2,1,0:T(8,128)S(1)} %get-tuple-element.63), channel_id=1, source_target_pairs={{0,2},{1,3},{2,0},{3,1},{4,6},{5,7},{6,4},{7,5},{8,10},{9,11},{10,... | collective-permute-start | bytes 393224 | tf_op jit(solution)/shard_map/ppermute | solution.py:344
  89.4 10.1 %collective-permute-start.17 = (f32[8,32,128]{2,1,0:T(8,128)S(1)}, f32[8,32,128]{2,1,0:T(8,128)S(1)}, u32[]{:S(2)}, u32[]{:S(2)}) collective-permute-start(f32[8,32,128]{2,1,0:T(8,128)S(1)} %get-tuple-element.64), channel_id=1, source_target_pairs={{0,4},{1,5},{2,6},{3,7},{4,0},{5,1},{6,2},{7,3},{8,12},{9,13},{10,... | collective-permute-start | bytes 393224 | tf_op jit(solution)/shard_map/ppermute | solution.py:344
  90.6 8.9 %collective-permute-start.18 = (f32[8,32,128]{2,1,0:T(8,128)S(1)}, f32[8,32,128]{2,1,0:T(8,128)S(1)}, u32[]{:S(2)}, u32[]{:S(2)}) collective-permute-start(f32[8,32,128]{2,1,0:T(8,128)S(1)} %get-tuple-element.65), channel_id=1, source_target_pairs={{0,6},{1,7},{2,4},{3,5},{4,2},{5,3},{6,0},{7,1},{8,14},{9,15},{10,... | collective-permute-start | bytes 393224 | tf_op jit(solution)/shard_map/ppermute | solution.py:344
  91.3 8.2 %collective-permute-start.20 = (f32[8,24,128]{2,1,0:T(8,128)S(1)}, f32[8,24,128]{2,1,0:T(8,128)S(1)}, u32[]{:S(2)}, u32[]{:S(2)}) collective-permute-start(f32[8,24,128]{2,1,0:T(8,128)S(1)} %get-tuple-element.67), channel_id=1, source_target_pairs={{0,16},{1,17},{2,18},{3,19},{4,20},{5,21},{6,22},{7,23},{8,24},{9,... | collective-permute-start | bytes 294920 | tf_op jit(solution)/shard_map/ppermute | solution.py:344
  93.3 6.2 %collective-permute-start.21 = (f32[8,24,128]{2,1,0:T(8,128)S(1)}, f32[8,24,128]{2,1,0:T(8,128)S(1)}, u32[]{:S(2)}, u32[]{:S(2)}) collective-permute-start(f32[8,24,128]{2,1,0:T(8,128)S(1)} %get-tuple-element.68), channel_id=1, source_target_pairs={{0,24},{1,25},{2,26},{3,27},{4,28},{5,29},{6,30},{7,31},{8,0},{9,1... | collective-permute-start | bytes 294920 | tf_op jit(solution)/shard_map/ppermute | solution.py:344
  (2 other events, 1.4 us)
where the time goes:
time: 101 us; the launch traced here: 100 us
  Pallas kernels  33.7 us (33%)
  starting transfers between devices  32.4 us (32%)
  waiting for transfers between devices  29.9 us (30%)
  local copies, waits for them, and re-layouts  3.4 us (3%)
    ppermute x22, waiting for transfers between devices, across(): return lax.ppermute(value, 'elem', [(i, partner(i)) for i in range(n)])  29.9 us
    ppermute x22, starting transfers between devices, across(): return lax.ppermute(value, 'elem', [(i, partner(i)) for i in range(n)])  25.1 us
    pallas_call x1, Pallas kernels, body(): pl.pallas_call(functools.partial(near_kernel, n), grid=(rows,), out_shape...  22.7 us
    all_to_all x1, starting transfers between devices, body(): lax.all_to_all(send.reshape(n, serve_count * B, LANES), 'elem', split_axi...  7.3 us
    pallas_call x1, Pallas kernels, body(): pl.pallas_call(functools.partial(far_kernel, n, cap), out_shape=slot_shap...  4.79 us
    pallas_call x1, Pallas kernels, body(): pl.pallas_call(functools.partial(prep_kernel, n), out_shape=(shape((rows,...  3.18 us
    unnamed x7, local copies, waits for them, and re-layouts  3.01 us
    pallas_call x2, Pallas kernels, combine(): pl.pallas_call(functools.partial(kernel, n), out_shape=out_shape, in_spec...  2.22 us
  transfers between devices with their start and end apart: 23, of which 7 were waited for; matrix products, arithmetic and copies ran while one was open for 3% of the time, Pallas kernels for 25%

commit v1 on v0

--- a/solution.py
+++ b/solution.py
@@ -14,10 +14,10 @@
 PLACES = 4
 GROUP = 2 * PLACES
 CHUNKS = 4
-FIRST = 24
-REST = HALF - FIRST
-DEPTH = 3
-UNROLL = 16
+REST = HALF // 2
+FETCH = 16
+DEPTH = 6
+UNROLL = 32
 META = 8
 MIB = 1 << 20
 
@@ -30,6 +30,15 @@
     high = value.astype(jnp.bfloat16)
     low = (value - high.astype(jnp.float32)).astype(jnp.bfloat16)
     return jnp.concatenate([high, high, low, low], axis=0)
+
+
+def split_steps(groups):
+    steps, first = {}, 0
+    for step in range(1, groups):
+        rows = HALF if step == groups // 2 else HALF - REST
+        steps[step] = first, rows
+        first += rows
+    return steps, first, [step for step, (_, rows) in steps.items() if rows < HALF]
 
 
 def params(mib, **more):
@@ -87,12 +96,15 @@
 
 
 def add_products(acc, out, dest):
-    mask = low_lanes(B)
+    mask = low_lanes(HALF)
     for p in range(2):
-        rows = out[p * B : (p + 1) * B]
-        left = jnp.where(mask, rows, 0.0)
-        acc[dest[2 * p]] += left
-        acc[dest[2 * p + 1]] += rows - left
+        even, odd = out[p * B : p * B + HALF], out[p * B + HALF : (p + 1) * B]
+        turned = pltpu.roll(jnp.where(mask, odd, even), B, 1)
+        first, second = dest[2 * p], dest[2 * p + 1]
+        left, right = jnp.where(mask, even, turned), jnp.where(mask, turned, odd)
+        old_first, old_second = acc[first], acc[second]
+        acc[first] = old_first + left
+        acc[second] = old_second + right + jnp.where(first == second, left, 0.0)
 
 
 def add_entry(acc, meta, e, lp, right_ref):
@@ -101,19 +113,13 @@
     add_products(acc, out, [meta[e * META + 1 + j] for j in range(4)])
 
 
-def fold(acc, slot):
-    mask = low_lanes(HALF)
-    even, odd = acc[slot, :HALF], acc[slot, HALF:]
-    return jnp.where(mask, even, odd) + pltpu.roll(jnp.where(mask, odd, even), B, 1)
-
-
 def near_kernel(
-    n, count_row, a_slot, contrib, me_ref, own_ref, a_ref, left_hbm, slots_hbm, meta_ref, acc, left_ref, slots_ref, turned_rows, near_meta, place_of, sems
+    n, count_row, a_slot, contrib, me_ref, own_ref, a_ref, left_hbm, slots_hbm, meta_ref, acc, left_ref, turned_rows, near_meta, place_of, sems
 ):
     step = pl.program_id(0)
     rows = own_ref.shape[0]
     blocks = a_ref.shape[1]
-    slot_count = slots_ref.shape[0]
+    slot_count = acc.shape[0] - 1
     per_row = contrib.shape[1] // 2
     entries = rows * blocks
     last = near_meta.shape[0] - 1
@@ -194,12 +200,7 @@
 
         lax.fori_loop(0, (near_meta[last] + UNROLL - 1) // UNROLL, products, 0)
 
-        def pack(slot, carry):
-            slots_ref[slot] = fold(acc, slot)
-            return carry
-
-        lax.fori_loop(0, slot_count, pack, 0, unroll=8)
-        slots_copy = pltpu.make_async_copy(slots_ref, slots_hbm, sems.at[1])
+        slots_copy = pltpu.make_async_copy(acc.at[pl.ds(0, slot_count)], slots_hbm, sems.at[1])
         slots_copy.start()
         left_copy.wait()
         slots_copy.wait()
@@ -207,32 +208,40 @@
 
 def far_kernel(n, cap, me_ref, meta, left_hbm, recv, near_hbm, *refs):
     groups = n // GROUP
-    far_slots, rest_slots = refs[:PLACES], refs[PLACES : PLACES + groups - 1]
-    own_mine, own_other, acc, near, ring, ring_sems, near_sem = refs[PLACES + groups - 1 :]
+    steps, _, rest_steps = split_steps(groups)
+    outs = PLACES + len(rest_steps)
+    far_slots, rest_slots = refs[:PLACES], dict(zip(rest_steps, refs[PLACES:outs]))
+    own_mine, own_other, acc, near, ring, ring_sems, near_sem = refs[outs:]
     me = me_ref[0]
     count = meta[meta.shape[0] - 1]
     turns = (count + UNROLL - 1) // UNROLL
 
-    def left_copy(g):
-        buffer = lax.rem(g, DEPTH)
-        return pltpu.make_async_copy(left_hbm.at[pl.ds(g * UNROLL, UNROLL)], ring.at[buffer], ring_sems.at[buffer])
+    per_turn = UNROLL // FETCH
+
+    def left_copy(i):
+        buffer = lax.rem(i, DEPTH)
+        return pltpu.make_async_copy(left_hbm.at[pl.ds(i * FETCH, FETCH)], ring.at[buffer], ring_sems.at[buffer])
 
     def fetch(g):
         @pl.when(g < turns)
         def go():
-            left_copy(g).start()
-
-    for g in range(DEPTH - 1):
+            for i in range(per_turn):
+                left_copy(g * per_turn + i).start()
+
+    ahead = DEPTH // per_turn - 1
+    for g in range(ahead):
         fetch(g)
+    acc[...] = jnp.zeros_like(acc)
     near_copy = pltpu.make_async_copy(near_hbm, near, near_sem)
     near_copy.start()
-    acc[...] = jnp.zeros_like(acc)
 
     def products(g, carry):
-        fetch(g + DEPTH - 1)
-        left_copy(g).wait()
+        fetch(g + ahead)
+        for i in range(per_turn):
+            left_copy(g * per_turn + i).wait()
         for u in range(UNROLL):
-            add_entry(acc, meta, g * UNROLL + u, ring[lax.rem(g, DEPTH), u], recv)
+            buffer = lax.rem(g * per_turn + u // FETCH, DEPTH)
+            add_entry(acc, meta, g * UNROLL + u, ring[buffer, u % FETCH], recv)
         return carry
 
     lax.fori_loop(0, turns, products, 0)
@@ -247,22 +256,25 @@
         at = jnp.where(at >= groups, at - groups, at)
         m = at * GROUP + (place ^ j) * 2 + side - me
         m = jnp.where(m < 0, m + n, m)
-        return [fold(acc, m * cap + c) + near[m * cap + c] for c in range(cap)]
+        return [acc[m * cap + c] + near[m * cap + c] for c in range(cap)]
 
     for j in range(PLACES):
         for other in range(2):
             side = 1 - core if other else core
-            for step in range(1, groups):
+            for step, (first, count) in steps.items():
                 for c, slot in enumerate(packed(j, step, side)):
-                    far_slots[j][step - 1, side, c] = slot[:FIRST]
-                    rest_slots[step - 1][other, j, c] = slot[FIRST:]
+                    far_slots[j][side, c, first : first + count] = slot[:count]
+                    if step in rest_slots:
+                        rest_slots[step][other, j, c] = slot[count:]
             for c, slot in enumerate(packed(j, 0, side)):
                 (own_other if other else own_mine)[j, c] = slot
 
 
-def add_slots(target, table, entry, m, slots, first=0):
+def add_slots(target, table, entry, m, slots, rows=None, from_rows=None):
+    rows = pl.ds(0, HALF) if rows is None else rows
     for c in range(slots.shape[0]):
-        target[table[entry * slots.shape[0] + c, m], pl.ds(first, slots.shape[1]), :] += slots[c]
+        value = slots[c] if from_rows is None else slots[c, from_rows]
+        target[table[entry * slots.shape[0] + c, m], rows, :] += value
 
 
 def combine_far_kernel(n, me_ref, table, *refs):
@@ -273,19 +285,18 @@
     place = lax.rem(me // 2, PLACES)
     group = me // GROUP
 
-    def gather(step, carry):
+    steps, _, _ = split_steps(groups)
+    for target in (mine, other):
+        target[...] = jnp.zeros_like(target)
+    for step, (first, count) in steps.items():
+        part = pl.ds(first, count)
         at = group + step
         at = jnp.where(at >= groups, at - groups, at)
         for target, side in ((mine, core), (other, 1 - core)):
-            tiles = target.at[step - 1]
-            tiles[...] = jnp.zeros_like(tiles)
             for j in range(PLACES):
                 m = (at - group) * GROUP + (place - (place ^ j)) * 2 + side - core
                 m = jnp.where(m < 0, m + n, m)
-                add_slots(tiles, table, (at ^ group) * 2 + (side ^ core), m, slots[j].at[step - 1, side])
-        return carry
-
-    lax.fori_loop(1, groups, gather, 0)
+                add_slots(target, table, (at ^ group) * 2 + (side ^ core), m, slots[j].at[side], part, part)
 
 
 def combine_own_kernel(n, me_ref, table, mine, got, rest_got, *refs):
@@ -299,20 +310,19 @@
             m = ((place ^ j) - place) * 2 + other * (2 * core - 1)
             m = jnp.where(m < 0, m + n, m)
             add_slots(tiles[j], table, j, m, (got if other else mine).at[j])
-            for step, rest in enumerate(rest_mine, 1):
+            for index, step in enumerate(split_steps(n // GROUP)[2]):
                 at = m + step * GROUP
                 at = jnp.where(at >= n, at - n, at)
-                add_slots(tiles[j], table, j, at, rest_got.at[step - 1, j] if other else rest.at[0, j], FIRST)
+                rest = rest_got.at[index, j] if other else rest_mine[index].at[0, j]
+                add_slots(tiles[j], table, j, at, rest, pl.ds(HALF - REST, REST))
 
 
 def final_kernel(*refs):
     own, far, out_ref, total = refs[:PLACES], refs[PLACES:-2], refs[-2], refs[-1]
     for t in range(TO):
         total[t * HALF : (t + 1) * HALF] = own[0][t] + own[1][t] + own[2][t] + own[3][t]
-        value = far[0][t]
-        for part in far[1:]:
-            value = value + part[t]
-        total[t * HALF : t * HALF + FIRST] += value
+        for part in far:
+            total[t * HALF : t * HALF + part.shape[1]] += part[t]
     for r in range(HALF):
         out_ref[:, r * LANES : (r + 1) * LANES] = total[pl.ds(r, TO, stride=HALF), :]
 
@@ -391,9 +401,8 @@
         in_specs=[smem, smem, smem, smem, vmem, pl.BlockSpec((1, blocks, HALF, LANES), lambda i: (i, 0, 0, 0))],
         out_specs=(hbm, hbm, smem),
         scratch_shapes=[
-            pltpu.VMEM((slot_count + 1, B, LANES), f32),
+            pltpu.VMEM((slot_count + 1, HALF, LANES), f32),
             pltpu.VMEM((entries + UNROLL, 2 * B, LANES), bf16),
-            pltpu.VMEM((slot_count, HALF, LANES), f32),
             pltpu.VMEM((2 * B, LANES), f32),
             pltpu.SMEM((meta_size,), i32),
             pltpu.SMEM((entries,), i32),
@@ -404,8 +413,9 @@
         name="near",
     )(row_count, a_slot.T, contrib_slot, me, pin(own), a_tiles)
 
-    slot_shapes = [shape((groups - 1, 2, cap, FIRST, LANES), f32)] * PLACES
-    slot_shapes += [shape((2, PLACES, cap, REST, LANES), f32)] * (groups - 1)
+    steps, far_rows, rest_steps = split_steps(groups)
+    slot_shapes = [shape((2, cap, far_rows, LANES), f32)] * PLACES
+    slot_shapes += [shape((2, PLACES, cap, REST, LANES), f32)] * len(rest_steps)
     slot_shapes += [shape((PLACES, cap, HALF, LANES), f32)] * 2
     slots = pl.pallas_call(
         functools.partial(far_kernel, n, cap),
@@ -413,9 +423,9 @@
         in_specs=[smem, smem, hbm, vmem, hbm],
         out_specs=[vmem] * len(slot_shapes),
         scratch_shapes=[
-            pltpu.VMEM((slot_count + 1, B, LANES), f32),
+            pltpu.VMEM((slot_count + 1, HALF, LANES), f32),
             pltpu.VMEM((slot_count, HALF, LANES), f32),
-            pltpu.VMEM((DEPTH, UNROLL, 2 * B, LANES), bf16),
+            pltpu.VMEM((DEPTH, FETCH, 2 * B, LANES), bf16),
             pltpu.SemaphoreType.DMA((DEPTH,)),
             pltpu.SemaphoreType.DMA,
         ],
@@ -438,23 +448,23 @@
         return [values[0]] + [across(values[j], lambda i, j=j: i ^ (2 * j)) for j in range(1, PLACES)]
 
     def over_groups(values):
-        return [across(value, lambda i, step=step: (i + step * GROUP) % n) for step, value in enumerate(values, 1)]
+        return [across(value, lambda i, step=step: (i + step * GROUP) % n) for step, value in values]
 
     def other_core(value):
         return across(value, lambda i: i ^ 1)
 
     own_mine, own_other = slots[-2:]
-    rest = over_groups(slots[PLACES:-2])
+    rest = over_groups(zip(rest_steps, slots[PLACES:-2]))
     far_slots = in_group(slots[:PLACES])
     rest_got = other_core(jnp.stack([part[1] for part in rest]))
     own_shape = [shape((TO, HALF, LANES), f32)] * PLACES
     own_tiles = combine(combine_own_kernel, own_shape, own_table, [own_mine, other_core(own_other), rest_got] + rest)
-    far_shape = [shape((groups - 1, TO, FIRST, LANES), f32)] * 2
+    far_shape = [shape((TO, far_rows, LANES), f32)] * 2
     mine, other = combine(combine_far_kernel, far_shape, far_table, far_slots)
     got = other_core(other)
-    summed = [mine[step] + got[step] for step in range(groups - 1)]
+    summed = [mine[:, first : first + count] + got[:, first : first + count] for first, count in steps.values()]
     summed, own_tiles = lax.optimization_barrier((summed, own_tiles))
-    far_parts = over_groups(summed)
+    far_parts = over_groups(zip(steps, summed))
     parts = in_group(own_tiles) + far_parts
 
     return pl.pallas_call(

time: 101 us -> 99.3 us (0.983)
  Pallas kernels: 33.7 us -> 31.8 us
  starting transfers between devices: 32.4 us -> 33.9 us
    ppermute x22 -> x21, starting transfers between devices: 25.1 us -> 26.6 us  [across(): return lax.ppermute(value, 'elem', [(i, partner(i)) for i in range(n)])]
    pallas_call x1, Pallas kernels: 22.7 us -> 21.3 us  [body(): pl.pallas_call(functools.partial(near_kernel, n), grid=(rows,), out_shape...]
    ppermute x22 -> x21, waiting for transfers between devices: 29.9 us -> 28.9 us  [across(): return lax.ppermute(value, 'elem', [(i, partner(i)) for i in range(n)])]
  transfers between devices with their start and end apart: 23 -> 22, of which waited for: 7 -> 9; matrix products, arithmetic and copies ran while one was open for 3% -> 3% of each run, Pallas kernels for 25% -> 23%
where the time goes in v1:
time: 99.3 us; the launch traced here: 98.9 us
  starting transfers between devices  33.9 us (34%)
  Pallas kernels  31.8 us (32%)
  waiting for transfers between devices  28.9 us (29%)
  local copies, waits for them, and re-layouts  3.4 us (3%)
    ppermute x21, waiting for transfers between devices, across(): return lax.ppermute(value, 'elem', [(i, partner(i)) for i in range(n)])  28.9 us
    ppermute x21, starting transfers between devices, across(): return lax.ppermute(value, 'elem', [(i, partner(i)) for i in range(n)])  26.6 us
    pallas_call x1, Pallas kernels, body(): pl.pallas_call(functools.partial(near_kernel, n), grid=(rows,), out_shape...  21.3 us
    all_to_all x1, starting transfers between devices, body(): lax.all_to_all(send.reshape(n, serve_count * B, LANES), 'elem', split_axi...  7.3 us
    pallas_call x1, Pallas kernels, body(): pl.pallas_call(functools.partial(far_kernel, n, cap), out_shape=slot_shap...  4.54 us
    pallas_call x1, Pallas kernels, body(): pl.pallas_call(functools.partial(prep_kernel, n), out_shape=(shape((rows,...  3.16 us
    unnamed x7, local copies, waits for them, and re-layouts  3.01 us
    pallas_call x2, Pallas kernels, combine(): pl.pallas_call(functools.partial(kernel, n), out_shape=out_shape, in_spec...  2.07 us
  transfers between devices with their start and end apart: 22, of which 9 were waited for; matrix products, arithmetic and copies ran while one was open for 3% of the time, Pallas kernels for 23%

profile of v1, /device:TPU:0, one launch (start us, length us, event | category | flops | bytes accessed | tf_op | source)
XLA Modules:
  0.0 98.9 jit_solution(11199868676438771662)
XLA Ops:
  0.0 3.2 %prep.1 = (f32[32,64,128]{2,1,0:T(8,128)S(1)}, f32[32,2,64,128]{3,2,1,0:T(8,128)}) custom-call(s32[1]{0:T(128)} %bitcast.me_ref, s32[2,31]{1,0:T(2,128)} %bitcast.35, f32[32,64,128]{2,1,0:T(8,128)} %bitcast.28), custom_call_target="tpu_custom_call" | custom-call | tf_op jit(solution)/shard_map/prep/pallas_call | solution.py:357
  3.2 7.3 %all-to-all-start = ((f32[32,128,128]{2,1,0:T(8,128)}), f32[32,128,128]{2,1,0:T(8,128)S(1)}, u32[]{:S(2)}, u32[]{:S(2)}) async-start(f32[32,128,128]{2,1,0:T(8,128)} %bitcast.27), calls=%async_computation | async-start | bytes 4194304 | tf_op jit(solution)/shard_map/all_to_all | solution.py:374
  10.8 2.6 %collective-permute-start.2 = (s32[1,4,32]{2,1,0:T(4,128)S(1)}, s32[1,4,32]{2,1,0:T(4,128)S(1)}, u32[]{:S(2)}, u32[]{:S(2)}) collective-permute-start(s32[1,4,32]{2,1,0:T(4,128)S(1)} %bitcast.30), channel_id=1, source_target_pairs={{0,6},{1,7},{2,4},{3,5},{4,2},{5,3},{6,0},{7,1},{8,14},{9,15},{10,... | collective-permute-start | bytes 1544 | tf_op jit(solution)/shard_map/ppermute | solution.py:354
  15.0 3.6 %collective-permute-start.6 = (s32[2,4,32]{2,1,0:T(4,128)S(1)}, s32[2,4,32]{2,1,0:T(4,128)S(1)}, u32[]{:S(2)}, u32[]{:S(2)}) collective-permute-start(s32[2,4,32]{2,1,0:T(4,128)S(1)} %pad_add_fusion.2), channel_id=1, source_target_pairs={{0,24},{1,25},{2,26},{3,27},{4,28},{5,29},{6,30},{7,31},{8,16},{9,... | collective-permute-start | bytes 3080 | tf_op jit(solution)/shard_map/ppermute | solution.py:354
  18.6 2.7 %copy.12 = f32[28,8,32,128]{3,2,1,0:T(8,128)S(1)} copy(f32[28,8,32,128]{3,1,2,0:T(8,128)} %bitcast.26) | data formatting | bytes 7340032
  22.0 21.3 %near.1 = (bf16[256,128,128]{2,1,0:T(8,128)(2,1)}, f32[128,32,128]{2,1,0:T(8,128)}, s32[2304]{0:T(1024)S(1)}) custom-call(s32[1]{0:T(128)S(6)} %copy.13.count_row, s32[7,32]{1,0:T(8,128)S(1)} %bitcast.24, s32[32,28]{1,0:T(8,128)S(1)} %copy-done, s32[1]{0:T(128)} %bitcast.me_ref, f32[32,64,128]{2,1,0:T(8,128)S(1)} %get-tuple-element.39.own_ref, ...), custom_call_target="tpu_custom_call" | custom-call | flops 3758096384 | bytes 16777216 | tf_op jit(solution)/shard_map/near/pallas_call | solution.py:393
  43.3 1.3 %collective-permute-start.4 = (s32[2,4,32]{2,1,0:T(4,128)S(1)}, s32[2,4,32]{2,1,0:T(4,128)S(1)}, u32[]{:S(2)}, u32[]{:S(2)}) collective-permute-start(s32[2,4,32]{2,1,0:T(4,128)S(1)} %pad_add_fusion.2), channel_id=1, source_target_pairs={{0,8},{1,9},{2,10},{3,11},{4,12},{5,13},{6,14},{7,15},{8,0},{9,1},... | collective-permute-start | bytes 3080 | tf_op jit(solution)/shard_map/ppermute | solution.py:354
  44.6 4.7 %collective-permute-done.6 = s32[2,4,32]{2,1,0:T(4,128)S(1)} collective-permute-done((s32[2,4,32]{2,1,0:T(4,128)S(1)}, s32[2,4,32]{2,1,0:T(4,128)S(1)}, u32[]{:S(2)}, u32[]{:S(2)}) %collective-permute-start.6) | collective-permute-done | bytes 1056 | tf_op jit(solution)/shard_map/ppermute | solution.py:354
  49.3 10.4 %collective-permute-done.5 = s32[2,4,32]{2,1,0:T(4,128)S(1)} collective-permute-done((s32[2,4,32]{2,1,0:T(4,128)S(1)}, s32[2,4,32]{2,1,0:T(4,128)S(1)}, u32[]{:S(2)}, u32[]{:S(2)}) %collective-permute-start.5) | collective-permute-done | bytes 1056 | tf_op jit(solution)/shard_map/ppermute | solution.py:354
  59.8 4.5 %far.1 = (f32[2,4,64,128]{3,2,1,0:T(8,128)S(1)}, f32[2,4,64,128]{3,2,1,0:T(8,128)S(1)}, f32[2,4,64,128]{3,2,1,0:T(8,128)S(1)}, f32[2,4,64,128]{3,2,1,0:T(8,128)S...) custom-call(s32[1]{0:T(128)} %bitcast.me_ref, ...), custom_call_target="tpu_custom_call" | custom-call | flops 1879048192 | bytes 16777216 | tf_op jit(solution)/shard_map/far/pallas_call | solution.py:420
  64.3 1.4 %collective-permute-start.7 = (f32[2,4,64,128]{3,2,1,0:T(8,128)S(1)}, f32[2,4,64,128]{3,2,1,0:T(8,128)S(1)}, u32[]{:S(2)}, u32[]{:S(2)}) collective-permute-start(f32[2,4,64,128]{3,2,1,0:T(8,128)S(1)} %get-tuple-element.46), channel_id=1, source_target_pairs={{0,2},{1,3},{2,0},{3,1},{4,6},{5,7},{6,4},{7,5},{8,10},{9,11},{10,... | collective-permute-start | bytes 786440 | tf_op jit(solution)/shard_map/ppermute | solution.py:354
  65.7 2.3 %collective-permute-start.8 = (f32[2,4,64,128]{3,2,1,0:T(8,128)S(1)}, f32[2,4,64,128]{3,2,1,0:T(8,128)S(1)}, u32[]{:S(2)}, u32[]{:S(2)}) collective-permute-start(f32[2,4,64,128]{3,2,1,0:T(8,128)S(1)} %get-tuple-element.47), channel_id=1, source_target_pairs={{0,4},{1,5},{2,6},{3,7},{4,0},{5,1},{6,2},{7,3},{8,12},{9,13},{10,... | collective-permute-start | bytes 786440 | tf_op jit(solution)/shard_map/ppermute | solution.py:354
  69.4 3.2 %collective-permute-start.13 = (f32[2,4,4,16,128]{4,3,2,1,0:T(8,128)S(1)}, f32[2,4,4,16,128]{4,3,2,1,0:T(8,128)S(1)}, u32[]{:S(2)}, u32[]{:S(2)}) collective-permute-start(f32[2,4,4,16,128]{4,3,2,1,0:T(8,128)S(1)} %get-tuple-element.55), channel_id=1, source_target_pairs={{0,24},{1,25},{2,26},{3,27},{4,28},{5,29},{6,30},{7,31},{8,0},{9,1... | collective-permute-start | bytes 786440 | tf_op jit(solution)/shard_map/ppermute | solution.py:354
  73.3 6.3 %collective-permute-done.8.refs_2_ = f32[2,4,64,128]{3,2,1,0:T(8,128)S(1)} collective-permute-done((f32[2,4,64,128]{3,2,1,0:T(8,128)S(1)}, f32[2,4,64,128]{3,2,1,0:T(8,128)S(1)}, u32[]{:S(2)}, u32[]{:S(2)}) %collective-permute-start.8) | collective-permute-done | bytes 262176 | tf_op jit(solution)/shard_map/ppermute | solution.py:354
  79.6 1.1 %combine_far_kernel.1 = (f32[8,64,128]{2,1,0:T(8,128)S(1)}, f32[8,64,128]{2,1,0:T(8,128)S(1)}) custom-call(s32[1]{0:T(128)} %bitcast.me_ref, s32[32,32]{1,0:T(8,128)S(1)} %bitcast.22, f32[2,4,64,128]{3,2,1,0:T(8,128)S(1)} %get-tuple-element.45.refs_0_, f32[2,4,64,128]{3,2,1,0:T(8,128)S(1)} %collective-permute-done.7.refs_1_, ...), custom_call_target="tpu_custom_call" | custom-call | tf_op jit(solution)/shard_map/combine_far_kernel/pallas_call | solution.py:438
  82.7 1.1 %collective-permute-done.14.rest_got = f32[2,4,4,16,128]{4,3,2,1,0:T(8,128)S(1)} collective-permute-done((f32[2,4,4,16,128]{4,3,2,1,0:T(8,128)S(1)}, f32[2,4,4,16,128]{4,3,2,1,0:T(8,128)S(1)}, u32[]{:S(2)}, u32[]{:S(2)}) %collective-permute-start.14) | collective-permute-done | bytes 262176 | tf_op jit(solution)/shard_map/ppermute | solution.py:354
  83.8 0.9 combine_own_kernel.1
  85.6 0.9 collective-permute-start.15
  86.4 1.7 %collective-permute-start.16 = (f32[8,32,128]{2,1,0:T(8,128)S(1)}, f32[8,32,128]{2,1,0:T(8,128)S(1)}, u32[]{:S(2)}, u32[]{:S(2)}) collective-permute-start(f32[8,32,128]{2,1,0:T(8,128)S(1)} %get-tuple-element.62), channel_id=1, source_target_pairs={{0,4},{1,5},{2,6},{3,7},{4,0},{5,1},{6,2},{7,3},{8,12},{9,13},{10,... | collective-permute-start | bytes 393224 | tf_op jit(solution)/shard_map/ppermute | solution.py:354
  88.2 0.9 collective-permute-start.17
  89.1 1.9 %collective-permute-start.19 = (f32[8,32,128]{2,1,0:T(8,128)S(1)}, f32[8,32,128]{2,1,0:T(8,128)S(1)}, u32[]{:S(2)}, u32[]{:S(2)}) collective-permute-start(f32[8,32,128]{2,1,0:T(8,128)S(1)} %slice_add_fusion), channel_id=1, source_target_pairs={{0,16},{1,17},{2,18},{3,19},{4,20},{5,21},{6,22},{7,23},{8,24},{9,... | collective-permute-start | bytes 393224 | tf_op jit(solution)/shard_map/ppermute | solution.py:354
  90.9 2.7 %collective-permute-start.20 = (f32[8,16,128]{2,1,0:T(8,128)S(1)}, f32[8,16,128]{2,1,0:T(8,128)S(1)}, u32[]{:S(2)}, u32[]{:S(2)}) collective-permute-start(f32[8,16,128]{2,1,0:T(8,128)S(1)} %get-tuple-element.66), channel_id=1, source_target_pairs={{0,24},{1,25},{2,26},{3,27},{4,28},{5,29},{6,30},{7,31},{8,0},{9,1... | collective-permute-start | bytes 196616 | tf_op jit(solution)/shard_map/ppermute | solution.py:354
  93.6 1.9 %collective-permute-done.20.refs_6_ = f32[8,16,128]{2,1,0:T(8,128)S(1)} collective-permute-done((f32[8,16,128]{2,1,0:T(8,128)S(1)}, f32[8,16,128]{2,1,0:T(8,128)S(1)}, u32[]{:S(2)}, u32[]{:S(2)}) %collective-permute-start.20) | collective-permute-done | bytes 65568 | tf_op jit(solution)/shard_map/ppermute | solution.py:354
  95.6 2.6 %collective-permute-done.19.refs_5_ = f32[8,32,128]{2,1,0:T(8,128)S(1)} collective-permute-done((f32[8,32,128]{2,1,0:T(8,128)S(1)}, f32[8,32,128]{2,1,0:T(8,128)S(1)}, u32[]{:S(2)}, u32[]{:S(2)}) %collective-permute-start.19) | collective-permute-done | bytes 131104 | tf_op jit(solution)/shard_map/ppermute | solution.py:354
  (42 shorter events, 7.5 us)
Async XLA Ops:
  0.0 10.5 %copy-start.2 = (s32[1,32,4]{1,2,0:T(4,128)S(1)}, s32[1,32,4]{1,2,0:T(4,128)}, u32[]{:S(2)}) copy-start(s32[1,32,4]{1,2,0:T(4,128)} %param.13) | copy-start | bytes 1540
  3.2 56.6 %all-to-all-start = ((f32[32,128,128]{2,1,0:T(8,128)}), f32[32,128,128]{2,1,0:T(8,128)S(1)}, u32[]{:S(2)}, u32[]{:S(2)}) async-start(f32[32,128,128]{2,1,0:T(8,128)} %bitcast.27), calls=%async_computation | async-start | bytes 4194304 | tf_op jit(solution)/shard_map/all_to_all | solution.py:374
  10.5 4.5 %collective-permute-start.3 = (s32[1,4,32]{2,1,0:T(4,128)S(1)}, s32[1,4,32]{2,1,0:T(4,128)S(1)}, u32[]{:S(2)}, u32[]{:S(2)}) collective-permute-start(s32[1,4,32]{2,1,0:T(4,128)S(1)} %bitcast.29), channel_id=1, source_target_pairs={{0,1},{1,0},{2,3},{3,2},{4,5},{5,4},{6,7},{7,6},{8,9},{9,8},{10,11... | collective-permute-start | bytes 1544 | tf_op jit(solution)/shard_map/ppermute | solution.py:354
  10.8 32.5 %collective-permute-start.2 = (s32[1,4,32]{2,1,0:T(4,128)S(1)}, s32[1,4,32]{2,1,0:T(4,128)S(1)}, u32[]{:S(2)}, u32[]{:S(2)}) collective-permute-start(s32[1,4,32]{2,1,0:T(4,128)S(1)} %bitcast.30), channel_id=1, source_target_pairs={{0,6},{1,7},{2,4},{3,5},{4,2},{5,3},{6,0},{7,1},{8,14},{9,15},{10,... | collective-permute-start | bytes 1544 | tf_op jit(solution)/shard_map/ppermute | solution.py:354
  13.4 31.2 %collective-permute-start.1 = (s32[1,4,32]{2,1,0:T(4,128)S(1)}, s32[1,4,32]{2,1,0:T(4,128)S(1)}, u32[]{:S(2)}, u32[]{:S(2)}) collective-permute-start(s32[1,4,32]{2,1,0:T(4,128)S(1)} %bitcast.31), channel_id=1, source_target_pairs={{0,4},{1,5},{2,6},{3,7},{4,0},{5,1},{6,2},{7,3},{8,12},{9,13},{10,... | collective-permute-start | bytes 1544 | tf_op jit(solution)/shard_map/ppermute | solution.py:354
  14.0 30.7 %collective-permute-start = (s32[1,4,32]{2,1,0:T(4,128)S(1)}, s32[1,4,32]{2,1,0:T(4,128)S(1)}, u32[]{:S(2)}, u32[]{:S(2)}) collective-permute-start(s32[1,4,32]{2,1,0:T(4,128)S(1)} %bitcast.32), channel_id=1, source_target_pairs={{0,2},{1,3},{2,0},{3,1},{4,6},{5,7},{6,4},{7,5},{8,10},{9,11},{10,... | collective-permute-start | bytes 1544 | tf_op jit(solution)/shard_map/ppermute | solution.py:354
  15.0 34.3 %collective-permute-start.6 = (s32[2,4,32]{2,1,0:T(4,128)S(1)}, s32[2,4,32]{2,1,0:T(4,128)S(1)}, u32[]{:S(2)}, u32[]{:S(2)}) collective-permute-start(s32[2,4,32]{2,1,0:T(4,128)S(1)} %pad_add_fusion.2), channel_id=1, source_target_pairs={{0,24},{1,25},{2,26},{3,27},{4,28},{5,29},{6,30},{7,31},{8,16},{9,... | collective-permute-start | bytes 3080 | tf_op jit(solution)/shard_map/ppermute | solution.py:354
  18.6 41.2 %collective-permute-start.5 = (s32[2,4,32]{2,1,0:T(4,128)S(1)}, s32[2,4,32]{2,1,0:T(4,128)S(1)}, u32[]{:S(2)}, u32[]{:S(2)}) collective-permute-start(s32[2,4,32]{2,1,0:T(4,128)S(1)} %pad_add_fusion.2), channel_id=1, source_target_pairs={{0,16},{1,17},{2,18},{3,19},{4,20},{5,21},{6,22},{7,23},{8,24},{9,... | collective-permute-start | bytes 3080 | tf_op jit(solution)/shard_map/ppermute | solution.py:354
  21.3 0.7 copy-start
  43.3 16.5 %collective-permute-start.4 = (s32[2,4,32]{2,1,0:T(4,128)S(1)}, s32[2,4,32]{2,1,0:T(4,128)S(1)}, u32[]{:S(2)}, u32[]{:S(2)}) collective-permute-start(s32[2,4,32]{2,1,0:T(4,128)S(1)} %pad_add_fusion.2), channel_id=1, source_target_pairs={{0,8},{1,9},{2,10},{3,11},{4,12},{5,13},{6,14},{7,15},{8,0},{9,1},... | collective-permute-start | bytes 3080 | tf_op jit(solution)/shard_map/ppermute | solution.py:354
  64.3 9.0 %collective-permute-start.7 = (f32[2,4,64,128]{3,2,1,0:T(8,128)S(1)}, f32[2,4,64,128]{3,2,1,0:T(8,128)S(1)}, u32[]{:S(2)}, u32[]{:S(2)}) collective-permute-start(f32[2,4,64,128]{3,2,1,0:T(8,128)S(1)} %get-tuple-element.46), channel_id=1, source_target_pairs={{0,2},{1,3},{2,0},{3,1},{4,6},{5,7},{6,4},{7,5},{8,10},{9,11},{10,... | collective-permute-start | bytes 786440 | tf_op jit(solution)/shard_map/ppermute | solution.py:354
  65.7 13.9 %collective-permute-start.8 = (f32[2,4,64,128]{3,2,1,0:T(8,128)S(1)}, f32[2,4,64,128]{3,2,1,0:T(8,128)S(1)}, u32[]{:S(2)}, u32[]{:S(2)}) collective-permute-start(f32[2,4,64,128]{3,2,1,0:T(8,128)S(1)} %get-tuple-element.47), channel_id=1, source_target_pairs={{0,4},{1,5},{2,6},{3,7},{4,0},{5,1},{6,2},{7,3},{8,12},{9,13},{10,... | collective-permute-start | bytes 786440 | tf_op jit(solution)/shard_map/ppermute | solution.py:354
  68.0 11.6 %collective-permute-start.9 = (f32[2,4,64,128]{3,2,1,0:T(8,128)S(1)}, f32[2,4,64,128]{3,2,1,0:T(8,128)S(1)}, u32[]{:S(2)}, u32[]{:S(2)}) collective-permute-start(f32[2,4,64,128]{3,2,1,0:T(8,128)S(1)} %get-tuple-element.48), channel_id=1, source_target_pairs={{0,6},{1,7},{2,4},{3,5},{4,2},{5,3},{6,0},{7,1},{8,14},{9,15},{10,... | collective-permute-start | bytes 786440 | tf_op jit(solution)/shard_map/ppermute | solution.py:354
  68.8 12.5 %collective-permute-start.12 = (f32[2,4,4,16,128]{4,3,2,1,0:T(8,128)S(1)}, f32[2,4,4,16,128]{4,3,2,1,0:T(8,128)S(1)}, u32[]{:S(2)}, u32[]{:S(2)}) collective-permute-start(f32[2,4,4,16,128]{4,3,2,1,0:T(8,128)S(1)} %get-tuple-element.54), channel_id=1, source_target_pairs={{0,8},{1,9},{2,10},{3,11},{4,12},{5,13},{6,14},{7,15},{8,16},{9,17... | collective-permute-start | bytes 786440 | tf_op jit(solution)/shard_map/ppermute | solution.py:354
  69.4 12.8 %collective-permute-start.13 = (f32[2,4,4,16,128]{4,3,2,1,0:T(8,128)S(1)}, f32[2,4,4,16,128]{4,3,2,1,0:T(8,128)S(1)}, u32[]{:S(2)}, u32[]{:S(2)}) collective-permute-start(f32[2,4,4,16,128]{4,3,2,1,0:T(8,128)S(1)} %get-tuple-element.55), channel_id=1, source_target_pairs={{0,24},{1,25},{2,26},{3,27},{4,28},{5,29},{6,30},{7,31},{8,0},{9,1... | collective-permute-start | bytes 786440 | tf_op jit(solution)/shard_map/ppermute | solution.py:354
  80.7 1.6 %collective-permute-start.10 = (f32[8,64,128]{2,1,0:T(8,128)S(1)}, f32[8,64,128]{2,1,0:T(8,128)S(1)}, u32[]{:S(2)}, u32[]{:S(2)}) collective-permute-start(f32[8,64,128]{2,1,0:T(8,128)S(1)} %get-tuple-element.50), channel_id=1, source_target_pairs={{0,1},{1,0},{2,3},{3,2},{4,5},{5,4},{6,7},{7,6},{8,9},{9,8},{10,11... | collective-permute-start | bytes 786440 | tf_op jit(solution)/shard_map/ppermute | solution.py:354
  80.8 1.9 %collective-permute-start.11 = (f32[4,4,32,128]{3,2,1,0:T(8,128)S(1)}, f32[4,4,32,128]{3,2,1,0:T(8,128)S(1)}, u32[]{:S(2)}, u32[]{:S(2)}) collective-permute-start(f32[4,4,32,128]{3,2,1,0:T(8,128)S(1)} %get-tuple-element.53), channel_id=1, source_target_pairs={{0,1},{1,0},{2,3},{3,2},{4,5},{5,4},{6,7},{7,6},{8,9},{9,8},{10,11... | collective-permute-start | bytes 786440 | tf_op jit(solution)/shard_map/ppermute | solution.py:354
  82.2 1.6 %collective-permute-start.14 = (f32[2,4,4,16,128]{4,3,2,1,0:T(8,128)S(1)}, f32[2,4,4,16,128]{4,3,2,1,0:T(8,128)S(1)}, u32[]{:S(2)}, u32[]{:S(2)}) collective-permute-start(f32[2,4,4,16,128]{4,3,2,1,0:T(8,128)S(1)} %pad_maximum_fusion), channel_id=1, source_target_pairs={{0,1},{1,0},{2,3},{3,2},{4,5},{5,4},{6,7},{7,6},{8,9},{9,8},{10,11... | collective-permute-start | bytes 786440 | tf_op jit(solution)/shard_map/ppermute | solution.py:354
  84.8 6.2 %collective-permute-start.18 = (f32[8,16,128]{2,1,0:T(8,128)S(1)}, f32[8,16,128]{2,1,0:T(8,128)S(1)}, u32[]{:S(2)}, u32[]{:S(2)}) collective-permute-start(f32[8,16,128]{2,1,0:T(8,128)S(1)} %get-tuple-element.64), channel_id=1, source_target_pairs={{0,8},{1,9},{2,10},{3,11},{4,12},{5,13},{6,14},{7,15},{8,16},{9,17... | collective-permute-start | bytes 196616 | tf_op jit(solution)/shard_map/ppermute | solution.py:354
  85.6 10.0 %collective-permute-start.15 = (f32[8,32,128]{2,1,0:T(8,128)S(1)}, f32[8,32,128]{2,1,0:T(8,128)S(1)}, u32[]{:S(2)}, u32[]{:S(2)}) collective-permute-start(f32[8,32,128]{2,1,0:T(8,128)S(1)} %get-tuple-element.61), channel_id=1, source_target_pairs={{0,2},{1,3},{2,0},{3,1},{4,6},{5,7},{6,4},{7,5},{8,10},{9,11},{10,... | collective-permute-start | bytes 393224 | tf_op jit(solution)/shard_map/ppermute | solution.py:354
  86.4 9.1 %collective-permute-start.16 = (f32[8,32,128]{2,1,0:T(8,128)S(1)}, f32[8,32,128]{2,1,0:T(8,128)S(1)}, u32[]{:S(2)}, u32[]{:S(2)}) collective-permute-start(f32[8,32,128]{2,1,0:T(8,128)S(1)} %get-tuple-element.62), channel_id=1, source_target_pairs={{0,4},{1,5},{2,6},{3,7},{4,0},{5,1},{6,2},{7,3},{8,12},{9,13},{10,... | collective-permute-start | bytes 393224 | tf_op jit(solution)/shard_map/ppermute | solution.py:354
  88.2 7.4 %collective-permute-start.17 = (f32[8,32,128]{2,1,0:T(8,128)S(1)}, f32[8,32,128]{2,1,0:T(8,128)S(1)}, u32[]{:S(2)}, u32[]{:S(2)}) collective-permute-start(f32[8,32,128]{2,1,0:T(8,128)S(1)} %get-tuple-element.63), channel_id=1, source_target_pairs={{0,6},{1,7},{2,4},{3,5},{4,2},{5,3},{6,0},{7,1},{8,14},{9,15},{10,... | collective-permute-start | bytes 393224 | tf_op jit(solution)/shard_map/ppermute | solution.py:354
  89.1 9.1 %collective-permute-start.19 = (f32[8,32,128]{2,1,0:T(8,128)S(1)}, f32[8,32,128]{2,1,0:T(8,128)S(1)}, u32[]{:S(2)}, u32[]{:S(2)}) collective-permute-start(f32[8,32,128]{2,1,0:T(8,128)S(1)} %slice_add_fusion), channel_id=1, source_target_pairs={{0,16},{1,17},{2,18},{3,19},{4,20},{5,21},{6,22},{7,23},{8,24},{9,... | collective-permute-start | bytes 393224 | tf_op jit(solution)/shard_map/ppermute | solution.py:354
  90.9 4.6 %collective-permute-start.20 = (f32[8,16,128]{2,1,0:T(8,128)S(1)}, f32[8,16,128]{2,1,0:T(8,128)S(1)}, u32[]{:S(2)}, u32[]{:S(2)}) collective-permute-start(f32[8,16,128]{2,1,0:T(8,128)S(1)} %get-tuple-element.66), channel_id=1, source_target_pairs={{0,24},{1,25},{2,26},{3,27},{4,28},{5,29},{6,30},{7,31},{8,0},{9,1... | collective-permute-start | bytes 196616 | tf_op jit(solution)/shard_map/ppermute | solution.py:354
  (1 other events, 0.7 us)

commit v2 on v1

--- a/solution.py
+++ b/solution.py
@@ -318,7 +318,7 @@
 
 
 def final_kernel(*refs):
-    own, far, out_ref, total = refs[:PLACES], refs[PLACES:-2], refs[-2], refs[-1]
+    far, own, out_ref, total = refs[: -2 - PLACES], refs[-2 - PLACES : -2], refs[-2], refs[-1]
     for t in range(TO):
         total[t * HALF : (t + 1) * HALF] = own[0][t] + own[1][t] + own[2][t] + own[3][t]
         for part in far:
@@ -463,9 +463,9 @@
     mine, other = combine(combine_far_kernel, far_shape, far_table, far_slots)
     got = other_core(other)
     summed = [mine[:, first : first + count] + got[:, first : first + count] for first, count in steps.values()]
-    summed, own_tiles = lax.optimization_barrier((summed, own_tiles))
-    far_parts = over_groups(zip(steps, summed))
-    parts = in_group(own_tiles) + far_parts
+    order = sorted(zip(steps, summed), key=lambda item: abs(item[0] - groups // 2) * 2 - (item[0] > groups // 2))
+    far_parts = over_groups(order)
+    parts = far_parts + in_group(own_tiles)
 
     return pl.pallas_call(
         final_kernel,

time: 99.3 us -> 96.6 us (0.973)
  starting transfers between devices: 33.9 us -> 30.9 us
  Pallas kernels: 31.8 us -> 33.8 us
  waiting for transfers between devices: 28.9 us -> 27.3 us
    ppermute x21, starting transfers between devices: 26.6 us -> 23.6 us  [across(): return lax.ppermute(value, 'elem', [(i, partner(i)) for i in range(n)])]
    ppermute x21, waiting for transfers between devices: 28.9 us -> 27.3 us  [across(): return lax.ppermute(value, 'elem', [(i, partner(i)) for i in range(n)])]
    pallas_call x1, Pallas kernels: 21.3 us -> 22.4 us  [body(): pl.pallas_call(functools.partial(near_kernel, n), grid=(rows,), out_shape...]
  transfers between devices with their start and end apart: 22 -> 22, of which waited for: 9 -> 8; matrix products, arithmetic and copies ran while one was open for 3% -> 3% of each run, Pallas kernels for 23% -> 25%
where the time goes in v2:
time: 96.6 us; the launch traced here: 96.3 us
  Pallas kernels  33.8 us (35%)
  starting transfers between devices  30.9 us (32%)
  waiting for transfers between devices  27.3 us (28%)
  local copies, waits for them, and re-layouts  3.4 us (4%)
    ppermute x21, waiting for transfers between devices, across(): return lax.ppermute(value, 'elem', [(i, partner(i)) for i in range(n)])  27.3 us
    ppermute x21, starting transfers between devices, across(): return lax.ppermute(value, 'elem', [(i, partner(i)) for i in range(n)])  23.6 us
    pallas_call x1, Pallas kernels, body(): pl.pallas_call(functools.partial(near_kernel, n), grid=(rows,), out_shape...  22.4 us
    all_to_all x1, starting transfers between devices, body(): lax.all_to_all(send.reshape(n, serve_count * B, LANES), 'elem', split_axi...  7.3 us
    pallas_call x1, Pallas kernels, body(): pl.pallas_call(functools.partial(far_kernel, n, cap), out_shape=slot_shap...  5.39 us
    pallas_call x1, Pallas kernels, body(): pl.pallas_call(functools.partial(prep_kernel, n), out_shape=(shape((rows,...  3.16 us
    unnamed x7, local copies, waits for them, and re-layouts  3.01 us
    pallas_call x2, Pallas kernels, combine(): pl.pallas_call(functools.partial(kernel, n), out_shape=out_shape, in_spec...  2.06 us
  transfers between devices with their start and end apart: 22, of which 8 were waited for; matrix products, arithmetic and copies ran while one was open for 3% of the time, Pallas kernels for 25%

profile of v2, /device:TPU:0, one launch (start us, length us, event | category | flops | bytes accessed | tf_op | source)
XLA Modules:
  0.0 96.3 jit_solution(12862355963943349398)
XLA Ops:
  0.0 3.2 %prep.1 = (f32[32,64,128]{2,1,0:T(8,128)S(1)}, f32[32,2,64,128]{3,2,1,0:T(8,128)}) custom-call(s32[1]{0:T(128)} %bitcast.me_ref, s32[2,31]{1,0:T(2,128)} %bitcast.35, f32[32,64,128]{2,1,0:T(8,128)} %bitcast.28), custom_call_target="tpu_custom_call" | custom-call | tf_op jit(solution)/shard_map/prep/pallas_call | solution.py:357
  3.2 7.3 %all-to-all-start = ((f32[32,128,128]{2,1,0:T(8,128)}), f32[32,128,128]{2,1,0:T(8,128)S(1)}, u32[]{:S(2)}, u32[]{:S(2)}) async-start(f32[32,128,128]{2,1,0:T(8,128)} %bitcast.27), calls=%async_computation | async-start | bytes 4194304 | tf_op jit(solution)/shard_map/all_to_all | solution.py:374
  10.8 2.6 %collective-permute-start.2 = (s32[1,4,32]{2,1,0:T(4,128)S(1)}, s32[1,4,32]{2,1,0:T(4,128)S(1)}, u32[]{:S(2)}, u32[]{:S(2)}) collective-permute-start(s32[1,4,32]{2,1,0:T(4,128)S(1)} %bitcast.30), channel_id=1, source_target_pairs={{0,6},{1,7},{2,4},{3,5},{4,2},{5,3},{6,0},{7,1},{8,14},{9,15},{10,... | collective-permute-start | bytes 1544 | tf_op jit(solution)/shard_map/ppermute | solution.py:354
  15.0 3.6 %collective-permute-start.6 = (s32[2,4,32]{2,1,0:T(4,128)S(1)}, s32[2,4,32]{2,1,0:T(4,128)S(1)}, u32[]{:S(2)}, u32[]{:S(2)}) collective-permute-start(s32[2,4,32]{2,1,0:T(4,128)S(1)} %pad_add_fusion.2), channel_id=1, source_target_pairs={{0,24},{1,25},{2,26},{3,27},{4,28},{5,29},{6,30},{7,31},{8,16},{9,... | collective-permute-start | bytes 3080 | tf_op jit(solution)/shard_map/ppermute | solution.py:354
  18.6 2.7 %copy.12 = f32[28,8,32,128]{3,2,1,0:T(8,128)S(1)} copy(f32[28,8,32,128]{3,1,2,0:T(8,128)} %bitcast.26) | data formatting | bytes 7340032
  22.0 22.4 %near.1 = (bf16[256,128,128]{2,1,0:T(8,128)(2,1)}, f32[128,32,128]{2,1,0:T(8,128)}, s32[2304]{0:T(1024)S(1)}) custom-call(s32[1]{0:T(128)S(6)} %copy.13.count_row, s32[7,32]{1,0:T(8,128)S(1)} %bitcast.24, s32[32,28]{1,0:T(8,128)S(1)} %copy-done, s32[1]{0:T(128)} %bitcast.me_ref, f32[32,64,128]{2,1,0:T(8,128)S(1)} %get-tuple-element.32.own_ref, ...), custom_call_target="tpu_custom_call" | custom-call | flops 3758096384 | bytes 16777216 | tf_op jit(solution)/shard_map/near/pallas_call | solution.py:393
  44.5 4.8 %collective-permute-done.6 = s32[2,4,32]{2,1,0:T(4,128)S(1)} collective-permute-done((s32[2,4,32]{2,1,0:T(4,128)S(1)}, s32[2,4,32]{2,1,0:T(4,128)S(1)}, u32[]{:S(2)}, u32[]{:S(2)}) %collective-permute-start.6) | collective-permute-done | bytes 1056 | tf_op jit(solution)/shard_map/ppermute | solution.py:354
  49.3 10.4 %collective-permute-done.5 = s32[2,4,32]{2,1,0:T(4,128)S(1)} collective-permute-done((s32[2,4,32]{2,1,0:T(4,128)S(1)}, s32[2,4,32]{2,1,0:T(4,128)S(1)}, u32[]{:S(2)}, u32[]{:S(2)}) %collective-permute-start.5) | collective-permute-done | bytes 1056 | tf_op jit(solution)/shard_map/ppermute | solution.py:354
  59.8 5.4 %far.1 = (f32[2,4,64,128]{3,2,1,0:T(8,128)S(1)}, f32[2,4,64,128]{3,2,1,0:T(8,128)S(1)}, f32[2,4,64,128]{3,2,1,0:T(8,128)S(1)}, f32[2,4,64,128]{3,2,1,0:T(8,128)S...) custom-call(s32[1]{0:T(128)} %bitcast.me_ref, ...), custom_call_target="tpu_custom_call" | custom-call | flops 1879048192 | bytes 16777216 | tf_op jit(solution)/shard_map/far/pallas_call | solution.py:420
  65.2 1.5 %collective-permute-start.7 = (f32[2,4,64,128]{3,2,1,0:T(8,128)S(1)}, f32[2,4,64,128]{3,2,1,0:T(8,128)S(1)}, u32[]{:S(2)}, u32[]{:S(2)}) collective-permute-start(f32[2,4,64,128]{3,2,1,0:T(8,128)S(1)} %get-tuple-element.39), channel_id=1, source_target_pairs={{0,2},{1,3},{2,0},{3,1},{4,6},{5,7},{6,4},{7,5},{8,10},{9,11},{10,... | collective-permute-start | bytes 786440 | tf_op jit(solution)/shard_map/ppermute | solution.py:354
  66.6 2.2 %collective-permute-start.8 = (f32[2,4,64,128]{3,2,1,0:T(8,128)S(1)}, f32[2,4,64,128]{3,2,1,0:T(8,128)S(1)}, u32[]{:S(2)}, u32[]{:S(2)}) collective-permute-start(f32[2,4,64,128]{3,2,1,0:T(8,128)S(1)} %get-tuple-element.40), channel_id=1, source_target_pairs={{0,4},{1,5},{2,6},{3,7},{4,0},{5,1},{6,2},{7,3},{8,12},{9,13},{10,... | collective-permute-start | bytes 786440 | tf_op jit(solution)/shard_map/ppermute | solution.py:354
  69.4 3.3 %collective-permute-start.16 = (f32[2,4,4,16,128]{4,3,2,1,0:T(8,128)S(1)}, f32[2,4,4,16,128]{4,3,2,1,0:T(8,128)S(1)}, u32[]{:S(2)}, u32[]{:S(2)}) collective-permute-start(f32[2,4,4,16,128]{4,3,2,1,0:T(8,128)S(1)} %get-tuple-element.48), channel_id=1, source_target_pairs={{0,24},{1,25},{2,26},{3,27},{4,28},{5,29},{6,30},{7,31},{8,0},{9,1... | collective-permute-start | bytes 786440 | tf_op jit(solution)/shard_map/ppermute | solution.py:354
  72.7 1.8 %collective-permute-done.7.refs_1_ = f32[2,4,64,128]{3,2,1,0:T(8,128)S(1)} collective-permute-done((f32[2,4,64,128]{3,2,1,0:T(8,128)S(1)}, f32[2,4,64,128]{3,2,1,0:T(8,128)S(1)}, u32[]{:S(2)}, u32[]{:S(2)}) %collective-permute-start.7) | collective-permute-done | bytes 262176 | tf_op jit(solution)/shard_map/ppermute | solution.py:354
  74.4 5.3 %collective-permute-done.8.refs_2_ = f32[2,4,64,128]{3,2,1,0:T(8,128)S(1)} collective-permute-done((f32[2,4,64,128]{3,2,1,0:T(8,128)S(1)}, f32[2,4,64,128]{3,2,1,0:T(8,128)S(1)}, u32[]{:S(2)}, u32[]{:S(2)}) %collective-permute-start.8) | collective-permute-done | bytes 262176 | tf_op jit(solution)/shard_map/ppermute | solution.py:354
  79.8 1.1 %combine_far_kernel.1 = (f32[8,64,128]{2,1,0:T(8,128)S(1)}, f32[8,64,128]{2,1,0:T(8,128)S(1)}) custom-call(s32[1]{0:T(128)} %bitcast.me_ref, s32[32,32]{1,0:T(8,128)S(1)} %bitcast.22, f32[2,4,64,128]{3,2,1,0:T(8,128)S(1)} %get-tuple-element.38.refs_0_, f32[2,4,64,128]{3,2,1,0:T(8,128)S(1)} %collective-permute-done.7.refs_1_, ...), custom_call_target="tpu_custom_call" | custom-call | tf_op jit(solution)/shard_map/combine_far_kernel/pallas_call | solution.py:438
  81.5 0.6 collective-permute-done.16.refs_1_
  82.5 1.3 %collective-permute-start.13 = (f32[8,16,128]{2,1,0:T(8,128)S(1)}, f32[8,16,128]{2,1,0:T(8,128)S(1)}, u32[]{:S(2)}, u32[]{:S(2)}) collective-permute-start(f32[8,16,128]{2,1,0:T(8,128)S(1)} %get-tuple-element.53), channel_id=1, source_target_pairs={{0,8},{1,9},{2,10},{3,11},{4,12},{5,13},{6,14},{7,15},{8,16},{9,17... | collective-permute-start | bytes 196616 | tf_op jit(solution)/shard_map/ppermute | solution.py:354
  83.8 1.7 %collective-permute-start.11 = (f32[8,32,128]{2,1,0:T(8,128)S(1)}, f32[8,32,128]{2,1,0:T(8,128)S(1)}, u32[]{:S(2)}, u32[]{:S(2)}) collective-permute-start(f32[8,32,128]{2,1,0:T(8,128)S(1)} %slice_add_fusion), channel_id=1, source_target_pairs={{0,16},{1,17},{2,18},{3,19},{4,20},{5,21},{6,22},{7,23},{8,24},{9,... | collective-permute-start | bytes 393224 | tf_op jit(solution)/shard_map/ppermute | solution.py:354
  85.5 0.9 combine_own_kernel.1
  86.5 1.2 %collective-permute-start.18 = (f32[8,32,128]{2,1,0:T(8,128)S(1)}, f32[8,32,128]{2,1,0:T(8,128)S(1)}, u32[]{:S(2)}, u32[]{:S(2)}) collective-permute-start(f32[8,32,128]{2,1,0:T(8,128)S(1)} %get-tuple-element.50), channel_id=1, source_target_pairs={{0,2},{1,3},{2,0},{3,1},{4,6},{5,7},{6,4},{7,5},{8,10},{9,11},{10,... | collective-permute-start | bytes 393224 | tf_op jit(solution)/shard_map/ppermute | solution.py:354
  88.3 1.7 %collective-permute-start.20 = (f32[8,32,128]{2,1,0:T(8,128)S(1)}, f32[8,32,128]{2,1,0:T(8,128)S(1)}, u32[]{:S(2)}, u32[]{:S(2)}) collective-permute-start(f32[8,32,128]{2,1,0:T(8,128)S(1)} %get-tuple-element.52), channel_id=1, source_target_pairs={{0,6},{1,7},{2,4},{3,5},{4,2},{5,3},{6,0},{7,1},{8,14},{9,15},{10,... | collective-permute-start | bytes 393224 | tf_op jit(solution)/shard_map/ppermute | solution.py:354
  90.0 1.4 %collective-permute-start.12 = (f32[8,16,128]{2,1,0:T(8,128)S(1)}, f32[8,16,128]{2,1,0:T(8,128)S(1)}, u32[]{:S(2)}, u32[]{:S(2)}) collective-permute-start(f32[8,16,128]{2,1,0:T(8,128)S(1)} %get-tuple-element.54), channel_id=1, source_target_pairs={{0,24},{1,25},{2,26},{3,27},{4,28},{5,29},{6,30},{7,31},{8,0},{9,1... | collective-permute-start | bytes 196616 | tf_op jit(solution)/shard_map/ppermute | solution.py:354
  91.4 4.0 %collective-permute-done.12.refs_1_ = f32[8,16,128]{2,1,0:T(8,128)S(1)} collective-permute-done((f32[8,16,128]{2,1,0:T(8,128)S(1)}, f32[8,16,128]{2,1,0:T(8,128)S(1)}, u32[]{:S(2)}, u32[]{:S(2)}) %collective-permute-start.12) | collective-permute-done | bytes 65568 | tf_op jit(solution)/shard_map/ppermute | solution.py:354
  95.6 0.8 final.1
  (42 shorter events, 4.2 us)
Async XLA Ops:
  0.0 10.5 %copy-start.2 = (s32[1,32,4]{1,2,0:T(4,128)S(1)}, s32[1,32,4]{1,2,0:T(4,128)}, u32[]{:S(2)}) copy-start(s32[1,32,4]{1,2,0:T(4,128)} %param.13) | copy-start | bytes 1540
  3.2 56.6 %all-to-all-start = ((f32[32,128,128]{2,1,0:T(8,128)}), f32[32,128,128]{2,1,0:T(8,128)S(1)}, u32[]{:S(2)}, u32[]{:S(2)}) async-start(f32[32,128,128]{2,1,0:T(8,128)} %bitcast.27), calls=%async_computation | async-start | bytes 4194304 | tf_op jit(solution)/shard_map/all_to_all | solution.py:374
  10.5 4.5 %collective-permute-start.3 = (s32[1,4,32]{2,1,0:T(4,128)S(1)}, s32[1,4,32]{2,1,0:T(4,128)S(1)}, u32[]{:S(2)}, u32[]{:S(2)}) collective-permute-start(s32[1,4,32]{2,1,0:T(4,128)S(1)} %bitcast.29), channel_id=1, source_target_pairs={{0,1},{1,0},{2,3},{3,2},{4,5},{5,4},{6,7},{7,6},{8,9},{9,8},{10,11... | collective-permute-start | bytes 1544 | tf_op jit(solution)/shard_map/ppermute | solution.py:354
  10.8 33.6 %collective-permute-start.2 = (s32[1,4,32]{2,1,0:T(4,128)S(1)}, s32[1,4,32]{2,1,0:T(4,128)S(1)}, u32[]{:S(2)}, u32[]{:S(2)}) collective-permute-start(s32[1,4,32]{2,1,0:T(4,128)S(1)} %bitcast.30), channel_id=1, source_target_pairs={{0,6},{1,7},{2,4},{3,5},{4,2},{5,3},{6,0},{7,1},{8,14},{9,15},{10,... | collective-permute-start | bytes 1544 | tf_op jit(solution)/shard_map/ppermute | solution.py:354
  13.4 31.1 %collective-permute-start.1 = (s32[1,4,32]{2,1,0:T(4,128)S(1)}, s32[1,4,32]{2,1,0:T(4,128)S(1)}, u32[]{:S(2)}, u32[]{:S(2)}) collective-permute-start(s32[1,4,32]{2,1,0:T(4,128)S(1)} %bitcast.31), channel_id=1, source_target_pairs={{0,4},{1,5},{2,6},{3,7},{4,0},{5,1},{6,2},{7,3},{8,12},{9,13},{10,... | collective-permute-start | bytes 1544 | tf_op jit(solution)/shard_map/ppermute | solution.py:354
  14.0 30.6 %collective-permute-start = (s32[1,4,32]{2,1,0:T(4,128)S(1)}, s32[1,4,32]{2,1,0:T(4,128)S(1)}, u32[]{:S(2)}, u32[]{:S(2)}) collective-permute-start(s32[1,4,32]{2,1,0:T(4,128)S(1)} %bitcast.32), channel_id=1, source_target_pairs={{0,2},{1,3},{2,0},{3,1},{4,6},{5,7},{6,4},{7,5},{8,10},{9,11},{10,... | collective-permute-start | bytes 1544 | tf_op jit(solution)/shard_map/ppermute | solution.py:354
  15.0 34.3 %collective-permute-start.6 = (s32[2,4,32]{2,1,0:T(4,128)S(1)}, s32[2,4,32]{2,1,0:T(4,128)S(1)}, u32[]{:S(2)}, u32[]{:S(2)}) collective-permute-start(s32[2,4,32]{2,1,0:T(4,128)S(1)} %pad_add_fusion.2), channel_id=1, source_target_pairs={{0,24},{1,25},{2,26},{3,27},{4,28},{5,29},{6,30},{7,31},{8,16},{9,... | collective-permute-start | bytes 3080 | tf_op jit(solution)/shard_map/ppermute | solution.py:354
  18.6 41.2 %collective-permute-start.5 = (s32[2,4,32]{2,1,0:T(4,128)S(1)}, s32[2,4,32]{2,1,0:T(4,128)S(1)}, u32[]{:S(2)}, u32[]{:S(2)}) collective-permute-start(s32[2,4,32]{2,1,0:T(4,128)S(1)} %pad_add_fusion.2), channel_id=1, source_target_pairs={{0,16},{1,17},{2,18},{3,19},{4,20},{5,21},{6,22},{7,23},{8,24},{9,... | collective-permute-start | bytes 3080 | tf_op jit(solution)/shard_map/ppermute | solution.py:354
  21.3 0.7 copy-start
  44.4 15.3 %collective-permute-start.4 = (s32[2,4,32]{2,1,0:T(4,128)S(1)}, s32[2,4,32]{2,1,0:T(4,128)S(1)}, u32[]{:S(2)}, u32[]{:S(2)}) collective-permute-start(s32[2,4,32]{2,1,0:T(4,128)S(1)} %pad_add_fusion.2), channel_id=1, source_target_pairs={{0,8},{1,9},{2,10},{3,11},{4,12},{5,13},{6,14},{7,15},{8,0},{9,1},... | collective-permute-start | bytes 3080 | tf_op jit(solution)/shard_map/ppermute | solution.py:354
  65.2 9.3 %collective-permute-start.7 = (f32[2,4,64,128]{3,2,1,0:T(8,128)S(1)}, f32[2,4,64,128]{3,2,1,0:T(8,128)S(1)}, u32[]{:S(2)}, u32[]{:S(2)}) collective-permute-start(f32[2,4,64,128]{3,2,1,0:T(8,128)S(1)} %get-tuple-element.39), channel_id=1, source_target_pairs={{0,2},{1,3},{2,0},{3,1},{4,6},{5,7},{6,4},{7,5},{8,10},{9,11},{10,... | collective-permute-start | bytes 786440 | tf_op jit(solution)/shard_map/ppermute | solution.py:354
  66.6 13.1 %collective-permute-start.8 = (f32[2,4,64,128]{3,2,1,0:T(8,128)S(1)}, f32[2,4,64,128]{3,2,1,0:T(8,128)S(1)}, u32[]{:S(2)}, u32[]{:S(2)}) collective-permute-start(f32[2,4,64,128]{3,2,1,0:T(8,128)S(1)} %get-tuple-element.40), channel_id=1, source_target_pairs={{0,4},{1,5},{2,6},{3,7},{4,0},{5,1},{6,2},{7,3},{8,12},{9,13},{10,... | collective-permute-start | bytes 786440 | tf_op jit(solution)/shard_map/ppermute | solution.py:354
  68.9 10.9 %collective-permute-start.9 = (f32[2,4,64,128]{3,2,1,0:T(8,128)S(1)}, f32[2,4,64,128]{3,2,1,0:T(8,128)S(1)}, u32[]{:S(2)}, u32[]{:S(2)}) collective-permute-start(f32[2,4,64,128]{3,2,1,0:T(8,128)S(1)} %get-tuple-element.41), channel_id=1, source_target_pairs={{0,6},{1,7},{2,4},{3,5},{4,2},{5,3},{6,0},{7,1},{8,14},{9,15},{10,... | collective-permute-start | bytes 786440 | tf_op jit(solution)/shard_map/ppermute | solution.py:354
  68.9 12.6 %collective-permute-start.15 = (f32[2,4,4,16,128]{4,3,2,1,0:T(8,128)S(1)}, f32[2,4,4,16,128]{4,3,2,1,0:T(8,128)S(1)}, u32[]{:S(2)}, u32[]{:S(2)}) collective-permute-start(f32[2,4,4,16,128]{4,3,2,1,0:T(8,128)S(1)} %get-tuple-element.47), channel_id=1, source_target_pairs={{0,8},{1,9},{2,10},{3,11},{4,12},{5,13},{6,14},{7,15},{8,16},{9,17... | collective-permute-start | bytes 786440 | tf_op jit(solution)/shard_map/ppermute | solution.py:354
  69.4 12.7 %collective-permute-start.16 = (f32[2,4,4,16,128]{4,3,2,1,0:T(8,128)S(1)}, f32[2,4,4,16,128]{4,3,2,1,0:T(8,128)S(1)}, u32[]{:S(2)}, u32[]{:S(2)}) collective-permute-start(f32[2,4,4,16,128]{4,3,2,1,0:T(8,128)S(1)} %get-tuple-element.48), channel_id=1, source_target_pairs={{0,24},{1,25},{2,26},{3,27},{4,28},{5,29},{6,30},{7,31},{8,0},{9,1... | collective-permute-start | bytes 786440 | tf_op jit(solution)/shard_map/ppermute | solution.py:354
  80.9 1.6 %collective-permute-start.10 = (f32[8,64,128]{2,1,0:T(8,128)S(1)}, f32[8,64,128]{2,1,0:T(8,128)S(1)}, u32[]{:S(2)}, u32[]{:S(2)}) collective-permute-start(f32[8,64,128]{2,1,0:T(8,128)S(1)} %get-tuple-element.43), channel_id=1, source_target_pairs={{0,1},{1,0},{2,3},{3,2},{4,5},{5,4},{6,7},{7,6},{8,9},{9,8},{10,11... | collective-permute-start | bytes 786440 | tf_op jit(solution)/shard_map/ppermute | solution.py:354
  81.0 4.6 %collective-permute-start.14 = (f32[4,4,32,128]{3,2,1,0:T(8,128)S(1)}, f32[4,4,32,128]{3,2,1,0:T(8,128)S(1)}, u32[]{:S(2)}, u32[]{:S(2)}) collective-permute-start(f32[4,4,32,128]{3,2,1,0:T(8,128)S(1)} %get-tuple-element.46), channel_id=1, source_target_pairs={{0,1},{1,0},{2,3},{3,2},{4,5},{5,4},{6,7},{7,6},{8,9},{9,8},{10,11... | collective-permute-start | bytes 786440 | tf_op jit(solution)/shard_map/ppermute | solution.py:354
  82.1 3.4 %collective-permute-start.17 = (f32[2,4,4,16,128]{4,3,2,1,0:T(8,128)S(1)}, f32[2,4,4,16,128]{4,3,2,1,0:T(8,128)S(1)}, u32[]{:S(2)}, u32[]{:S(2)}) collective-permute-start(f32[2,4,4,16,128]{4,3,2,1,0:T(8,128)S(1)} %pad_maximum_fusion), channel_id=1, source_target_pairs={{0,1},{1,0},{2,3},{3,2},{4,5},{5,4},{6,7},{7,6},{8,9},{9,8},{10,11... | collective-permute-start | bytes 786440 | tf_op jit(solution)/shard_map/ppermute | solution.py:354
  82.5 7.5 %collective-permute-start.13 = (f32[8,16,128]{2,1,0:T(8,128)S(1)}, f32[8,16,128]{2,1,0:T(8,128)S(1)}, u32[]{:S(2)}, u32[]{:S(2)}) collective-permute-start(f32[8,16,128]{2,1,0:T(8,128)S(1)} %get-tuple-element.53), channel_id=1, source_target_pairs={{0,8},{1,9},{2,10},{3,11},{4,12},{5,13},{6,14},{7,15},{8,16},{9,17... | collective-permute-start | bytes 196616 | tf_op jit(solution)/shard_map/ppermute | solution.py:354
  83.8 11.6 %collective-permute-start.11 = (f32[8,32,128]{2,1,0:T(8,128)S(1)}, f32[8,32,128]{2,1,0:T(8,128)S(1)}, u32[]{:S(2)}, u32[]{:S(2)}) collective-permute-start(f32[8,32,128]{2,1,0:T(8,128)S(1)} %slice_add_fusion), channel_id=1, source_target_pairs={{0,16},{1,17},{2,18},{3,19},{4,20},{5,21},{6,22},{7,23},{8,24},{9,... | collective-permute-start | bytes 393224 | tf_op jit(solution)/shard_map/ppermute | solution.py:354
  86.5 9.0 %collective-permute-start.18 = (f32[8,32,128]{2,1,0:T(8,128)S(1)}, f32[8,32,128]{2,1,0:T(8,128)S(1)}, u32[]{:S(2)}, u32[]{:S(2)}) collective-permute-start(f32[8,32,128]{2,1,0:T(8,128)S(1)} %get-tuple-element.50), channel_id=1, source_target_pairs={{0,2},{1,3},{2,0},{3,1},{4,6},{5,7},{6,4},{7,5},{8,10},{9,11},{10,... | collective-permute-start | bytes 393224 | tf_op jit(solution)/shard_map/ppermute | solution.py:354
  87.7 7.9 %collective-permute-start.19 = (f32[8,32,128]{2,1,0:T(8,128)S(1)}, f32[8,32,128]{2,1,0:T(8,128)S(1)}, u32[]{:S(2)}, u32[]{:S(2)}) collective-permute-start(f32[8,32,128]{2,1,0:T(8,128)S(1)} %get-tuple-element.51), channel_id=1, source_target_pairs={{0,4},{1,5},{2,6},{3,7},{4,0},{5,1},{6,2},{7,3},{8,12},{9,13},{10,... | collective-permute-start | bytes 393224 | tf_op jit(solution)/shard_map/ppermute | solution.py:354
  88.3 7.3 %collective-permute-start.20 = (f32[8,32,128]{2,1,0:T(8,128)S(1)}, f32[8,32,128]{2,1,0:T(8,128)S(1)}, u32[]{:S(2)}, u32[]{:S(2)}) collective-permute-start(f32[8,32,128]{2,1,0:T(8,128)S(1)} %get-tuple-element.52), channel_id=1, source_target_pairs={{0,6},{1,7},{2,4},{3,5},{4,2},{5,3},{6,0},{7,1},{8,14},{9,15},{10,... | collective-permute-start | bytes 393224 | tf_op jit(solution)/shard_map/ppermute | solution.py:354
  90.0 5.4 %collective-permute-start.12 = (f32[8,16,128]{2,1,0:T(8,128)S(1)}, f32[8,16,128]{2,1,0:T(8,128)S(1)}, u32[]{:S(2)}, u32[]{:S(2)}) collective-permute-start(f32[8,16,128]{2,1,0:T(8,128)S(1)} %get-tuple-element.54), channel_id=1, source_target_pairs={{0,24},{1,25},{2,26},{3,27},{4,28},{5,29},{6,30},{7,31},{8,0},{9,1... | collective-permute-start | bytes 196616 | tf_op jit(solution)/shard_map/ppermute | solution.py:354
  (1 other events, 0.7 us)

commit v3 on v2

--- a/solution.py
+++ b/solution.py
@@ -16,7 +16,7 @@
 CHUNKS = 4
 REST = HALF // 2
 FETCH = 16
-DEPTH = 6
+DEPTH = 8
 UNROLL = 32
 META = 8
 MIB = 1 << 20

time: 96.6 us -> 95.9 us (level)
  Pallas kernels: 33.8 us -> 29.6 us
  starting transfers between devices: 30.9 us -> 34.1 us
    ppermute x21, starting transfers between devices: 23.6 us -> 26.8 us  [across(): return lax.ppermute(value, 'elem', [(i, partner(i)) for i in range(n)])]
    pallas_call x1, Pallas kernels: 5.39 us -> 3.04 us  [body(): pl.pallas_call(functools.partial(far_kernel, n, cap), out_shape=slot_shap...]
    pallas_call x1, Pallas kernels: 22.4 us -> 20.6 us  [body(): pl.pallas_call(functools.partial(near_kernel, n), grid=(rows,), out_shape...]
  transfers between devices with their start and end apart: 22 -> 22, of which waited for: 8 -> 7; matrix products, arithmetic and copies ran while one was open for 3% -> 3% of each run, Pallas kernels for 25% -> 24%
where the time goes in v3:
time: 95.9 us; the launch traced here: 95.4 us
  starting transfers between devices  34.1 us (36%)
  Pallas kernels  29.6 us (31%)
  waiting for transfers between devices  27.4 us (29%)
  local copies, waits for them, and re-layouts  3.4 us (4%)
    ppermute x21, waiting for transfers between devices, across(): return lax.ppermute(value, 'elem', [(i, partner(i)) for i in range(n)])  27.4 us
    ppermute x21, starting transfers between devices, across(): return lax.ppermute(value, 'elem', [(i, partner(i)) for i in range(n)])  26.8 us
    pallas_call x1, Pallas kernels, body(): pl.pallas_call(functools.partial(near_kernel, n), grid=(rows,), out_shape...  20.6 us
    all_to_all x1, starting transfers between devices, body(): lax.all_to_all(send.reshape(n, serve_count * B, LANES), 'elem', split_axi...  7.3 us
    pallas_call x1, Pallas kernels, body(): pl.pallas_call(functools.partial(prep_kernel, n), out_shape=(shape((rows,...  3.16 us
    pallas_call x1, Pallas kernels, body(): pl.pallas_call(functools.partial(far_kernel, n, cap), out_shape=slot_shap...  3.04 us
    unnamed x7, local copies, waits for them, and re-layouts  3.01 us
    pallas_call x2, Pallas kernels, combine(): pl.pallas_call(functools.partial(kernel, n), out_shape=out_shape, in_spec...  2.06 us
  transfers between devices with their start and end apart: 22, of which 7 were waited for; matrix products, arithmetic and copies ran while one was open for 3% of the time, Pallas kernels for 24%

profile of v3, /device:TPU:0, one launch (start us, length us, event | category | flops | bytes accessed | tf_op | source)
XLA Modules:
  0.0 95.4 jit_solution(62206678344051051)
XLA Ops:
  0.0 3.2 %prep.1 = (f32[32,64,128]{2,1,0:T(8,128)S(1)}, f32[32,2,64,128]{3,2,1,0:T(8,128)}) custom-call(s32[1]{0:T(128)} %bitcast.me_ref, s32[2,31]{1,0:T(2,128)} %bitcast.35, f32[32,64,128]{2,1,0:T(8,128)} %bitcast.28), custom_call_target="tpu_custom_call" | custom-call | tf_op jit(solution)/shard_map/prep/pallas_call | solution.py:357
  3.2 7.3 %all-to-all-start = ((f32[32,128,128]{2,1,0:T(8,128)}), f32[32,128,128]{2,1,0:T(8,128)S(1)}, u32[]{:S(2)}, u32[]{:S(2)}) async-start(f32[32,128,128]{2,1,0:T(8,128)} %bitcast.27), calls=%async_computation | async-start | bytes 4194304 | tf_op jit(solution)/shard_map/all_to_all | solution.py:374
  10.8 2.6 %collective-permute-start.2 = (s32[1,4,32]{2,1,0:T(4,128)S(1)}, s32[1,4,32]{2,1,0:T(4,128)S(1)}, u32[]{:S(2)}, u32[]{:S(2)}) collective-permute-start(s32[1,4,32]{2,1,0:T(4,128)S(1)} %bitcast.30), channel_id=1, source_target_pairs={{0,6},{1,7},{2,4},{3,5},{4,2},{5,3},{6,0},{7,1},{8,14},{9,15},{10,... | collective-permute-start | bytes 1544 | tf_op jit(solution)/shard_map/ppermute | solution.py:354
  15.0 3.6 %collective-permute-start.6 = (s32[2,4,32]{2,1,0:T(4,128)S(1)}, s32[2,4,32]{2,1,0:T(4,128)S(1)}, u32[]{:S(2)}, u32[]{:S(2)}) collective-permute-start(s32[2,4,32]{2,1,0:T(4,128)S(1)} %pad_add_fusion.2), channel_id=1, source_target_pairs={{0,24},{1,25},{2,26},{3,27},{4,28},{5,29},{6,30},{7,31},{8,16},{9,... | collective-permute-start | bytes 3080 | tf_op jit(solution)/shard_map/ppermute | solution.py:354
  18.6 2.7 %copy.12 = f32[28,8,32,128]{3,2,1,0:T(8,128)S(1)} copy(f32[28,8,32,128]{3,1,2,0:T(8,128)} %bitcast.26) | data formatting | bytes 7340032
  22.0 20.6 %near.1 = (bf16[256,128,128]{2,1,0:T(8,128)(2,1)}, f32[128,32,128]{2,1,0:T(8,128)}, s32[2304]{0:T(1024)S(1)}) custom-call(s32[1]{0:T(128)S(6)} %copy.13.count_row, s32[7,32]{1,0:T(8,128)S(1)} %bitcast.24, s32[32,28]{1,0:T(8,128)S(1)} %copy-done, s32[1]{0:T(128)} %bitcast.me_ref, f32[32,64,128]{2,1,0:T(8,128)S(1)} %get-tuple-element.32.own_ref, ...), custom_call_target="tpu_custom_call" | custom-call | flops 3758096384 | bytes 16777216 | tf_op jit(solution)/shard_map/near/pallas_call | solution.py:393
  42.6 1.3 %collective-permute-start.4 = (s32[2,4,32]{2,1,0:T(4,128)S(1)}, s32[2,4,32]{2,1,0:T(4,128)S(1)}, u32[]{:S(2)}, u32[]{:S(2)}) collective-permute-start(s32[2,4,32]{2,1,0:T(4,128)S(1)} %pad_add_fusion.2), channel_id=1, source_target_pairs={{0,8},{1,9},{2,10},{3,11},{4,12},{5,13},{6,14},{7,15},{8,0},{9,1},... | collective-permute-start | bytes 3080 | tf_op jit(solution)/shard_map/ppermute | solution.py:354
  43.9 5.4 %collective-permute-done.6 = s32[2,4,32]{2,1,0:T(4,128)S(1)} collective-permute-done((s32[2,4,32]{2,1,0:T(4,128)S(1)}, s32[2,4,32]{2,1,0:T(4,128)S(1)}, u32[]{:S(2)}, u32[]{:S(2)}) %collective-permute-start.6) | collective-permute-done | bytes 1056 | tf_op jit(solution)/shard_map/ppermute | solution.py:354
  49.3 10.4 %collective-permute-done.5 = s32[2,4,32]{2,1,0:T(4,128)S(1)} collective-permute-done((s32[2,4,32]{2,1,0:T(4,128)S(1)}, s32[2,4,32]{2,1,0:T(4,128)S(1)}, u32[]{:S(2)}, u32[]{:S(2)}) %collective-permute-start.5) | collective-permute-done | bytes 1056 | tf_op jit(solution)/shard_map/ppermute | solution.py:354
  59.8 3.0 %far.1 = (f32[2,4,64,128]{3,2,1,0:T(8,128)S(1)}, f32[2,4,64,128]{3,2,1,0:T(8,128)S(1)}, f32[2,4,64,128]{3,2,1,0:T(8,128)S(1)}, f32[2,4,64,128]{3,2,1,0:T(8,128)S...) custom-call(s32[1]{0:T(128)} %bitcast.me_ref, ...), custom_call_target="tpu_custom_call" | custom-call | flops 1879048192 | bytes 16777216 | tf_op jit(solution)/shard_map/far/pallas_call | solution.py:420
  62.8 4.0 %collective-permute-start.7 = (f32[2,4,64,128]{3,2,1,0:T(8,128)S(1)}, f32[2,4,64,128]{3,2,1,0:T(8,128)S(1)}, u32[]{:S(2)}, u32[]{:S(2)}) collective-permute-start(f32[2,4,64,128]{3,2,1,0:T(8,128)S(1)} %get-tuple-element.39), channel_id=1, source_target_pairs={{0,2},{1,3},{2,0},{3,1},{4,6},{5,7},{6,4},{7,5},{8,10},{9,11},{10,... | collective-permute-start | bytes 786440 | tf_op jit(solution)/shard_map/ppermute | solution.py:354
  66.8 1.5 %collective-permute-start.9 = (f32[2,4,64,128]{3,2,1,0:T(8,128)S(1)}, f32[2,4,64,128]{3,2,1,0:T(8,128)S(1)}, u32[]{:S(2)}, u32[]{:S(2)}) collective-permute-start(f32[2,4,64,128]{3,2,1,0:T(8,128)S(1)} %get-tuple-element.41), channel_id=1, source_target_pairs={{0,6},{1,7},{2,4},{3,5},{4,2},{5,3},{6,0},{7,1},{8,14},{9,15},{10,... | collective-permute-start | bytes 786440 | tf_op jit(solution)/shard_map/ppermute | solution.py:354
  68.9 3.3 %collective-permute-start.16 = (f32[2,4,4,16,128]{4,3,2,1,0:T(8,128)S(1)}, f32[2,4,4,16,128]{4,3,2,1,0:T(8,128)S(1)}, u32[]{:S(2)}, u32[]{:S(2)}) collective-permute-start(f32[2,4,4,16,128]{4,3,2,1,0:T(8,128)S(1)} %get-tuple-element.48), channel_id=1, source_target_pairs={{0,24},{1,25},{2,26},{3,27},{4,28},{5,29},{6,30},{7,31},{8,0},{9,1... | collective-permute-start | bytes 786440 | tf_op jit(solution)/shard_map/ppermute | solution.py:354
  72.2 1.4 %collective-permute-done.7.refs_1_ = f32[2,4,64,128]{3,2,1,0:T(8,128)S(1)} collective-permute-done((f32[2,4,64,128]{3,2,1,0:T(8,128)S(1)}, f32[2,4,64,128]{3,2,1,0:T(8,128)S(1)}, u32[]{:S(2)}, u32[]{:S(2)}) %collective-permute-start.7) | collective-permute-done | bytes 262176 | tf_op jit(solution)/shard_map/ppermute | solution.py:354
  73.6 5.2 %collective-permute-done.8.refs_2_ = f32[2,4,64,128]{3,2,1,0:T(8,128)S(1)} collective-permute-done((f32[2,4,64,128]{3,2,1,0:T(8,128)S(1)}, f32[2,4,64,128]{3,2,1,0:T(8,128)S(1)}, u32[]{:S(2)}, u32[]{:S(2)}) %collective-permute-start.8) | collective-permute-done | bytes 262176 | tf_op jit(solution)/shard_map/ppermute | solution.py:354
  78.8 1.1 %combine_far_kernel.1 = (f32[8,64,128]{2,1,0:T(8,128)S(1)}, f32[8,64,128]{2,1,0:T(8,128)S(1)}) custom-call(s32[1]{0:T(128)} %bitcast.me_ref, s32[32,32]{1,0:T(8,128)S(1)} %bitcast.22, f32[2,4,64,128]{3,2,1,0:T(8,128)S(1)} %get-tuple-element.38.refs_0_, f32[2,4,64,128]{3,2,1,0:T(8,128)S(1)} %collective-permute-done.7.refs_1_, ...), custom_call_target="tpu_custom_call" | custom-call | tf_op jit(solution)/shard_map/combine_far_kernel/pallas_call | solution.py:438
  81.6 1.2 %collective-permute-start.13 = (f32[8,16,128]{2,1,0:T(8,128)S(1)}, f32[8,16,128]{2,1,0:T(8,128)S(1)}, u32[]{:S(2)}, u32[]{:S(2)}) collective-permute-start(f32[8,16,128]{2,1,0:T(8,128)S(1)} %get-tuple-element.53), channel_id=1, source_target_pairs={{0,8},{1,9},{2,10},{3,11},{4,12},{5,13},{6,14},{7,15},{8,16},{9,17... | collective-permute-start | bytes 196616 | tf_op jit(solution)/shard_map/ppermute | solution.py:354
  82.8 2.1 %collective-permute-start.11 = (f32[8,32,128]{2,1,0:T(8,128)S(1)}, f32[8,32,128]{2,1,0:T(8,128)S(1)}, u32[]{:S(2)}, u32[]{:S(2)}) collective-permute-start(f32[8,32,128]{2,1,0:T(8,128)S(1)} %slice_add_fusion), channel_id=1, source_target_pairs={{0,16},{1,17},{2,18},{3,19},{4,20},{5,21},{6,22},{7,23},{8,24},{9,... | collective-permute-start | bytes 393224 | tf_op jit(solution)/shard_map/ppermute | solution.py:354
  84.9 0.9 combine_own_kernel.1
  86.4 1.7 %collective-permute-start.19 = (f32[8,32,128]{2,1,0:T(8,128)S(1)}, f32[8,32,128]{2,1,0:T(8,128)S(1)}, u32[]{:S(2)}, u32[]{:S(2)}) collective-permute-start(f32[8,32,128]{2,1,0:T(8,128)S(1)} %get-tuple-element.51), channel_id=1, source_target_pairs={{0,4},{1,5},{2,6},{3,7},{4,0},{5,1},{6,2},{7,3},{8,12},{9,13},{10,... | collective-permute-start | bytes 393224 | tf_op jit(solution)/shard_map/ppermute | solution.py:354
  88.2 1.2 %collective-permute-start.20 = (f32[8,32,128]{2,1,0:T(8,128)S(1)}, f32[8,32,128]{2,1,0:T(8,128)S(1)}, u32[]{:S(2)}, u32[]{:S(2)}) collective-permute-start(f32[8,32,128]{2,1,0:T(8,128)S(1)} %get-tuple-element.52), channel_id=1, source_target_pairs={{0,6},{1,7},{2,4},{3,5},{4,2},{5,3},{6,0},{7,1},{8,14},{9,15},{10,... | collective-permute-start | bytes 393224 | tf_op jit(solution)/shard_map/ppermute | solution.py:354
  89.4 1.2 %collective-permute-start.12 = (f32[8,16,128]{2,1,0:T(8,128)S(1)}, f32[8,16,128]{2,1,0:T(8,128)S(1)}, u32[]{:S(2)}, u32[]{:S(2)}) collective-permute-start(f32[8,16,128]{2,1,0:T(8,128)S(1)} %get-tuple-element.54), channel_id=1, source_target_pairs={{0,24},{1,25},{2,26},{3,27},{4,28},{5,29},{6,30},{7,31},{8,0},{9,1... | collective-permute-start | bytes 196616 | tf_op jit(solution)/shard_map/ppermute | solution.py:354
  90.6 4.0 %collective-permute-done.12.refs_1_ = f32[8,16,128]{2,1,0:T(8,128)S(1)} collective-permute-done((f32[8,16,128]{2,1,0:T(8,128)S(1)}, f32[8,16,128]{2,1,0:T(8,128)S(1)}, u32[]{:S(2)}, u32[]{:S(2)}) %collective-permute-start.12) | collective-permute-done | bytes 65568 | tf_op jit(solution)/shard_map/ppermute | solution.py:354
  94.6 0.8 final.1
  (42 shorter events, 4.8 us)
Async XLA Ops:
  0.0 10.5 %copy-start.2 = (s32[1,32,4]{1,2,0:T(4,128)S(1)}, s32[1,32,4]{1,2,0:T(4,128)}, u32[]{:S(2)}) copy-start(s32[1,32,4]{1,2,0:T(4,128)} %param.13) | copy-start | bytes 1540
  3.2 56.6 %all-to-all-start = ((f32[32,128,128]{2,1,0:T(8,128)}), f32[32,128,128]{2,1,0:T(8,128)S(1)}, u32[]{:S(2)}, u32[]{:S(2)}) async-start(f32[32,128,128]{2,1,0:T(8,128)} %bitcast.27), calls=%async_computation | async-start | bytes 4194304 | tf_op jit(solution)/shard_map/all_to_all | solution.py:374
  10.5 4.5 %collective-permute-start.3 = (s32[1,4,32]{2,1,0:T(4,128)S(1)}, s32[1,4,32]{2,1,0:T(4,128)S(1)}, u32[]{:S(2)}, u32[]{:S(2)}) collective-permute-start(s32[1,4,32]{2,1,0:T(4,128)S(1)} %bitcast.29), channel_id=1, source_target_pairs={{0,1},{1,0},{2,3},{3,2},{4,5},{5,4},{6,7},{7,6},{8,9},{9,8},{10,11... | collective-permute-start | bytes 1544 | tf_op jit(solution)/shard_map/ppermute | solution.py:354
  10.8 31.8 %collective-permute-start.2 = (s32[1,4,32]{2,1,0:T(4,128)S(1)}, s32[1,4,32]{2,1,0:T(4,128)S(1)}, u32[]{:S(2)}, u32[]{:S(2)}) collective-permute-start(s32[1,4,32]{2,1,0:T(4,128)S(1)} %bitcast.30), channel_id=1, source_target_pairs={{0,6},{1,7},{2,4},{3,5},{4,2},{5,3},{6,0},{7,1},{8,14},{9,15},{10,... | collective-permute-start | bytes 1544 | tf_op jit(solution)/shard_map/ppermute | solution.py:354
  13.4 30.5 %collective-permute-start.1 = (s32[1,4,32]{2,1,0:T(4,128)S(1)}, s32[1,4,32]{2,1,0:T(4,128)S(1)}, u32[]{:S(2)}, u32[]{:S(2)}) collective-permute-start(s32[1,4,32]{2,1,0:T(4,128)S(1)} %bitcast.31), channel_id=1, source_target_pairs={{0,4},{1,5},{2,6},{3,7},{4,0},{5,1},{6,2},{7,3},{8,12},{9,13},{10,... | collective-permute-start | bytes 1544 | tf_op jit(solution)/shard_map/ppermute | solution.py:354
  14.0 30.0 %collective-permute-start = (s32[1,4,32]{2,1,0:T(4,128)S(1)}, s32[1,4,32]{2,1,0:T(4,128)S(1)}, u32[]{:S(2)}, u32[]{:S(2)}) collective-permute-start(s32[1,4,32]{2,1,0:T(4,128)S(1)} %bitcast.32), channel_id=1, source_target_pairs={{0,2},{1,3},{2,0},{3,1},{4,6},{5,7},{6,4},{7,5},{8,10},{9,11},{10,... | collective-permute-start | bytes 1544 | tf_op jit(solution)/shard_map/ppermute | solution.py:354
  15.0 34.3 %collective-permute-start.6 = (s32[2,4,32]{2,1,0:T(4,128)S(1)}, s32[2,4,32]{2,1,0:T(4,128)S(1)}, u32[]{:S(2)}, u32[]{:S(2)}) collective-permute-start(s32[2,4,32]{2,1,0:T(4,128)S(1)} %pad_add_fusion.2), channel_id=1, source_target_pairs={{0,24},{1,25},{2,26},{3,27},{4,28},{5,29},{6,30},{7,31},{8,16},{9,... | collective-permute-start | bytes 3080 | tf_op jit(solution)/shard_map/ppermute | solution.py:354
  18.6 41.2 %collective-permute-start.5 = (s32[2,4,32]{2,1,0:T(4,128)S(1)}, s32[2,4,32]{2,1,0:T(4,128)S(1)}, u32[]{:S(2)}, u32[]{:S(2)}) collective-permute-start(s32[2,4,32]{2,1,0:T(4,128)S(1)} %pad_add_fusion.2), channel_id=1, source_target_pairs={{0,16},{1,17},{2,18},{3,19},{4,20},{5,21},{6,22},{7,23},{8,24},{9,... | collective-permute-start | bytes 3080 | tf_op jit(solution)/shard_map/ppermute | solution.py:354
  21.3 0.7 copy-start
  42.6 17.2 %collective-permute-start.4 = (s32[2,4,32]{2,1,0:T(4,128)S(1)}, s32[2,4,32]{2,1,0:T(4,128)S(1)}, u32[]{:S(2)}, u32[]{:S(2)}) collective-permute-start(s32[2,4,32]{2,1,0:T(4,128)S(1)} %pad_add_fusion.2), channel_id=1, source_target_pairs={{0,8},{1,9},{2,10},{3,11},{4,12},{5,13},{6,14},{7,15},{8,0},{9,1},... | collective-permute-start | bytes 3080 | tf_op jit(solution)/shard_map/ppermute | solution.py:354
  62.8 10.8 %collective-permute-start.7 = (f32[2,4,64,128]{3,2,1,0:T(8,128)S(1)}, f32[2,4,64,128]{3,2,1,0:T(8,128)S(1)}, u32[]{:S(2)}, u32[]{:S(2)}) collective-permute-start(f32[2,4,64,128]{3,2,1,0:T(8,128)S(1)} %get-tuple-element.39), channel_id=1, source_target_pairs={{0,2},{1,3},{2,0},{3,1},{4,6},{5,7},{6,4},{7,5},{8,10},{9,11},{10,... | collective-permute-start | bytes 786440 | tf_op jit(solution)/shard_map/ppermute | solution.py:354
  66.8 12.0 %collective-permute-start.8 = (f32[2,4,64,128]{3,2,1,0:T(8,128)S(1)}, f32[2,4,64,128]{3,2,1,0:T(8,128)S(1)}, u32[]{:S(2)}, u32[]{:S(2)}) collective-permute-start(f32[2,4,64,128]{3,2,1,0:T(8,128)S(1)} %get-tuple-element.40), channel_id=1, source_target_pairs={{0,4},{1,5},{2,6},{3,7},{4,0},{5,1},{6,2},{7,3},{8,12},{9,13},{10,... | collective-permute-start | bytes 786440 | tf_op jit(solution)/shard_map/ppermute | solution.py:354
  66.8 12.0 %collective-permute-start.9 = (f32[2,4,64,128]{3,2,1,0:T(8,128)S(1)}, f32[2,4,64,128]{3,2,1,0:T(8,128)S(1)}, u32[]{:S(2)}, u32[]{:S(2)}) collective-permute-start(f32[2,4,64,128]{3,2,1,0:T(8,128)S(1)} %get-tuple-element.41), channel_id=1, source_target_pairs={{0,6},{1,7},{2,4},{3,5},{4,2},{5,3},{6,0},{7,1},{8,14},{9,15},{10,... | collective-permute-start | bytes 786440 | tf_op jit(solution)/shard_map/ppermute | solution.py:354
  68.3 12.2 %collective-permute-start.15 = (f32[2,4,4,16,128]{4,3,2,1,0:T(8,128)S(1)}, f32[2,4,4,16,128]{4,3,2,1,0:T(8,128)S(1)}, u32[]{:S(2)}, u32[]{:S(2)}) collective-permute-start(f32[2,4,4,16,128]{4,3,2,1,0:T(8,128)S(1)} %get-tuple-element.47), channel_id=1, source_target_pairs={{0,8},{1,9},{2,10},{3,11},{4,12},{5,13},{6,14},{7,15},{8,16},{9,17... | collective-permute-start | bytes 786440 | tf_op jit(solution)/shard_map/ppermute | solution.py:354
  68.9 11.9 %collective-permute-start.16 = (f32[2,4,4,16,128]{4,3,2,1,0:T(8,128)S(1)}, f32[2,4,4,16,128]{4,3,2,1,0:T(8,128)S(1)}, u32[]{:S(2)}, u32[]{:S(2)}) collective-permute-start(f32[2,4,4,16,128]{4,3,2,1,0:T(8,128)S(1)} %get-tuple-element.48), channel_id=1, source_target_pairs={{0,24},{1,25},{2,26},{3,27},{4,28},{5,29},{6,30},{7,31},{8,0},{9,1... | collective-permute-start | bytes 786440 | tf_op jit(solution)/shard_map/ppermute | solution.py:354
  80.0 1.6 %collective-permute-start.10 = (f32[8,64,128]{2,1,0:T(8,128)S(1)}, f32[8,64,128]{2,1,0:T(8,128)S(1)}, u32[]{:S(2)}, u32[]{:S(2)}) collective-permute-start(f32[8,64,128]{2,1,0:T(8,128)S(1)} %get-tuple-element.43), channel_id=1, source_target_pairs={{0,1},{1,0},{2,3},{3,2},{4,5},{5,4},{6,7},{7,6},{8,9},{9,8},{10,11... | collective-permute-start | bytes 786440 | tf_op jit(solution)/shard_map/ppermute | solution.py:354
  80.0 4.8 %collective-permute-start.14 = (f32[4,4,32,128]{3,2,1,0:T(8,128)S(1)}, f32[4,4,32,128]{3,2,1,0:T(8,128)S(1)}, u32[]{:S(2)}, u32[]{:S(2)}) collective-permute-start(f32[4,4,32,128]{3,2,1,0:T(8,128)S(1)} %get-tuple-element.46), channel_id=1, source_target_pairs={{0,1},{1,0},{2,3},{3,2},{4,5},{5,4},{6,7},{7,6},{8,9},{9,8},{10,11... | collective-permute-start | bytes 786440 | tf_op jit(solution)/shard_map/ppermute | solution.py:354
  80.8 4.0 %collective-permute-start.17 = (f32[2,4,4,16,128]{4,3,2,1,0:T(8,128)S(1)}, f32[2,4,4,16,128]{4,3,2,1,0:T(8,128)S(1)}, u32[]{:S(2)}, u32[]{:S(2)}) collective-permute-start(f32[2,4,4,16,128]{4,3,2,1,0:T(8,128)S(1)} %pad_maximum_fusion), channel_id=1, source_target_pairs={{0,1},{1,0},{2,3},{3,2},{4,5},{5,4},{6,7},{7,6},{8,9},{9,8},{10,11... | collective-permute-start | bytes 786440 | tf_op jit(solution)/shard_map/ppermute | solution.py:354
  81.6 7.8 %collective-permute-start.13 = (f32[8,16,128]{2,1,0:T(8,128)S(1)}, f32[8,16,128]{2,1,0:T(8,128)S(1)}, u32[]{:S(2)}, u32[]{:S(2)}) collective-permute-start(f32[8,16,128]{2,1,0:T(8,128)S(1)} %get-tuple-element.53), channel_id=1, source_target_pairs={{0,8},{1,9},{2,10},{3,11},{4,12},{5,13},{6,14},{7,15},{8,16},{9,17... | collective-permute-start | bytes 196616 | tf_op jit(solution)/shard_map/ppermute | solution.py:354
  82.8 11.8 %collective-permute-start.11 = (f32[8,32,128]{2,1,0:T(8,128)S(1)}, f32[8,32,128]{2,1,0:T(8,128)S(1)}, u32[]{:S(2)}, u32[]{:S(2)}) collective-permute-start(f32[8,32,128]{2,1,0:T(8,128)S(1)} %slice_add_fusion), channel_id=1, source_target_pairs={{0,16},{1,17},{2,18},{3,19},{4,20},{5,21},{6,22},{7,23},{8,24},{9,... | collective-permute-start | bytes 393224 | tf_op jit(solution)/shard_map/ppermute | solution.py:354
  85.8 8.8 %collective-permute-start.18 = (f32[8,32,128]{2,1,0:T(8,128)S(1)}, f32[8,32,128]{2,1,0:T(8,128)S(1)}, u32[]{:S(2)}, u32[]{:S(2)}) collective-permute-start(f32[8,32,128]{2,1,0:T(8,128)S(1)} %get-tuple-element.50), channel_id=1, source_target_pairs={{0,2},{1,3},{2,0},{3,1},{4,6},{5,7},{6,4},{7,5},{8,10},{9,11},{10,... | collective-permute-start | bytes 393224 | tf_op jit(solution)/shard_map/ppermute | solution.py:354
  86.4 8.2 %collective-permute-start.19 = (f32[8,32,128]{2,1,0:T(8,128)S(1)}, f32[8,32,128]{2,1,0:T(8,128)S(1)}, u32[]{:S(2)}, u32[]{:S(2)}) collective-permute-start(f32[8,32,128]{2,1,0:T(8,128)S(1)} %get-tuple-element.51), channel_id=1, source_target_pairs={{0,4},{1,5},{2,6},{3,7},{4,0},{5,1},{6,2},{7,3},{8,12},{9,13},{10,... | collective-permute-start | bytes 393224 | tf_op jit(solution)/shard_map/ppermute | solution.py:354
  88.2 6.4 %collective-permute-start.20 = (f32[8,32,128]{2,1,0:T(8,128)S(1)}, f32[8,32,128]{2,1,0:T(8,128)S(1)}, u32[]{:S(2)}, u32[]{:S(2)}) collective-permute-start(f32[8,32,128]{2,1,0:T(8,128)S(1)} %get-tuple-element.52), channel_id=1, source_target_pairs={{0,6},{1,7},{2,4},{3,5},{4,2},{5,3},{6,0},{7,1},{8,14},{9,15},{10,... | collective-permute-start | bytes 393224 | tf_op jit(solution)/shard_map/ppermute | solution.py:354
  89.4 5.2 %collective-permute-start.12 = (f32[8,16,128]{2,1,0:T(8,128)S(1)}, f32[8,16,128]{2,1,0:T(8,128)S(1)}, u32[]{:S(2)}, u32[]{:S(2)}) collective-permute-start(f32[8,16,128]{2,1,0:T(8,128)S(1)} %get-tuple-element.54), channel_id=1, source_target_pairs={{0,24},{1,25},{2,26},{3,27},{4,28},{5,29},{6,30},{7,31},{8,0},{9,1... | collective-permute-start | bytes 196616 | tf_op jit(solution)/shard_map/ppermute | solution.py:354
  (1 other events, 0.7 us)

commit v4 on v3

--- a/solution.py
+++ b/solution.py
@@ -214,7 +214,7 @@
     own_mine, own_other, acc, near, ring, ring_sems, near_sem = refs[outs:]
     me = me_ref[0]
     count = meta[meta.shape[0] - 1]
-    turns = (count + UNROLL - 1) // UNROLL
+    chunks = (count + FETCH - 1) // FETCH
 
     per_turn = UNROLL // FETCH
 
@@ -223,9 +223,10 @@
         return pltpu.make_async_copy(left_hbm.at[pl.ds(i * FETCH, FETCH)], ring.at[buffer], ring_sems.at[buffer])
 
     def fetch(g):
-        @pl.when(g < turns)
-        def go():
-            for i in range(per_turn):
+        for i in range(per_turn):
+
+            @pl.when(g * per_turn + i < chunks)
+            def go():
                 left_copy(g * per_turn + i).start()
 
     ahead = DEPTH // per_turn - 1
@@ -244,7 +245,15 @@
             add_entry(acc, meta, g * UNROLL + u, ring[buffer, u % FETCH], recv)
         return carry
 
-    lax.fori_loop(0, turns, products, 0)
+    def chunk_products(i, carry):
+        left_copy(i).wait()
+        for u in range(FETCH):
+            add_entry(acc, meta, i * FETCH + u, ring[lax.rem(i, DEPTH), u], recv)
+        return carry
+
+    whole = count // UNROLL
+    lax.fori_loop(0, whole, products, 0)
+    lax.fori_loop(whole * per_turn, chunks, chunk_products, 0)
     near_copy.wait()
     place = lax.rem(me // 2, PLACES)
     group = me // GROUP

time: 95.9 us -> 95.5 us (level)
  waiting for transfers between devices: 27.4 us -> 25 us
  Pallas kernels: 29.6 us -> 31.9 us
    ppermute x21, waiting for transfers between devices: 27.4 us -> 25 us  [across(): return lax.ppermute(value, 'elem', [(i, partner(i)) for i in range(n)])]
    pallas_call x1, Pallas kernels: 20.6 us -> 21.7 us  [body(): pl.pallas_call(functools.partial(near_kernel, n), grid=(rows,), out_shape...]
    pallas_call x1, Pallas kernels: 3.04 us -> 4.13 us  [body(): pl.pallas_call(functools.partial(far_kernel, n, cap), out_shape=slot_shap...]
  transfers between devices with their start and end apart: 22 -> 22, of which waited for: 7 -> 8; matrix products, arithmetic and copies ran while one was open for 3% -> 3% of each run, Pallas kernels for 24% -> 25%
where the time goes in v4:
time: 95.5 us; the launch traced here: 95.3 us
  starting transfers between devices  34.1 us (36%)
  Pallas kernels  31.9 us (33%)
  waiting for transfers between devices  25 us (26%)
  local copies, waits for them, and re-layouts  3.4 us (4%)
    ppermute x21, starting transfers between devices, across(): return lax.ppermute(value, 'elem', [(i, partner(i)) for i in range(n)])  26.8 us
    ppermute x21, waiting for transfers between devices, across(): return lax.ppermute(value, 'elem', [(i, partner(i)) for i in range(n)])  25 us
    pallas_call x1, Pallas kernels, body(): pl.pallas_call(functools.partial(near_kernel, n), grid=(rows,), out_shape...  21.7 us
    all_to_all x1, starting transfers between devices, body(): lax.all_to_all(send.reshape(n, serve_count * B, LANES), 'elem', split_axi...  7.3 us
    pallas_call x1, Pallas kernels, body(): pl.pallas_call(functools.partial(far_kernel, n, cap), out_shape=slot_shap...  4.13 us
    pallas_call x1, Pallas kernels, body(): pl.pallas_call(functools.partial(prep_kernel, n), out_shape=(shape((rows,...  3.16 us
    unnamed x7, local copies, waits for them, and re-layouts  3.01 us
    pallas_call x2, Pallas kernels, combine(): pl.pallas_call(functools.partial(kernel, n), out_shape=out_shape, in_spec...  2.06 us
  transfers between devices with their start and end apart: 22, of which 8 were waited for; matrix products, arithmetic and copies ran while one was open for 3% of the time, Pallas kernels for 25%

profile of v4, /device:TPU:0, one launch (start us, length us, event | category | flops | bytes accessed | tf_op | source)
XLA Modules:
  0.0 95.3 jit_solution(17825556620519538516)
XLA Ops:
  0.0 3.2 %prep.1 = (f32[32,64,128]{2,1,0:T(8,128)S(1)}, f32[32,2,64,128]{3,2,1,0:T(8,128)}) custom-call(s32[1]{0:T(128)} %bitcast.me_ref, s32[2,31]{1,0:T(2,128)} %bitcast.35, f32[32,64,128]{2,1,0:T(8,128)} %bitcast.28), custom_call_target="tpu_custom_call" | custom-call | tf_op jit(solution)/shard_map/prep/pallas_call | solution.py:366
  3.2 7.3 %all-to-all-start = ((f32[32,128,128]{2,1,0:T(8,128)}), f32[32,128,128]{2,1,0:T(8,128)S(1)}, u32[]{:S(2)}, u32[]{:S(2)}) async-start(f32[32,128,128]{2,1,0:T(8,128)} %bitcast.27), calls=%async_computation | async-start | bytes 4194304 | tf_op jit(solution)/shard_map/all_to_all | solution.py:383
  10.8 2.6 %collective-permute-start.2 = (s32[1,4,32]{2,1,0:T(4,128)S(1)}, s32[1,4,32]{2,1,0:T(4,128)S(1)}, u32[]{:S(2)}, u32[]{:S(2)}) collective-permute-start(s32[1,4,32]{2,1,0:T(4,128)S(1)} %bitcast.30), channel_id=1, source_target_pairs={{0,6},{1,7},{2,4},{3,5},{4,2},{5,3},{6,0},{7,1},{8,14},{9,15},{10,... | collective-permute-start | bytes 1544 | tf_op jit(solution)/shard_map/ppermute | solution.py:363
  15.0 3.6 %collective-permute-start.6 = (s32[2,4,32]{2,1,0:T(4,128)S(1)}, s32[2,4,32]{2,1,0:T(4,128)S(1)}, u32[]{:S(2)}, u32[]{:S(2)}) collective-permute-start(s32[2,4,32]{2,1,0:T(4,128)S(1)} %pad_add_fusion.2), channel_id=1, source_target_pairs={{0,24},{1,25},{2,26},{3,27},{4,28},{5,29},{6,30},{7,31},{8,16},{9,... | collective-permute-start | bytes 3080 | tf_op jit(solution)/shard_map/ppermute | solution.py:363
  18.6 2.7 %copy.12 = f32[28,8,32,128]{3,2,1,0:T(8,128)S(1)} copy(f32[28,8,32,128]{3,1,2,0:T(8,128)} %bitcast.26) | data formatting | bytes 7340032
  22.0 21.7 %near.1 = (bf16[256,128,128]{2,1,0:T(8,128)(2,1)}, f32[128,32,128]{2,1,0:T(8,128)}, s32[2304]{0:T(1024)S(1)}) custom-call(s32[1]{0:T(128)S(6)} %copy.13.count_row, s32[7,32]{1,0:T(8,128)S(1)} %bitcast.24, s32[32,28]{1,0:T(8,128)S(1)} %copy-done, s32[1]{0:T(128)} %bitcast.me_ref, f32[32,64,128]{2,1,0:T(8,128)S(1)} %get-tuple-element.32.own_ref, ...), custom_call_target="tpu_custom_call" | custom-call | flops 3758096384 | bytes 16777216 | tf_op jit(solution)/shard_map/near/pallas_call | solution.py:402
  43.7 3.8 %collective-permute-start.4 = (s32[2,4,32]{2,1,0:T(4,128)S(1)}, s32[2,4,32]{2,1,0:T(4,128)S(1)}, u32[]{:S(2)}, u32[]{:S(2)}) collective-permute-start(s32[2,4,32]{2,1,0:T(4,128)S(1)} %pad_add_fusion.2), channel_id=1, source_target_pairs={{0,8},{1,9},{2,10},{3,11},{4,12},{5,13},{6,14},{7,15},{8,0},{9,1},... | collective-permute-start | bytes 3080 | tf_op jit(solution)/shard_map/ppermute | solution.py:363
  47.6 1.7 %collective-permute-done.6 = s32[2,4,32]{2,1,0:T(4,128)S(1)} collective-permute-done((s32[2,4,32]{2,1,0:T(4,128)S(1)}, s32[2,4,32]{2,1,0:T(4,128)S(1)}, u32[]{:S(2)}, u32[]{:S(2)}) %collective-permute-start.6) | collective-permute-done | bytes 1056 | tf_op jit(solution)/shard_map/ppermute | solution.py:363
  49.3 10.4 %collective-permute-done.5 = s32[2,4,32]{2,1,0:T(4,128)S(1)} collective-permute-done((s32[2,4,32]{2,1,0:T(4,128)S(1)}, s32[2,4,32]{2,1,0:T(4,128)S(1)}, u32[]{:S(2)}, u32[]{:S(2)}) %collective-permute-start.5) | collective-permute-done | bytes 1056 | tf_op jit(solution)/shard_map/ppermute | solution.py:363
  59.8 4.1 %far.1 = (f32[2,4,64,128]{3,2,1,0:T(8,128)S(1)}, f32[2,4,64,128]{3,2,1,0:T(8,128)S(1)}, f32[2,4,64,128]{3,2,1,0:T(8,128)S(1)}, f32[2,4,64,128]{3,2,1,0:T(8,128)S...) custom-call(s32[1]{0:T(128)} %bitcast.me_ref, ...), custom_call_target="tpu_custom_call" | custom-call | flops 1879048192 | bytes 16777216 | tf_op jit(solution)/shard_map/far/pallas_call | solution.py:429
  63.9 0.9 collective-permute-start.7
  64.8 1.0 %collective-permute-start.8 = (f32[2,4,64,128]{3,2,1,0:T(8,128)S(1)}, f32[2,4,64,128]{3,2,1,0:T(8,128)S(1)}, u32[]{:S(2)}, u32[]{:S(2)}) collective-permute-start(f32[2,4,64,128]{3,2,1,0:T(8,128)S(1)} %get-tuple-element.40), channel_id=1, source_target_pairs={{0,4},{1,5},{2,6},{3,7},{4,0},{5,1},{6,2},{7,3},{8,12},{9,13},{10,... | collective-permute-start | bytes 786440 | tf_op jit(solution)/shard_map/ppermute | solution.py:363
  65.7 1.7 %collective-permute-start.9 = (f32[2,4,64,128]{3,2,1,0:T(8,128)S(1)}, f32[2,4,64,128]{3,2,1,0:T(8,128)S(1)}, u32[]{:S(2)}, u32[]{:S(2)}) collective-permute-start(f32[2,4,64,128]{3,2,1,0:T(8,128)S(1)} %get-tuple-element.41), channel_id=1, source_target_pairs={{0,6},{1,7},{2,4},{3,5},{4,2},{5,3},{6,0},{7,1},{8,14},{9,15},{10,... | collective-permute-start | bytes 786440 | tf_op jit(solution)/shard_map/ppermute | solution.py:363
  67.4 1.7 %collective-permute-start.15 = (f32[2,4,4,16,128]{4,3,2,1,0:T(8,128)S(1)}, f32[2,4,4,16,128]{4,3,2,1,0:T(8,128)S(1)}, u32[]{:S(2)}, u32[]{:S(2)}) collective-permute-start(f32[2,4,4,16,128]{4,3,2,1,0:T(8,128)S(1)} %get-tuple-element.47), channel_id=1, source_target_pairs={{0,8},{1,9},{2,10},{3,11},{4,12},{5,13},{6,14},{7,15},{8,16},{9,17... | collective-permute-start | bytes 786440 | tf_op jit(solution)/shard_map/ppermute | solution.py:363
  69.1 2.2 %collective-permute-start.16 = (f32[2,4,4,16,128]{4,3,2,1,0:T(8,128)S(1)}, f32[2,4,4,16,128]{4,3,2,1,0:T(8,128)S(1)}, u32[]{:S(2)}, u32[]{:S(2)}) collective-permute-start(f32[2,4,4,16,128]{4,3,2,1,0:T(8,128)S(1)} %get-tuple-element.48), channel_id=1, source_target_pairs={{0,24},{1,25},{2,26},{3,27},{4,28},{5,29},{6,30},{7,31},{8,0},{9,1... | collective-permute-start | bytes 786440 | tf_op jit(solution)/shard_map/ppermute | solution.py:363
  71.3 1.8 %collective-permute-done.7.refs_1_ = f32[2,4,64,128]{3,2,1,0:T(8,128)S(1)} collective-permute-done((f32[2,4,64,128]{3,2,1,0:T(8,128)S(1)}, f32[2,4,64,128]{3,2,1,0:T(8,128)S(1)}, u32[]{:S(2)}, u32[]{:S(2)}) %collective-permute-start.7) | collective-permute-done | bytes 262176 | tf_op jit(solution)/shard_map/ppermute | solution.py:363
  73.1 6.2 %collective-permute-done.8.refs_2_ = f32[2,4,64,128]{3,2,1,0:T(8,128)S(1)} collective-permute-done((f32[2,4,64,128]{3,2,1,0:T(8,128)S(1)}, f32[2,4,64,128]{3,2,1,0:T(8,128)S(1)}, u32[]{:S(2)}, u32[]{:S(2)}) %collective-permute-start.8) | collective-permute-done | bytes 262176 | tf_op jit(solution)/shard_map/ppermute | solution.py:363
  79.3 1.1 %combine_far_kernel.1 = (f32[8,64,128]{2,1,0:T(8,128)S(1)}, f32[8,64,128]{2,1,0:T(8,128)S(1)}) custom-call(s32[1]{0:T(128)} %bitcast.me_ref, s32[32,32]{1,0:T(8,128)S(1)} %bitcast.22, f32[2,4,64,128]{3,2,1,0:T(8,128)S(1)} %get-tuple-element.38.refs_0_, f32[2,4,64,128]{3,2,1,0:T(8,128)S(1)} %collective-permute-done.7.refs_1_, ...), custom_call_target="tpu_custom_call" | custom-call | tf_op jit(solution)/shard_map/combine_far_kernel/pallas_call | solution.py:447
  82.2 2.1 %collective-permute-start.11 = (f32[8,32,128]{2,1,0:T(8,128)S(1)}, f32[8,32,128]{2,1,0:T(8,128)S(1)}, u32[]{:S(2)}, u32[]{:S(2)}) collective-permute-start(f32[8,32,128]{2,1,0:T(8,128)S(1)} %slice_add_fusion), channel_id=1, source_target_pairs={{0,16},{1,17},{2,18},{3,19},{4,20},{5,21},{6,22},{7,23},{8,24},{9,... | collective-permute-start | bytes 393224 | tf_op jit(solution)/shard_map/ppermute | solution.py:363
  84.3 0.9 combine_own_kernel.1
  85.2 1.5 %collective-permute-start.18 = (f32[8,32,128]{2,1,0:T(8,128)S(1)}, f32[8,32,128]{2,1,0:T(8,128)S(1)}, u32[]{:S(2)}, u32[]{:S(2)}) collective-permute-start(f32[8,32,128]{2,1,0:T(8,128)S(1)} %get-tuple-element.50), channel_id=1, source_target_pairs={{0,2},{1,3},{2,0},{3,1},{4,6},{5,7},{6,4},{7,5},{8,10},{9,11},{10,... | collective-permute-start | bytes 393224 | tf_op jit(solution)/shard_map/ppermute | solution.py:363
  87.4 1.4 %collective-permute-start.20 = (f32[8,32,128]{2,1,0:T(8,128)S(1)}, f32[8,32,128]{2,1,0:T(8,128)S(1)}, u32[]{:S(2)}, u32[]{:S(2)}) collective-permute-start(f32[8,32,128]{2,1,0:T(8,128)S(1)} %get-tuple-element.52), channel_id=1, source_target_pairs={{0,6},{1,7},{2,4},{3,5},{4,2},{5,3},{6,0},{7,1},{8,14},{9,15},{10,... | collective-permute-start | bytes 393224 | tf_op jit(solution)/shard_map/ppermute | solution.py:363
  89.0 1.8 %collective-permute-start.12 = (f32[8,16,128]{2,1,0:T(8,128)S(1)}, f32[8,16,128]{2,1,0:T(8,128)S(1)}, u32[]{:S(2)}, u32[]{:S(2)}) collective-permute-start(f32[8,16,128]{2,1,0:T(8,128)S(1)} %get-tuple-element.54), channel_id=1, source_target_pairs={{0,24},{1,25},{2,26},{3,27},{4,28},{5,29},{6,30},{7,31},{8,0},{9,1... | collective-permute-start | bytes 196616 | tf_op jit(solution)/shard_map/ppermute | solution.py:363
  90.7 3.3 %collective-permute-done.12.refs_1_ = f32[8,16,128]{2,1,0:T(8,128)S(1)} collective-permute-done((f32[8,16,128]{2,1,0:T(8,128)S(1)}, f32[8,16,128]{2,1,0:T(8,128)S(1)}, u32[]{:S(2)}, u32[]{:S(2)}) %collective-permute-start.12) | collective-permute-done | bytes 65568 | tf_op jit(solution)/shard_map/ppermute | solution.py:363
  (42 shorter events, 5.7 us)
Async XLA Ops:
  0.0 10.5 %copy-start.2 = (s32[1,32,4]{1,2,0:T(4,128)S(1)}, s32[1,32,4]{1,2,0:T(4,128)}, u32[]{:S(2)}) copy-start(s32[1,32,4]{1,2,0:T(4,128)} %param.13) | copy-start | bytes 1540
  3.2 56.6 %all-to-all-start = ((f32[32,128,128]{2,1,0:T(8,128)}), f32[32,128,128]{2,1,0:T(8,128)S(1)}, u32[]{:S(2)}, u32[]{:S(2)}) async-start(f32[32,128,128]{2,1,0:T(8,128)} %bitcast.27), calls=%async_computation | async-start | bytes 4194304 | tf_op jit(solution)/shard_map/all_to_all | solution.py:383
  10.5 4.5 %collective-permute-start.3 = (s32[1,4,32]{2,1,0:T(4,128)S(1)}, s32[1,4,32]{2,1,0:T(4,128)S(1)}, u32[]{:S(2)}, u32[]{:S(2)}) collective-permute-start(s32[1,4,32]{2,1,0:T(4,128)S(1)} %bitcast.29), channel_id=1, source_target_pairs={{0,1},{1,0},{2,3},{3,2},{4,5},{5,4},{6,7},{7,6},{8,9},{9,8},{10,11... | collective-permute-start | bytes 1544 | tf_op jit(solution)/shard_map/ppermute | solution.py:363
  10.8 32.9 %collective-permute-start.2 = (s32[1,4,32]{2,1,0:T(4,128)S(1)}, s32[1,4,32]{2,1,0:T(4,128)S(1)}, u32[]{:S(2)}, u32[]{:S(2)}) collective-permute-start(s32[1,4,32]{2,1,0:T(4,128)S(1)} %bitcast.30), channel_id=1, source_target_pairs={{0,6},{1,7},{2,4},{3,5},{4,2},{5,3},{6,0},{7,1},{8,14},{9,15},{10,... | collective-permute-start | bytes 1544 | tf_op jit(solution)/shard_map/ppermute | solution.py:363
  13.4 34.2 %collective-permute-start.1 = (s32[1,4,32]{2,1,0:T(4,128)S(1)}, s32[1,4,32]{2,1,0:T(4,128)S(1)}, u32[]{:S(2)}, u32[]{:S(2)}) collective-permute-start(s32[1,4,32]{2,1,0:T(4,128)S(1)} %bitcast.31), channel_id=1, source_target_pairs={{0,4},{1,5},{2,6},{3,7},{4,0},{5,1},{6,2},{7,3},{8,12},{9,13},{10,... | collective-permute-start | bytes 1544 | tf_op jit(solution)/shard_map/ppermute | solution.py:363
  14.0 33.6 %collective-permute-start = (s32[1,4,32]{2,1,0:T(4,128)S(1)}, s32[1,4,32]{2,1,0:T(4,128)S(1)}, u32[]{:S(2)}, u32[]{:S(2)}) collective-permute-start(s32[1,4,32]{2,1,0:T(4,128)S(1)} %bitcast.32), channel_id=1, source_target_pairs={{0,2},{1,3},{2,0},{3,1},{4,6},{5,7},{6,4},{7,5},{8,10},{9,11},{10,... | collective-permute-start | bytes 1544 | tf_op jit(solution)/shard_map/ppermute | solution.py:363
  15.0 34.3 %collective-permute-start.6 = (s32[2,4,32]{2,1,0:T(4,128)S(1)}, s32[2,4,32]{2,1,0:T(4,128)S(1)}, u32[]{:S(2)}, u32[]{:S(2)}) collective-permute-start(s32[2,4,32]{2,1,0:T(4,128)S(1)} %pad_add_fusion.2), channel_id=1, source_target_pairs={{0,24},{1,25},{2,26},{3,27},{4,28},{5,29},{6,30},{7,31},{8,16},{9,... | collective-permute-start | bytes 3080 | tf_op jit(solution)/shard_map/ppermute | solution.py:363
  18.6 41.2 %collective-permute-start.5 = (s32[2,4,32]{2,1,0:T(4,128)S(1)}, s32[2,4,32]{2,1,0:T(4,128)S(1)}, u32[]{:S(2)}, u32[]{:S(2)}) collective-permute-start(s32[2,4,32]{2,1,0:T(4,128)S(1)} %pad_add_fusion.2), channel_id=1, source_target_pairs={{0,16},{1,17},{2,18},{3,19},{4,20},{5,21},{6,22},{7,23},{8,24},{9,... | collective-permute-start | bytes 3080 | tf_op jit(solution)/shard_map/ppermute | solution.py:363
  21.3 0.7 copy-start
  43.7 16.0 %collective-permute-start.4 = (s32[2,4,32]{2,1,0:T(4,128)S(1)}, s32[2,4,32]{2,1,0:T(4,128)S(1)}, u32[]{:S(2)}, u32[]{:S(2)}) collective-permute-start(s32[2,4,32]{2,1,0:T(4,128)S(1)} %pad_add_fusion.2), channel_id=1, source_target_pairs={{0,8},{1,9},{2,10},{3,11},{4,12},{5,13},{6,14},{7,15},{8,0},{9,1},... | collective-permute-start | bytes 3080 | tf_op jit(solution)/shard_map/ppermute | solution.py:363
  63.9 9.2 %collective-permute-start.7 = (f32[2,4,64,128]{3,2,1,0:T(8,128)S(1)}, f32[2,4,64,128]{3,2,1,0:T(8,128)S(1)}, u32[]{:S(2)}, u32[]{:S(2)}) collective-permute-start(f32[2,4,64,128]{3,2,1,0:T(8,128)S(1)} %get-tuple-element.39), channel_id=1, source_target_pairs={{0,2},{1,3},{2,0},{3,1},{4,6},{5,7},{6,4},{7,5},{8,10},{9,11},{10,... | collective-permute-start | bytes 786440 | tf_op jit(solution)/shard_map/ppermute | solution.py:363
  64.8 14.6 %collective-permute-start.8 = (f32[2,4,64,128]{3,2,1,0:T(8,128)S(1)}, f32[2,4,64,128]{3,2,1,0:T(8,128)S(1)}, u32[]{:S(2)}, u32[]{:S(2)}) collective-permute-start(f32[2,4,64,128]{3,2,1,0:T(8,128)S(1)} %get-tuple-element.40), channel_id=1, source_target_pairs={{0,4},{1,5},{2,6},{3,7},{4,0},{5,1},{6,2},{7,3},{8,12},{9,13},{10,... | collective-permute-start | bytes 786440 | tf_op jit(solution)/shard_map/ppermute | solution.py:363
  65.7 13.6 %collective-permute-start.9 = (f32[2,4,64,128]{3,2,1,0:T(8,128)S(1)}, f32[2,4,64,128]{3,2,1,0:T(8,128)S(1)}, u32[]{:S(2)}, u32[]{:S(2)}) collective-permute-start(f32[2,4,64,128]{3,2,1,0:T(8,128)S(1)} %get-tuple-element.41), channel_id=1, source_target_pairs={{0,6},{1,7},{2,4},{3,5},{4,2},{5,3},{6,0},{7,1},{8,14},{9,15},{10,... | collective-permute-start | bytes 786440 | tf_op jit(solution)/shard_map/ppermute | solution.py:363
  67.4 13.6 %collective-permute-start.15 = (f32[2,4,4,16,128]{4,3,2,1,0:T(8,128)S(1)}, f32[2,4,4,16,128]{4,3,2,1,0:T(8,128)S(1)}, u32[]{:S(2)}, u32[]{:S(2)}) collective-permute-start(f32[2,4,4,16,128]{4,3,2,1,0:T(8,128)S(1)} %get-tuple-element.47), channel_id=1, source_target_pairs={{0,8},{1,9},{2,10},{3,11},{4,12},{5,13},{6,14},{7,15},{8,16},{9,17... | collective-permute-start | bytes 786440 | tf_op jit(solution)/shard_map/ppermute | solution.py:363
  69.1 12.0 %collective-permute-start.16 = (f32[2,4,4,16,128]{4,3,2,1,0:T(8,128)S(1)}, f32[2,4,4,16,128]{4,3,2,1,0:T(8,128)S(1)}, u32[]{:S(2)}, u32[]{:S(2)}) collective-permute-start(f32[2,4,4,16,128]{4,3,2,1,0:T(8,128)S(1)} %get-tuple-element.48), channel_id=1, source_target_pairs={{0,24},{1,25},{2,26},{3,27},{4,28},{5,29},{6,30},{7,31},{8,0},{9,1... | collective-permute-start | bytes 786440 | tf_op jit(solution)/shard_map/ppermute | solution.py:363
  80.5 1.6 %collective-permute-start.10 = (f32[8,64,128]{2,1,0:T(8,128)S(1)}, f32[8,64,128]{2,1,0:T(8,128)S(1)}, u32[]{:S(2)}, u32[]{:S(2)}) collective-permute-start(f32[8,64,128]{2,1,0:T(8,128)S(1)} %get-tuple-element.43), channel_id=1, source_target_pairs={{0,1},{1,0},{2,3},{3,2},{4,5},{5,4},{6,7},{7,6},{8,9},{9,8},{10,11... | collective-permute-start | bytes 786440 | tf_op jit(solution)/shard_map/ppermute | solution.py:363
  80.5 3.7 %collective-permute-start.14 = (f32[4,4,32,128]{3,2,1,0:T(8,128)S(1)}, f32[4,4,32,128]{3,2,1,0:T(8,128)S(1)}, u32[]{:S(2)}, u32[]{:S(2)}) collective-permute-start(f32[4,4,32,128]{3,2,1,0:T(8,128)S(1)} %get-tuple-element.46), channel_id=1, source_target_pairs={{0,1},{1,0},{2,3},{3,2},{4,5},{5,4},{6,7},{7,6},{8,9},{9,8},{10,11... | collective-permute-start | bytes 786440 | tf_op jit(solution)/shard_map/ppermute | solution.py:363
  81.1 3.2 %collective-permute-start.17 = (f32[2,4,4,16,128]{4,3,2,1,0:T(8,128)S(1)}, f32[2,4,4,16,128]{4,3,2,1,0:T(8,128)S(1)}, u32[]{:S(2)}, u32[]{:S(2)}) collective-permute-start(f32[2,4,4,16,128]{4,3,2,1,0:T(8,128)S(1)} %pad_maximum_fusion), channel_id=1, source_target_pairs={{0,1},{1,0},{2,3},{3,2},{4,5},{5,4},{6,7},{7,6},{8,9},{9,8},{10,11... | collective-permute-start | bytes 786440 | tf_op jit(solution)/shard_map/ppermute | solution.py:363
  82.1 6.9 %collective-permute-start.13 = (f32[8,16,128]{2,1,0:T(8,128)S(1)}, f32[8,16,128]{2,1,0:T(8,128)S(1)}, u32[]{:S(2)}, u32[]{:S(2)}) collective-permute-start(f32[8,16,128]{2,1,0:T(8,128)S(1)} %get-tuple-element.53), channel_id=1, source_target_pairs={{0,8},{1,9},{2,10},{3,11},{4,12},{5,13},{6,14},{7,15},{8,16},{9,17... | collective-permute-start | bytes 196616 | tf_op jit(solution)/shard_map/ppermute | solution.py:363
  82.2 11.8 %collective-permute-start.11 = (f32[8,32,128]{2,1,0:T(8,128)S(1)}, f32[8,32,128]{2,1,0:T(8,128)S(1)}, u32[]{:S(2)}, u32[]{:S(2)}) collective-permute-start(f32[8,32,128]{2,1,0:T(8,128)S(1)} %slice_add_fusion), channel_id=1, source_target_pairs={{0,16},{1,17},{2,18},{3,19},{4,20},{5,21},{6,22},{7,23},{8,24},{9,... | collective-permute-start | bytes 393224 | tf_op jit(solution)/shard_map/ppermute | solution.py:363
  85.2 8.8 %collective-permute-start.18 = (f32[8,32,128]{2,1,0:T(8,128)S(1)}, f32[8,32,128]{2,1,0:T(8,128)S(1)}, u32[]{:S(2)}, u32[]{:S(2)}) collective-permute-start(f32[8,32,128]{2,1,0:T(8,128)S(1)} %get-tuple-element.50), channel_id=1, source_target_pairs={{0,2},{1,3},{2,0},{3,1},{4,6},{5,7},{6,4},{7,5},{8,10},{9,11},{10,... | collective-permute-start | bytes 393224 | tf_op jit(solution)/shard_map/ppermute | solution.py:363
  86.7 7.7 %collective-permute-start.19 = (f32[8,32,128]{2,1,0:T(8,128)S(1)}, f32[8,32,128]{2,1,0:T(8,128)S(1)}, u32[]{:S(2)}, u32[]{:S(2)}) collective-permute-start(f32[8,32,128]{2,1,0:T(8,128)S(1)} %get-tuple-element.51), channel_id=1, source_target_pairs={{0,4},{1,5},{2,6},{3,7},{4,0},{5,1},{6,2},{7,3},{8,12},{9,13},{10,... | collective-permute-start | bytes 393224 | tf_op jit(solution)/shard_map/ppermute | solution.py:363
  87.4 7.1 %collective-permute-start.20 = (f32[8,32,128]{2,1,0:T(8,128)S(1)}, f32[8,32,128]{2,1,0:T(8,128)S(1)}, u32[]{:S(2)}, u32[]{:S(2)}) collective-permute-start(f32[8,32,128]{2,1,0:T(8,128)S(1)} %get-tuple-element.52), channel_id=1, source_target_pairs={{0,6},{1,7},{2,4},{3,5},{4,2},{5,3},{6,0},{7,1},{8,14},{9,15},{10,... | collective-permute-start | bytes 393224 | tf_op jit(solution)/shard_map/ppermute | solution.py:363
  89.0 5.0 %collective-permute-start.12 = (f32[8,16,128]{2,1,0:T(8,128)S(1)}, f32[8,16,128]{2,1,0:T(8,128)S(1)}, u32[]{:S(2)}, u32[]{:S(2)}) collective-permute-start(f32[8,16,128]{2,1,0:T(8,128)S(1)} %get-tuple-element.54), channel_id=1, source_target_pairs={{0,24},{1,25},{2,26},{3,27},{4,28},{5,29},{6,30},{7,31},{8,0},{9,1... | collective-permute-start | bytes 196616 | tf_op jit(solution)/shard_map/ppermute | solution.py:363
  (1 other events, 0.7 us)

commit v5 on v4

--- a/solution.py
+++ b/solution.py
@@ -279,11 +279,10 @@
                 (own_other if other else own_mine)[j, c] = slot
 
 
-def add_slots(target, table, entry, m, slots, rows=None, from_rows=None):
-    rows = pl.ds(0, HALF) if rows is None else rows
-    for c in range(slots.shape[0]):
-        value = slots[c] if from_rows is None else slots[c, from_rows]
-        target[table[entry * slots.shape[0] + c, m], rows, :] += value
+def add_slots(jobs):
+    for c in range(max(slots.shape[0] for _, _, _, _, slots, _, _ in jobs)):
+        for target, table, entry, m, slots, rows, from_rows in jobs:
+            target[table[entry * slots.shape[0] + c, m], rows, :] += slots[c, from_rows]
 
 
 def combine_far_kernel(n, me_ref, table, *refs):
@@ -301,11 +300,13 @@
         part = pl.ds(first, count)
         at = group + step
         at = jnp.where(at >= groups, at - groups, at)
-        for target, side in ((mine, core), (other, 1 - core)):
-            for j in range(PLACES):
+        for j in range(PLACES):
+            jobs = []
+            for target, side in ((mine, core), (other, 1 - core)):
                 m = (at - group) * GROUP + (place - (place ^ j)) * 2 + side - core
                 m = jnp.where(m < 0, m + n, m)
-                add_slots(target, table, (at ^ group) * 2 + (side ^ core), m, slots[j].at[side], part, part)
+                jobs.append((target, table, (at ^ group) * 2 + (side ^ core), m, slots[j].at[side], part, part))
+            add_slots(jobs)
 
 
 def combine_own_kernel(n, me_ref, table, mine, got, rest_got, *refs):
@@ -313,17 +314,24 @@
     me = me_ref[0]
     core = lax.rem(me, 2)
     place = lax.rem(me // 2, PLACES)
+    whole, rest_part = pl.ds(0, HALF), pl.ds(HALF - REST, REST)
     for j in range(PLACES):
         tiles[j][...] = jnp.zeros_like(tiles[j])
-        for other in range(2):
+    for other in range(2):
+        offsets = []
+        for j in range(PLACES):
             m = ((place ^ j) - place) * 2 + other * (2 * core - 1)
-            m = jnp.where(m < 0, m + n, m)
-            add_slots(tiles[j], table, j, m, (got if other else mine).at[j])
-            for index, step in enumerate(split_steps(n // GROUP)[2]):
-                at = m + step * GROUP
+            offsets.append(jnp.where(m < 0, m + n, m))
+        slots = got if other else mine
+        add_slots([(tiles[j], table, j, offsets[j], slots.at[j], whole, whole) for j in range(PLACES)])
+        for index, step in enumerate(split_steps(n // GROUP)[2]):
+            jobs = []
+            for j in range(PLACES):
+                at = offsets[j] + step * GROUP
                 at = jnp.where(at >= n, at - n, at)
                 rest = rest_got.at[index, j] if other else rest_mine[index].at[0, j]
-                add_slots(tiles[j], table, j, at, rest, pl.ds(HALF - REST, REST))
+                jobs.append((tiles[j], table, j, at, rest, rest_part, pl.ds(0, REST)))
+            add_slots(jobs)
 
 
 def final_kernel(*refs):

time: 95.5 us -> 96.2 us (level)
  starting transfers between devices: 34.1 us -> 31.7 us
  Pallas kernels: 31.9 us -> 34.2 us
    ppermute x21, starting transfers between devices: 26.8 us -> 24.4 us  [across(): return lax.ppermute(value, 'elem', [(i, partner(i)) for i in range(n)])]
    pallas_call x1, Pallas kernels: 21.7 us -> 23 us  [body(): pl.pallas_call(functools.partial(near_kernel, n), grid=(rows,), out_shape...]
    pallas_call x1, Pallas kernels: 4.13 us -> 5.29 us  [body(): pl.pallas_call(functools.partial(far_kernel, n, cap), out_shape=slot_shap...]
  transfers between devices with their start and end apart: 22 -> 22, of which waited for: 8 -> 8; matrix products, arithmetic and copies ran while one was open for 3% -> 3% of each run, Pallas kernels for 25% -> 26%
where the time goes in v5:
time: 96.2 us; the launch traced here: 95.2 us
  Pallas kernels  34.2 us (36%)
  starting transfers between devices  31.7 us (33%)
  waiting for transfers between devices  25 us (26%)
  local copies, waits for them, and re-layouts  3.4 us (4%)
    ppermute x21, waiting for transfers between devices, across(): return lax.ppermute(value, 'elem', [(i, partner(i)) for i in range(n)])  25 us
    ppermute x21, starting transfers between devices, across(): return lax.ppermute(value, 'elem', [(i, partner(i)) for i in range(n)])  24.4 us
    pallas_call x1, Pallas kernels, body(): pl.pallas_call(functools.partial(near_kernel, n), grid=(rows,), out_shape...  23 us
    all_to_all x1, starting transfers between devices, body(): lax.all_to_all(send.reshape(n, serve_count * B, LANES), 'elem', split_axi...  7.3 us
    pallas_call x1, Pallas kernels, body(): pl.pallas_call(functools.partial(far_kernel, n, cap), out_shape=slot_shap...  5.29 us
    pallas_call x1, Pallas kernels, body(): pl.pallas_call(functools.partial(prep_kernel, n), out_shape=(shape((rows,...  3.16 us
    unnamed x7, local copies, waits for them, and re-layouts  3.01 us
    pallas_call x2, Pallas kernels, combine(): pl.pallas_call(functools.partial(kernel, n), out_shape=out_shape, in_spec...  1.97 us
  transfers between devices with their start and end apart: 22, of which 8 were waited for; matrix products, arithmetic and copies ran while one was open for 3% of the time, Pallas kernels for 26%

profile of v5, /device:TPU:0, one launch (start us, length us, event | category | flops | bytes accessed | tf_op | source)
XLA Modules:
  0.0 95.2 jit_solution(15263410148808484088)
XLA Ops:
  0.0 3.2 %prep.1 = (f32[32,64,128]{2,1,0:T(8,128)S(1)}, f32[32,2,64,128]{3,2,1,0:T(8,128)}) custom-call(s32[1]{0:T(128)} %bitcast.me_ref, s32[2,31]{1,0:T(2,128)} %bitcast.35, f32[32,64,128]{2,1,0:T(8,128)} %bitcast.28), custom_call_target="tpu_custom_call" | custom-call | tf_op jit(solution)/shard_map/prep/pallas_call | solution.py:374
  3.2 7.3 %all-to-all-start = ((f32[32,128,128]{2,1,0:T(8,128)}), f32[32,128,128]{2,1,0:T(8,128)S(1)}, u32[]{:S(2)}, u32[]{:S(2)}) async-start(f32[32,128,128]{2,1,0:T(8,128)} %bitcast.27), calls=%async_computation | async-start | bytes 4194304 | tf_op jit(solution)/shard_map/all_to_all | solution.py:391
  10.8 2.6 %collective-permute-start.2 = (s32[1,4,32]{2,1,0:T(4,128)S(1)}, s32[1,4,32]{2,1,0:T(4,128)S(1)}, u32[]{:S(2)}, u32[]{:S(2)}) collective-permute-start(s32[1,4,32]{2,1,0:T(4,128)S(1)} %bitcast.30), channel_id=1, source_target_pairs={{0,6},{1,7},{2,4},{3,5},{4,2},{5,3},{6,0},{7,1},{8,14},{9,15},{10,... | collective-permute-start | bytes 1544 | tf_op jit(solution)/shard_map/ppermute | solution.py:371
  13.4 0.6 collective-permute-start.1
  15.0 3.6 %collective-permute-start.6 = (s32[2,4,32]{2,1,0:T(4,128)S(1)}, s32[2,4,32]{2,1,0:T(4,128)S(1)}, u32[]{:S(2)}, u32[]{:S(2)}) collective-permute-start(s32[2,4,32]{2,1,0:T(4,128)S(1)} %pad_add_fusion.2), channel_id=1, source_target_pairs={{0,24},{1,25},{2,26},{3,27},{4,28},{5,29},{6,30},{7,31},{8,16},{9,... | collective-permute-start | bytes 3080 | tf_op jit(solution)/shard_map/ppermute | solution.py:371
  18.6 2.7 %copy.12 = f32[28,8,32,128]{3,2,1,0:T(8,128)S(1)} copy(f32[28,8,32,128]{3,1,2,0:T(8,128)} %bitcast.26) | data formatting | bytes 7340032
  22.0 23.0 %near.1 = (bf16[256,128,128]{2,1,0:T(8,128)(2,1)}, f32[128,32,128]{2,1,0:T(8,128)}, s32[2304]{0:T(1024)S(1)}) custom-call(s32[1]{0:T(128)S(6)} %copy.13.count_row, s32[7,32]{1,0:T(8,128)S(1)} %bitcast.24, s32[32,28]{1,0:T(8,128)S(1)} %copy-done, s32[1]{0:T(128)} %bitcast.me_ref, f32[32,64,128]{2,1,0:T(8,128)S(1)} %get-tuple-element.32.own_ref, ...), custom_call_target="tpu_custom_call" | custom-call | flops 3758096384 | bytes 16777216 | tf_op jit(solution)/shard_map/near/pallas_call | solution.py:410
  45.5 3.8 %collective-permute-done.6 = s32[2,4,32]{2,1,0:T(4,128)S(1)} collective-permute-done((s32[2,4,32]{2,1,0:T(4,128)S(1)}, s32[2,4,32]{2,1,0:T(4,128)S(1)}, u32[]{:S(2)}, u32[]{:S(2)}) %collective-permute-start.6) | collective-permute-done | bytes 1056 | tf_op jit(solution)/shard_map/ppermute | solution.py:371
  49.3 10.4 %collective-permute-done.5 = s32[2,4,32]{2,1,0:T(4,128)S(1)} collective-permute-done((s32[2,4,32]{2,1,0:T(4,128)S(1)}, s32[2,4,32]{2,1,0:T(4,128)S(1)}, u32[]{:S(2)}, u32[]{:S(2)}) %collective-permute-start.5) | collective-permute-done | bytes 1056 | tf_op jit(solution)/shard_map/ppermute | solution.py:371
  59.8 5.3 %far.1 = (f32[2,4,64,128]{3,2,1,0:T(8,128)S(1)}, f32[2,4,64,128]{3,2,1,0:T(8,128)S(1)}, f32[2,4,64,128]{3,2,1,0:T(8,128)S(1)}, f32[2,4,64,128]{3,2,1,0:T(8,128)S...) custom-call(s32[1]{0:T(128)} %bitcast.me_ref, ...), custom_call_target="tpu_custom_call" | custom-call | flops 1879048192 | bytes 16777216 | tf_op jit(solution)/shard_map/far/pallas_call | solution.py:437
  65.1 1.1 %collective-permute-start.8 = (f32[2,4,64,128]{3,2,1,0:T(8,128)S(1)}, f32[2,4,64,128]{3,2,1,0:T(8,128)S(1)}, u32[]{:S(2)}, u32[]{:S(2)}) collective-permute-start(f32[2,4,64,128]{3,2,1,0:T(8,128)S(1)} %get-tuple-element.40), channel_id=1, source_target_pairs={{0,4},{1,5},{2,6},{3,7},{4,0},{5,1},{6,2},{7,3},{8,12},{9,13},{10,... | collective-permute-start | bytes 786440 | tf_op jit(solution)/shard_map/ppermute | solution.py:371
  66.2 2.4 %collective-permute-start.9 = (f32[2,4,64,128]{3,2,1,0:T(8,128)S(1)}, f32[2,4,64,128]{3,2,1,0:T(8,128)S(1)}, u32[]{:S(2)}, u32[]{:S(2)}) collective-permute-start(f32[2,4,64,128]{3,2,1,0:T(8,128)S(1)} %get-tuple-element.41), channel_id=1, source_target_pairs={{0,6},{1,7},{2,4},{3,5},{4,2},{5,3},{6,0},{7,1},{8,14},{9,15},{10,... | collective-permute-start | bytes 786440 | tf_op jit(solution)/shard_map/ppermute | solution.py:371
  68.9 3.5 %collective-permute-start.16 = (f32[2,4,4,16,128]{4,3,2,1,0:T(8,128)S(1)}, f32[2,4,4,16,128]{4,3,2,1,0:T(8,128)S(1)}, u32[]{:S(2)}, u32[]{:S(2)}) collective-permute-start(f32[2,4,4,16,128]{4,3,2,1,0:T(8,128)S(1)} %get-tuple-element.48), channel_id=1, source_target_pairs={{0,24},{1,25},{2,26},{3,27},{4,28},{5,29},{6,30},{7,31},{8,0},{9,1... | collective-permute-start | bytes 786440 | tf_op jit(solution)/shard_map/ppermute | solution.py:371
  72.4 1.9 %collective-permute-done.7.refs_1_ = f32[2,4,64,128]{3,2,1,0:T(8,128)S(1)} collective-permute-done((f32[2,4,64,128]{3,2,1,0:T(8,128)S(1)}, f32[2,4,64,128]{3,2,1,0:T(8,128)S(1)}, u32[]{:S(2)}, u32[]{:S(2)}) %collective-permute-start.7) | collective-permute-done | bytes 262176 | tf_op jit(solution)/shard_map/ppermute | solution.py:371
  74.3 4.8 %collective-permute-done.8.refs_2_ = f32[2,4,64,128]{3,2,1,0:T(8,128)S(1)} collective-permute-done((f32[2,4,64,128]{3,2,1,0:T(8,128)S(1)}, f32[2,4,64,128]{3,2,1,0:T(8,128)S(1)}, u32[]{:S(2)}, u32[]{:S(2)}) %collective-permute-start.8) | collective-permute-done | bytes 262176 | tf_op jit(solution)/shard_map/ppermute | solution.py:371
  79.1 1.1 %combine_far_kernel.1 = (f32[8,64,128]{2,1,0:T(8,128)S(1)}, f32[8,64,128]{2,1,0:T(8,128)S(1)}) custom-call(s32[1]{0:T(128)} %bitcast.me_ref, s32[32,32]{1,0:T(8,128)S(1)} %bitcast.22, f32[2,4,64,128]{3,2,1,0:T(8,128)S(1)} %get-tuple-element.38.refs_0_, f32[2,4,64,128]{3,2,1,0:T(8,128)S(1)} %collective-permute-done.7.refs_1_, ...), custom_call_target="tpu_custom_call" | custom-call | tf_op jit(solution)/shard_map/combine_far_kernel/pallas_call | solution.py:455
  82.3 1.9 %collective-permute-start.11 = (f32[8,32,128]{2,1,0:T(8,128)S(1)}, f32[8,32,128]{2,1,0:T(8,128)S(1)}, u32[]{:S(2)}, u32[]{:S(2)}) collective-permute-start(f32[8,32,128]{2,1,0:T(8,128)S(1)} %slice_add_fusion), channel_id=1, source_target_pairs={{0,16},{1,17},{2,18},{3,19},{4,20},{5,21},{6,22},{7,23},{8,24},{9,... | collective-permute-start | bytes 393224 | tf_op jit(solution)/shard_map/ppermute | solution.py:371
  84.2 0.9 combine_own_kernel.1
  85.1 1.5 %collective-permute-start.18 = (f32[8,32,128]{2,1,0:T(8,128)S(1)}, f32[8,32,128]{2,1,0:T(8,128)S(1)}, u32[]{:S(2)}, u32[]{:S(2)}) collective-permute-start(f32[8,32,128]{2,1,0:T(8,128)S(1)} %get-tuple-element.50), channel_id=1, source_target_pairs={{0,2},{1,3},{2,0},{3,1},{4,6},{5,7},{6,4},{7,5},{8,10},{9,11},{10,... | collective-permute-start | bytes 393224 | tf_op jit(solution)/shard_map/ppermute | solution.py:371
  86.6 0.7 collective-permute-start.19
  87.3 1.4 %collective-permute-start.20 = (f32[8,32,128]{2,1,0:T(8,128)S(1)}, f32[8,32,128]{2,1,0:T(8,128)S(1)}, u32[]{:S(2)}, u32[]{:S(2)}) collective-permute-start(f32[8,32,128]{2,1,0:T(8,128)S(1)} %get-tuple-element.52), channel_id=1, source_target_pairs={{0,6},{1,7},{2,4},{3,5},{4,2},{5,3},{6,0},{7,1},{8,14},{9,15},{10,... | collective-permute-start | bytes 393224 | tf_op jit(solution)/shard_map/ppermute | solution.py:371
  88.7 2.6 %collective-permute-start.12 = (f32[8,16,128]{2,1,0:T(8,128)S(1)}, f32[8,16,128]{2,1,0:T(8,128)S(1)}, u32[]{:S(2)}, u32[]{:S(2)}) collective-permute-start(f32[8,16,128]{2,1,0:T(8,128)S(1)} %get-tuple-element.54), channel_id=1, source_target_pairs={{0,24},{1,25},{2,26},{3,27},{4,28},{5,29},{6,30},{7,31},{8,0},{9,1... | collective-permute-start | bytes 196616 | tf_op jit(solution)/shard_map/ppermute | solution.py:371
  91.3 2.9 %collective-permute-done.12.refs_1_ = f32[8,16,128]{2,1,0:T(8,128)S(1)} collective-permute-done((f32[8,16,128]{2,1,0:T(8,128)S(1)}, f32[8,16,128]{2,1,0:T(8,128)S(1)}, u32[]{:S(2)}, u32[]{:S(2)}) %collective-permute-start.12) | collective-permute-done | bytes 65568 | tf_op jit(solution)/shard_map/ppermute | solution.py:371
  94.4 0.8 final.1
  (42 shorter events, 4.6 us)
Async XLA Ops:
  0.0 10.5 %copy-start.2 = (s32[1,32,4]{1,2,0:T(4,128)S(1)}, s32[1,32,4]{1,2,0:T(4,128)}, u32[]{:S(2)}) copy-start(s32[1,32,4]{1,2,0:T(4,128)} %param.13) | copy-start | bytes 1540
  3.2 56.6 %all-to-all-start = ((f32[32,128,128]{2,1,0:T(8,128)}), f32[32,128,128]{2,1,0:T(8,128)S(1)}, u32[]{:S(2)}, u32[]{:S(2)}) async-start(f32[32,128,128]{2,1,0:T(8,128)} %bitcast.27), calls=%async_computation | async-start | bytes 4194304 | tf_op jit(solution)/shard_map/all_to_all | solution.py:391
  10.5 4.5 %collective-permute-start.3 = (s32[1,4,32]{2,1,0:T(4,128)S(1)}, s32[1,4,32]{2,1,0:T(4,128)S(1)}, u32[]{:S(2)}, u32[]{:S(2)}) collective-permute-start(s32[1,4,32]{2,1,0:T(4,128)S(1)} %bitcast.29), channel_id=1, source_target_pairs={{0,1},{1,0},{2,3},{3,2},{4,5},{5,4},{6,7},{7,6},{8,9},{9,8},{10,11... | collective-permute-start | bytes 1544 | tf_op jit(solution)/shard_map/ppermute | solution.py:371
  10.8 34.2 %collective-permute-start.2 = (s32[1,4,32]{2,1,0:T(4,128)S(1)}, s32[1,4,32]{2,1,0:T(4,128)S(1)}, u32[]{:S(2)}, u32[]{:S(2)}) collective-permute-start(s32[1,4,32]{2,1,0:T(4,128)S(1)} %bitcast.30), channel_id=1, source_target_pairs={{0,6},{1,7},{2,4},{3,5},{4,2},{5,3},{6,0},{7,1},{8,14},{9,15},{10,... | collective-permute-start | bytes 1544 | tf_op jit(solution)/shard_map/ppermute | solution.py:371
  13.4 32.1 %collective-permute-start.1 = (s32[1,4,32]{2,1,0:T(4,128)S(1)}, s32[1,4,32]{2,1,0:T(4,128)S(1)}, u32[]{:S(2)}, u32[]{:S(2)}) collective-permute-start(s32[1,4,32]{2,1,0:T(4,128)S(1)} %bitcast.31), channel_id=1, source_target_pairs={{0,4},{1,5},{2,6},{3,7},{4,0},{5,1},{6,2},{7,3},{8,12},{9,13},{10,... | collective-permute-start | bytes 1544 | tf_op jit(solution)/shard_map/ppermute | solution.py:371
  14.0 31.5 %collective-permute-start = (s32[1,4,32]{2,1,0:T(4,128)S(1)}, s32[1,4,32]{2,1,0:T(4,128)S(1)}, u32[]{:S(2)}, u32[]{:S(2)}) collective-permute-start(s32[1,4,32]{2,1,0:T(4,128)S(1)} %bitcast.32), channel_id=1, source_target_pairs={{0,2},{1,3},{2,0},{3,1},{4,6},{5,7},{6,4},{7,5},{8,10},{9,11},{10,... | collective-permute-start | bytes 1544 | tf_op jit(solution)/shard_map/ppermute | solution.py:371
  15.0 34.3 %collective-permute-start.6 = (s32[2,4,32]{2,1,0:T(4,128)S(1)}, s32[2,4,32]{2,1,0:T(4,128)S(1)}, u32[]{:S(2)}, u32[]{:S(2)}) collective-permute-start(s32[2,4,32]{2,1,0:T(4,128)S(1)} %pad_add_fusion.2), channel_id=1, source_target_pairs={{0,24},{1,25},{2,26},{3,27},{4,28},{5,29},{6,30},{7,31},{8,16},{9,... | collective-permute-start | bytes 3080 | tf_op jit(solution)/shard_map/ppermute | solution.py:371
  18.6 41.2 %collective-permute-start.5 = (s32[2,4,32]{2,1,0:T(4,128)S(1)}, s32[2,4,32]{2,1,0:T(4,128)S(1)}, u32[]{:S(2)}, u32[]{:S(2)}) collective-permute-start(s32[2,4,32]{2,1,0:T(4,128)S(1)} %pad_add_fusion.2), channel_id=1, source_target_pairs={{0,16},{1,17},{2,18},{3,19},{4,20},{5,21},{6,22},{7,23},{8,24},{9,... | collective-permute-start | bytes 3080 | tf_op jit(solution)/shard_map/ppermute | solution.py:371
  21.3 0.7 copy-start
  45.0 14.8 %collective-permute-start.4 = (s32[2,4,32]{2,1,0:T(4,128)S(1)}, s32[2,4,32]{2,1,0:T(4,128)S(1)}, u32[]{:S(2)}, u32[]{:S(2)}) collective-permute-start(s32[2,4,32]{2,1,0:T(4,128)S(1)} %pad_add_fusion.2), channel_id=1, source_target_pairs={{0,8},{1,9},{2,10},{3,11},{4,12},{5,13},{6,14},{7,15},{8,0},{9,1},... | collective-permute-start | bytes 3080 | tf_op jit(solution)/shard_map/ppermute | solution.py:371
  65.1 9.3 %collective-permute-start.7 = (f32[2,4,64,128]{3,2,1,0:T(8,128)S(1)}, f32[2,4,64,128]{3,2,1,0:T(8,128)S(1)}, u32[]{:S(2)}, u32[]{:S(2)}) collective-permute-start(f32[2,4,64,128]{3,2,1,0:T(8,128)S(1)} %get-tuple-element.39), channel_id=1, source_target_pairs={{0,2},{1,3},{2,0},{3,1},{4,6},{5,7},{6,4},{7,5},{8,10},{9,11},{10,... | collective-permute-start | bytes 786440 | tf_op jit(solution)/shard_map/ppermute | solution.py:371
  65.1 14.0 %collective-permute-start.8 = (f32[2,4,64,128]{3,2,1,0:T(8,128)S(1)}, f32[2,4,64,128]{3,2,1,0:T(8,128)S(1)}, u32[]{:S(2)}, u32[]{:S(2)}) collective-permute-start(f32[2,4,64,128]{3,2,1,0:T(8,128)S(1)} %get-tuple-element.40), channel_id=1, source_target_pairs={{0,4},{1,5},{2,6},{3,7},{4,0},{5,1},{6,2},{7,3},{8,12},{9,13},{10,... | collective-permute-start | bytes 786440 | tf_op jit(solution)/shard_map/ppermute | solution.py:371
  66.2 12.9 %collective-permute-start.9 = (f32[2,4,64,128]{3,2,1,0:T(8,128)S(1)}, f32[2,4,64,128]{3,2,1,0:T(8,128)S(1)}, u32[]{:S(2)}, u32[]{:S(2)}) collective-permute-start(f32[2,4,64,128]{3,2,1,0:T(8,128)S(1)} %get-tuple-element.41), channel_id=1, source_target_pairs={{0,6},{1,7},{2,4},{3,5},{4,2},{5,3},{6,0},{7,1},{8,14},{9,15},{10,... | collective-permute-start | bytes 786440 | tf_op jit(solution)/shard_map/ppermute | solution.py:371
  68.6 12.2 %collective-permute-start.15 = (f32[2,4,4,16,128]{4,3,2,1,0:T(8,128)S(1)}, f32[2,4,4,16,128]{4,3,2,1,0:T(8,128)S(1)}, u32[]{:S(2)}, u32[]{:S(2)}) collective-permute-start(f32[2,4,4,16,128]{4,3,2,1,0:T(8,128)S(1)} %get-tuple-element.47), channel_id=1, source_target_pairs={{0,8},{1,9},{2,10},{3,11},{4,12},{5,13},{6,14},{7,15},{8,16},{9,17... | collective-permute-start | bytes 786440 | tf_op jit(solution)/shard_map/ppermute | solution.py:371
  68.9 12.3 %collective-permute-start.16 = (f32[2,4,4,16,128]{4,3,2,1,0:T(8,128)S(1)}, f32[2,4,4,16,128]{4,3,2,1,0:T(8,128)S(1)}, u32[]{:S(2)}, u32[]{:S(2)}) collective-permute-start(f32[2,4,4,16,128]{4,3,2,1,0:T(8,128)S(1)} %get-tuple-element.48), channel_id=1, source_target_pairs={{0,24},{1,25},{2,26},{3,27},{4,28},{5,29},{6,30},{7,31},{8,0},{9,1... | collective-permute-start | bytes 786440 | tf_op jit(solution)/shard_map/ppermute | solution.py:371
  80.2 1.6 %collective-permute-start.10 = (f32[8,64,128]{2,1,0:T(8,128)S(1)}, f32[8,64,128]{2,1,0:T(8,128)S(1)}, u32[]{:S(2)}, u32[]{:S(2)}) collective-permute-start(f32[8,64,128]{2,1,0:T(8,128)S(1)} %get-tuple-element.43), channel_id=1, source_target_pairs={{0,1},{1,0},{2,3},{3,2},{4,5},{5,4},{6,7},{7,6},{8,9},{9,8},{10,11... | collective-permute-start | bytes 786440 | tf_op jit(solution)/shard_map/ppermute | solution.py:371
  80.3 3.9 %collective-permute-start.14 = (f32[4,4,32,128]{3,2,1,0:T(8,128)S(1)}, f32[4,4,32,128]{3,2,1,0:T(8,128)S(1)}, u32[]{:S(2)}, u32[]{:S(2)}) collective-permute-start(f32[4,4,32,128]{3,2,1,0:T(8,128)S(1)} %get-tuple-element.46), channel_id=1, source_target_pairs={{0,1},{1,0},{2,3},{3,2},{4,5},{5,4},{6,7},{7,6},{8,9},{9,8},{10,11... | collective-permute-start | bytes 786440 | tf_op jit(solution)/shard_map/ppermute | solution.py:371
  81.3 2.9 %collective-permute-start.17 = (f32[2,4,4,16,128]{4,3,2,1,0:T(8,128)S(1)}, f32[2,4,4,16,128]{4,3,2,1,0:T(8,128)S(1)}, u32[]{:S(2)}, u32[]{:S(2)}) collective-permute-start(f32[2,4,4,16,128]{4,3,2,1,0:T(8,128)S(1)} %pad_maximum_fusion), channel_id=1, source_target_pairs={{0,1},{1,0},{2,3},{3,2},{4,5},{5,4},{6,7},{7,6},{8,9},{9,8},{10,11... | collective-permute-start | bytes 786440 | tf_op jit(solution)/shard_map/ppermute | solution.py:371
  81.9 6.8 %collective-permute-start.13 = (f32[8,16,128]{2,1,0:T(8,128)S(1)}, f32[8,16,128]{2,1,0:T(8,128)S(1)}, u32[]{:S(2)}, u32[]{:S(2)}) collective-permute-start(f32[8,16,128]{2,1,0:T(8,128)S(1)} %get-tuple-element.53), channel_id=1, source_target_pairs={{0,8},{1,9},{2,10},{3,11},{4,12},{5,13},{6,14},{7,15},{8,16},{9,17... | collective-permute-start | bytes 196616 | tf_op jit(solution)/shard_map/ppermute | solution.py:371
  82.3 11.8 %collective-permute-start.11 = (f32[8,32,128]{2,1,0:T(8,128)S(1)}, f32[8,32,128]{2,1,0:T(8,128)S(1)}, u32[]{:S(2)}, u32[]{:S(2)}) collective-permute-start(f32[8,32,128]{2,1,0:T(8,128)S(1)} %slice_add_fusion), channel_id=1, source_target_pairs={{0,16},{1,17},{2,18},{3,19},{4,20},{5,21},{6,22},{7,23},{8,24},{9,... | collective-permute-start | bytes 393224 | tf_op jit(solution)/shard_map/ppermute | solution.py:371
  85.1 9.0 %collective-permute-start.18 = (f32[8,32,128]{2,1,0:T(8,128)S(1)}, f32[8,32,128]{2,1,0:T(8,128)S(1)}, u32[]{:S(2)}, u32[]{:S(2)}) collective-permute-start(f32[8,32,128]{2,1,0:T(8,128)S(1)} %get-tuple-element.50), channel_id=1, source_target_pairs={{0,2},{1,3},{2,0},{3,1},{4,6},{5,7},{6,4},{7,5},{8,10},{9,11},{10,... | collective-permute-start | bytes 393224 | tf_op jit(solution)/shard_map/ppermute | solution.py:371
  86.6 7.8 %collective-permute-start.19 = (f32[8,32,128]{2,1,0:T(8,128)S(1)}, f32[8,32,128]{2,1,0:T(8,128)S(1)}, u32[]{:S(2)}, u32[]{:S(2)}) collective-permute-start(f32[8,32,128]{2,1,0:T(8,128)S(1)} %get-tuple-element.51), channel_id=1, source_target_pairs={{0,4},{1,5},{2,6},{3,7},{4,0},{5,1},{6,2},{7,3},{8,12},{9,13},{10,... | collective-permute-start | bytes 393224 | tf_op jit(solution)/shard_map/ppermute | solution.py:371
  87.3 7.1 %collective-permute-start.20 = (f32[8,32,128]{2,1,0:T(8,128)S(1)}, f32[8,32,128]{2,1,0:T(8,128)S(1)}, u32[]{:S(2)}, u32[]{:S(2)}) collective-permute-start(f32[8,32,128]{2,1,0:T(8,128)S(1)} %get-tuple-element.52), channel_id=1, source_target_pairs={{0,6},{1,7},{2,4},{3,5},{4,2},{5,3},{6,0},{7,1},{8,14},{9,15},{10,... | collective-permute-start | bytes 393224 | tf_op jit(solution)/shard_map/ppermute | solution.py:371
  88.7 5.5 %collective-permute-start.12 = (f32[8,16,128]{2,1,0:T(8,128)S(1)}, f32[8,16,128]{2,1,0:T(8,128)S(1)}, u32[]{:S(2)}, u32[]{:S(2)}) collective-permute-start(f32[8,16,128]{2,1,0:T(8,128)S(1)} %get-tuple-element.54), channel_id=1, source_target_pairs={{0,24},{1,25},{2,26},{3,27},{4,28},{5,29},{6,30},{7,31},{8,0},{9,1... | collective-permute-start | bytes 196616 | tf_op jit(solution)/shard_map/ppermute | solution.py:371
  (1 other events, 0.7 us)
